TPU v7x, 32 devices: a whole 2x2x4 slice. The times are simulated.
32 devices in a mesh: dp: 16 (over z, y, core), group: 2 (over x).
Axes of the slice: x: 2, y: 2, z: 4, core: 2. Of those that a mesh axis runs over, the one named last changes fastest.
Arguments:
- inputs_t: bfloat16 [64, 128, 2048], P(None, 'group', 'dp'), may hold values from -6 to 6
- grad_proj: bfloat16 [2, 112, 128, 2048], P(None, None, None, 'dp'), may hold values from -6 to 6
- stored_blocks: bfloat16 [16, 2, 128, 128], P('dp', None, 'group'), may hold values from -0.25 to 0.25
- block_scales: float32 [16, 2], P('dp'), may hold values from 0.5 to 2
- kept_blocks: int32 [2, 3584], replicated, may hold values from 0 to 7167, as said below
- assignment: int32 [24], replicated, may hold values from 0 to 7167, as said below
- owner_counts: int32 [16], replicated, may hold values from 1 to 2, 24 in all
Outputs:
- grad_inputs_t: bfloat16 [64, 128, 2048], P(None, 'group', 'dp')
- block_grads: float32 [16, 2, 128, 128], P('dp', None, 'group')
- scale_grads: float32 [16, 2], P('dp')
Inputs may be any that keep to these rules, and one draw needn't show every extreme that they name: `kept_blocks`: row m lists, in ascending order, 3584 distinct kept blocks of projection m (0 gate, 1 up); block b covers features from 128 * (b // 112) and hidden units from 128 * (b % 112). `assignment`: 24 distinct entries; entry e stands for block kept_blocks[e // 3584, e % 3584]; owner o holds in its slots 0 to owner_counts[o] - 1 the entries at positions offset(o) onward, offset(o) being the sum of the counts of the owners before o. `owner_counts`: the counts sum to 24.
All inputs are finite; a program needn't handle non-finite values.
Results may differ from a plain program's by a relative error of at most 0.0049.
Values may be sent and summed in bfloat16 or wider, within the bound.
No kernel may reach another device: no remote copies, remote signals or barrier semaphores. Data moves between devices by JAX's collectives and lax.ppermute only.
A program may use at most 64 MiB of HBM per device.

v0:
```python
import math

import jax
import jax.numpy as jnp
from jax import lax
from jax.sharding import PartitionSpec as P


def slot_tables(kept_blocks, assignment, owner_counts, slot_count, hid_blocks):
    keep_count = kept_blocks.shape[1]
    offsets = jnp.cumsum(owner_counts) - owner_counts
    slot_column = jnp.arange(slot_count, dtype=jnp.int32)
    live_slot = slot_column[None, :] < owner_counts[:, None]
    position = jnp.clip(offsets[:, None] + slot_column[None, :], 0, assignment.shape[0] - 1)
    entry_id = assignment[position]
    matrix = entry_id // keep_count
    kept_index = kept_blocks[matrix, entry_id % keep_count]
    return (live_slot, matrix, kept_index // hid_blocks, kept_index % hid_blocks)


def on_device(
    inputs_t, grad_proj, stored_blocks, block_scales, kept_blocks, assignment, owner_counts
):
    row_blocks, slab_rows, tokens_here = inputs_t.shape
    slot_count = stored_blocks.shape[1]
    block_side = stored_blocks.shape[3]
    hid_blocks = grad_proj.shape[1]
    owner_total = owner_counts.shape[0]
    live_slot, matrix, row_block, col_block = slot_tables(
        kept_blocks, assignment, owner_counts, slot_count, hid_blocks
    )
    source_rows = (matrix * hid_blocks + col_block).reshape(-1)
    grad_view = grad_proj.reshape(2 * hid_blocks, block_side, tokens_here)
    columns_all = grad_view[source_rows]
    scaled = (block_scales[:, :, None, None] * stored_blocks.astype(jnp.float32)).astype(
        jnp.bfloat16
    )
    grad_norm = 1.0 / math.sqrt(tokens_here * lax.axis_size("dp"))

    def table_slice(index_table):
        return index_table.reshape(-1)

    def column_slice():
        return columns_all

    empty_sum = jnp.zeros((row_blocks, slab_rows, tokens_here), jnp.float32)
    gathered = lax.all_gather(scaled, "dp", axis=0, tiled=True)
    rows_here = table_slice(row_block)
    live_here = table_slice(live_slot)
    columns = column_slice()
    pieces = gathered.reshape(-1, slab_rows, block_side)
    pieces = jnp.where(live_here[:, None, None], pieces, jnp.zeros_like(pieces))
    contrib = jnp.einsum("nsq,nqt->nst", pieces, columns, preferred_element_type=jnp.float32)
    totals = empty_sum.at[rows_here].add(contrib)
    grad_inputs_t = totals.astype(jnp.bfloat16)
    rows_here = table_slice(row_block)
    live_here = table_slice(live_slot)
    left_rows = inputs_t[rows_here]
    left_rows = jnp.where(live_here[:, None, None], left_rows, jnp.zeros_like(left_rows))
    columns = column_slice()
    product = (
        jnp.einsum("nst,nqt->nsq", left_rows, columns, preferred_element_type=jnp.float32)
        * grad_norm
    )
    owner_sums = lax.psum_scatter(
        product.reshape(owner_total, slot_count, slab_rows, block_side),
        "dp",
        scatter_dimension=0,
        tiled=True,
    )
    my_index = lax.axis_index("dp")
    own_live = lax.dynamic_slice_in_dim(live_slot, my_index, 1, 0)
    block_grads = jnp.where(
        own_live[:, :, None, None], block_scales[:, :, None, None] * owner_sums, 0.0
    )
    partial_scale = jnp.sum(stored_blocks.astype(jnp.float32) * owner_sums, axis=(2, 3))
    scale_total = lax.psum(partial_scale, "group")
    scale_grads = jnp.where(own_live, scale_total, 0.0)
    return (grad_inputs_t, block_grads, scale_grads)


def solution(mesh):
    return jax.shard_map(
        on_device,
        mesh=mesh,
        in_specs=(
            P(None, "group", "dp"),
            P(None, None, None, "dp"),
            P("dp", None, "group", None),
            P("dp", None),
            P(),
            P(),
            P(),
        ),
        out_specs=(P(None, "group", "dp"), P("dp", None, "group", None), P("dp", None)),
        check_vma=False,
    )
```

profile of v0, /device:TPU:0, one launch (start us, length us, event | category | flops | bytes accessed | tf_op | source)
XLA Modules:
  0.0 120.1 jit_solution(16924331982433442830)
XLA Ops:
  7.2 0.0 copy-start
  7.2 0.0 copy-start.1
  7.2 0.0 reduce-scatter.2.cloned.1.call-start
  7.2 0.8 iota_compare_fusion
  8.0 0.7 copy.12
  8.8 0.1 reduce.1
  8.9 0.7 sub.15
  9.6 0.1 compare_select_fusion.2
  9.7 0.1 reshape.331
  9.8 0.0 copy-done.1
  9.8 0.7 gather_fusion
  10.5 0.0 copy-start.2
  10.5 0.1 lt.89
  10.6 0.1 ne.113
  10.7 0.1 rem.65
  10.8 0.1 div.43
  10.9 0.1 reshape.337
  11.0 0.2 copy-done.2
  11.2 0.8 gather_fusion.1
  12.0 0.0 copy-done
  12.0 0.6 gather_fusion.3
  12.7 3.8 %gather_fusion.2 = bf16[32,128,128]{2,1,0:T(8,128)(2,1)S(1)} fusion(bf16[224,128,128]{2,1,0:T(8,128)(2,1)} %bitcast.46, s32[1024]{0:T(1024)S(1)} %get-tuple-element.11), kind=kCustom, calls=%fused_computation.2 | custom fusion | bytes 2097280 | tf_op jit(solution)/shard_map/gather | solution.py:34
  16.5 0.0 copy-start.3
  16.6 0.0 copy-start.4
  16.6 1.8 %convolution_multiply_fusion = f32[32,64,128]{2,1,0:T(8,128)} fusion(bf16[32,128,128]{2,1,0:T(8,128)(2,1)S(1)} %gather_fusion.2, bf16[32,64,128]{2,1,0:T(8,128)(2,1)S(1)} %gather_fusion.3, pred[32]{0:T(512)(128)(4,1)S(1)} %lt.89), kind=kOutput, calls=%fused_computation.5 | convolution fusion | flops 67633152 | bytes 2621472 | tf_op jit(solution)/shard_map/nst,nqt->nsq/dot_general | solution.py:62
  18.4 0.0 reduce-scatter.2.cloned.1.call-update
  18.4 60.3 %reduce-scatter.2.cloned.1.call-done = f32[1,2,64,128]{3,2,1,0:T(8,128)} async-done(((f32[16,2,64,128]{3,2,1,0:T(8,128)}), f32[1,2,64,128]{3,2,1,0:T(8,128)}) %reduce-scatter.2.cloned.1.call-update) | async-done | bytes 65552 | tf_op jit(solution)/shard_map/reduce_scatter | solution.py:65
  78.7 0.0 copy-done.3
  78.7 0.0 copy-done.4
  78.7 1.6 %fusion.4 = (f32[2]{0:T(128)S(1)}, f32[1,2,64,128]{3,2,1,0:T(8,128)}, bf16[1,2,64,128]{3,2,1,0:T(8,128)(2,1)S(1)}) fusion(f32[1,2,64,128]{3,2,1,0:T(8,128)} %reduce-scatter.2.cloned.1.call-done, bf16[1,2,64,128]{3,2,1,0:T(8,128)(2,1)S(1)} %copy-done.3, f32[2]{0:T(128)S(1)} %bitcast.48, pred[2]{0:T(512)(128)(4,1)S(1)} %fusion.14), kind=kLoop, calls=%fused_computation.13 | loop fusion | flops 114686 | bytes 196626 | tf_op jit(solution)/shard_map/reduce_sum | solution.py:76
  80.3 4.9 %psum.7 = f32[1,2]{1,0:T(1,128)S(1)} all-reduce(f32[1,2]{1,0:T(1,128)S(1)} %bitcast.49), channel_id=1, replica_groups=mesh['dp'=16,'group'=2] {'group'}, use_global_device_ids=true, to_apply=%region_4.5 | all-reduce | flops 2 | bytes 16 | tf_op jit(solution)/shard_map/psum | solution.py:77
  85.2 0.5 broadcast_select_fusion
  85.7 20.8 %all_gather.3 = bf16[16,2,64,128]{3,2,1,0:T(8,128)(2,1)S(1)} all-gather(bf16[1,2,64,128]{3,2,1,0:T(8,128)(2,1)S(1)} %get-tuple-element.5), channel_id=1, replica_groups=mesh['dp'=16,'group'=2] {'dp'}, dimensions={0}, use_global_device_ids=true | all-gather | bytes 557056 | tf_op jit(solution)/shard_map/all_gather | solution.py:47
  106.5 0.1 bitcast_select_fusion
  106.6 1.4 %fusion.16 = f32[32,64,128]{2,1,0:T(8,128)} fusion(bf16[32,64,128]{2,1,0:T(8,128)(2,1)S(1)} %bitcast_select_fusion, bf16[32,128,128]{2,1,0:T(8,128)(2,1)S(1)} %gather_fusion.2), kind=kOutput, calls=%fused_computation.45 | convolution fusion | flops 67108864 | bytes 2621440 | tf_op jit(solution)/shard_map/nsq,nqt->nst/dot_general | solution.py:53
  108.0 0.2 broadcast_in_dim.45
  108.2 3.8 %scatter_fusion = f32[64,64,128]{2,1,0:T(8,128)S(1)} fusion(f32[64,64,128]{2,1,0:T(8,128)S(1)} %broadcast_in_dim.45, s32[32]{0:T(128)S(1)} %get-tuple-element.7, f32[32,64,128]{2,1,0:T(8,128)} %fusion.16), kind=kCustom, calls=%fused_computation.4 | custom fusion | flops 262144 | bytes 3145856 | tf_op jit(solution)/shard_map/scatter-add | solution.py:54
  112.0 1.2 convert_element_type.12
  (8 shorter events, 0.1 us)
Async XLA Ops:
  7.2 4.9 %copy-start = (bf16[64,64,128]{2,1,0:T(8,128)(2,1)S(1)}, bf16[64,64,128]{2,1,0:T(8,128)(2,1)}, u32[]{:S(2)}) copy-start(bf16[64,64,128]{2,1,0:T(8,128)(2,1)} %param.7) | copy-start | bytes 3145732
  7.2 2.6 %copy-start.1 = (s32[24]{0:T(128)S(1)}, s32[24]{0:T(128)}, u32[]{:S(2)}) copy-start(s32[24]{0:T(128)} %param.12) | copy-start | bytes 292
  7.2 71.5 %reduce-scatter.2.cloned.1.call-start = ((), (), s32[]{:S(2)}) async-start(), calls=%async_computation.1 | async-start | bytes 1114112 | tf_op jit(solution)/shard_map/reduce_scatter | solution.py:65
  10.5 0.8 copy-start.2
  16.5 62.1 %copy-start.3 = (bf16[1,2,64,128]{3,2,1,0:T(8,128)(2,1)S(1)}, bf16[1,2,64,128]{3,2,1,0:T(8,128)(2,1)}, u32[]{:S(2)}) copy-start(bf16[1,2,64,128]{3,2,1,0:T(8,128)(2,1)} %param.9) | copy-start | bytes 98308
  16.6 62.1 %copy-start.4 = (f32[1,2]{1,0:T(1,128)S(1)}, f32[1,2]{1,0:T(1,128)}, u32[]{:S(2)}) copy-start(f32[1,2]{1,0:T(1,128)} %param.10) | copy-start | bytes 28
Sparse Core Ops, SparseCore 0:
  18.5 60.1 reduce-scatter.1
where the time goes:
time: 120 us
  waiting for transfers between devices  60.3 us (50%)
  blocking collectives  25.7 us (21%)
  between operations  14.2 us (12%)
  other arithmetic  8.95 us (7%)
  local copies, waits for them, and re-layouts  7.71 us (6%)
  matrix products  3.19 us (3%)
    reduce_scatter x1, waiting for transfers between devices, on_device(): lax.psum_scatter(product.reshape(owner_total, slot_count, slab_rows, bloc...  60.3 us
    all_gather x1, blocking collectives, on_device(): gathered = lax.all_gather(scaled, 'dp', axis=0, tiled=True)  20.8 us
    psum x1, blocking collectives, on_device(): scale_total = lax.psum(partial_scale, 'group')  4.92 us
    gather x1, local copies, waits for them, and re-layouts, on_device(): columns_all = grad_view[source_rows]  3.83 us
    scatter-add x1, other arithmetic, on_device(): totals = empty_sum.at[rows_here].add(contrib)  3.79 us
  transfers between devices with their start and end apart: 1, of which 1 were waited for; matrix products, arithmetic and copies ran while one was open for 0% of the time, Pallas kernels for 0%

commit v1 on v0

v1 whole, which is shorter than its diff:
```python
import functools
import math

import jax
import jax.numpy as jnp
from jax import lax
from jax.experimental import pallas as pl
from jax.experimental.pallas import tpu as pltpu
from jax.sharding import PartitionSpec as P

VMEM_LIMIT = 48 * 1024 * 1024
TAIL = 16
UNIT = 2.0**15
SMEM_SPEC = pl.BlockSpec(memory_space=pltpu.SMEM)
VMEM_SPEC = pl.BlockSpec(memory_space=pltpu.VMEM)
ANY_SPEC = pl.BlockSpec(memory_space=pl.ANY)
HBM_SPEC = pl.BlockSpec(memory_space=pltpu.HBM)


def magic_divide(value, divisor, limit):
    shift = 20
    factor = -(-(1 << shift) // divisor)
    assert limit * factor < 1 << 31
    assert all((v * factor) >> shift == v // divisor for v in range(limit))
    return (value * factor) >> shift


def partial_kernel(
    kept_hbm, assign_hbm, counts_hbm, x_hbm, grad_ref, stored_hbm, scales_hbm,
    near_keep, near_send, far_keep, far_send, cols_ref, tab_ref, scaled_ref, stored_ref, scale_rows,
    part_ref, x_ref, scales_ref, kept, assign, counts, slot_ref, sem, index_sems, x_sem
):
    x_copy = pltpu.make_async_copy(x_hbm, x_ref, x_sem)
    index_copies = [
        pltpu.make_async_copy(source, target, index_sems.at[i])
        for i, (source, target) in enumerate(
            (
                (assign_hbm, assign),
                (kept_hbm, kept),
                (counts_hbm, counts),
                (scales_hbm, scales_ref),
                (stored_hbm, stored_ref),
            )
        )
    ]
    for copy in index_copies:
        copy.start()
    x_copy.start()
    keep_count = kept.shape[1]
    hid_blocks = grad_ref.shape[1]
    total = x_ref.shape[0] * hid_blocks
    owners = counts.shape[0]
    entries = assign.shape[0]
    outer, cap = near_keep.shape[:2]
    me = lax.axis_index("dp")
    part_ref[...] = jnp.zeros_like(part_ref)
    for copy in index_copies[:2]:
        copy.wait()

    def fetch_step(p, carry):
        entry = assign[p]
        matrix = jnp.where(entry >= keep_count, 1, 0)
        block = kept[matrix, entry - matrix * keep_count]
        row = magic_divide(block, hid_blocks, total)
        column = block - row * hid_blocks
        pltpu.make_async_copy(grad_ref.at[matrix, column], cols_ref.at[p], sem).start()
        tab_ref[0, p] = row
        return carry

    lax.fori_loop(0, entries, fetch_step, 0, unroll=min(entries, 24))
    for copy in index_copies[2:]:
        copy.wait()

    def owner_step(owner, offset):
        kind = (owner & 3) ^ (me & 3)
        if is_paired(outer):
            step_to = step_from = (owner >> 2) ^ (me >> 2)
        else:
            away = (owner >> 2) - (me >> 2)
            step_to = jnp.where(away < 0, away + outer, away)
            step_from = jnp.where(away > 0, outer - away, -away)
        for c in range(cap):

            @pl.when(c < counts[owner])
            def _():
                p = offset + c
                slot_ref[p] = (kind * outer + step_to) * cap + c
                tab_ref[1, p] = kind
                tab_ref[2, p] = step_from
                tab_ref[3, p] = c

        return offset + counts[owner]

    lax.fori_loop(0, owners, owner_step, 0, unroll=min(owners, 16))
    for c in range(cap):
        scaled = scales_ref[0, c] * stored_ref[0, c].astype(jnp.float32)
        scaled_ref[c] = scaled.astype(jnp.bfloat16)
        scale_rows[c] = jnp.full(scale_rows.shape[1:], scales_ref[0, c], jnp.float32)
    x_copy.wait()
    pltpu.make_async_copy(cols_ref, cols_ref, sem).wait()

    def entry_step(p, carry):
        part_ref[slot_ref[p]] = lax.dot_general(
            x_ref[tab_ref[0, p]],
            cols_ref[p],
            (((1,), (1,)), ((), ())),
            preferred_element_type=jnp.float32,
        )
        return carry

    lax.fori_loop(0, entries, entry_step, 0, unroll=min(entries, 24))
    size = outer * cap
    for kind, ref in enumerate((near_keep, near_send, far_keep, far_send)):
        ref[...] = part_ref[kind * size : (kind + 1) * size].reshape(ref.shape)


def encode(total):
    largest = jnp.max(jnp.abs(total), axis=0, keepdims=True)
    power = jnp.ceil(jnp.log2(jnp.maximum(largest, 2.0**-126)))
    power = jnp.clip(power, -126.0, 126.0)
    level = jnp.floor(total * jnp.exp2(-power) * UNIT + 0.5)
    level = jnp.clip(level, -UNIT, UNIT - 1.0)
    return level.astype(jnp.int32).astype(jnp.int16), power


def message_rows(blocks, slab_rows):
    return blocks * slab_rows + -(-blocks // TAIL) * TAIL


def write_message(totals, out_ref):
    blocks, (slab_rows, side) = len(totals), totals[0].shape
    tail_rows = out_ref.shape[0] - blocks * slab_rows
    tail_row = lax.broadcasted_iota(jnp.int32, (tail_rows, side), 0)
    tail = jnp.zeros((tail_rows, side), jnp.float32)
    for i, total in enumerate(totals):
        level, power = encode(total)
        out_ref[i * slab_rows : (i + 1) * slab_rows] = level
        tail = jnp.where(tail_row == i, power, tail)
    out_ref[blocks * slab_rows :] = tail.astype(jnp.int32).astype(jnp.int16)


def read_message(blocks, slab_rows, ref):
    powers = ref[blocks * slab_rows :].astype(jnp.int32).astype(jnp.float32)
    units = jnp.exp2(powers) * (1.0 / UNIT)
    totals = []
    for i in range(blocks):
        level = ref[i * slab_rows : (i + 1) * slab_rows].astype(jnp.int32)
        totals.append(level.astype(jnp.float32) * units[i : i + 1])
    return totals


def far_sum_kernel(keep_ref, got_ref, near_send, out_ref, near_out):
    near_out[...] = near_send[...]
    outer, cap = keep_ref.shape[:2]
    totals = [keep_ref[k, c] + got_ref[k, c] for k in range(outer) for c in range(cap)]
    write_message(totals, out_ref)


def near_sum_kernel(keep_ref, got_ref, far_ref, *out_refs):
    outer, cap, slab_rows, side = keep_ref.shape
    far = read_message(outer * cap, slab_rows, far_ref)
    for step in range(outer):
        totals = [
            keep_ref[step, c] + got_ref[step, c] + far[step * cap + c] for c in range(cap)
        ]
        if step == 0:
            for c in range(cap):
                out_refs[0][c] = totals[c]
        else:
            write_message(totals, out_refs[step])


def add_kernel(own_ref, *refs):
    *got_refs, out_ref = refs
    cap, slab_rows, side = own_ref.shape
    totals = [own_ref[c] for c in range(cap)]
    for got_ref in got_refs:
        totals = [a + b for a, b in zip(totals, read_message(cap, slab_rows, got_ref))]
    for c in range(cap):
        out_ref[c] = totals[c]


def stack_kernel(*refs):
    *in_refs, _, out_ref = refs
    at = 0
    for in_ref in in_refs:
        if in_ref.ndim < out_ref.ndim:
            out_ref[at] = in_ref[...]
            at += 1
        else:
            out_ref[at : at + in_ref.shape[0]] = in_ref[...]
            at += in_ref.shape[0]


def input_grad_kernel(tab_ref, cols_ref, mine, other, block_ref, out_ref, block_out, acc_ref):
    entries = cols_ref.shape[0]
    block_out[...] = block_ref[...]
    acc_ref[...] = jnp.zeros_like(acc_ref)

    def entry_step(p, carry):
        kind, behind, c = tab_ref[1, p], tab_ref[2, p], tab_ref[3, p]
        block = jnp.where(
            (kind & 1) == 0, mine[behind, kind >> 1, c], other[behind, kind >> 1, c]
        )
        row = tab_ref[0, p]
        acc_ref[row] += jnp.dot(block, cols_ref[p], preferred_element_type=jnp.float32)
        return carry

    lax.fori_loop(0, entries, entry_step, 0, unroll=min(entries, 24))
    out_ref[...] = acc_ref[...].astype(out_ref.dtype)


def owner_sum_kernel(norm, scales_ref, stored_ref, own_ref, *refs):
    got_refs, (block_ref, dots_ref) = refs[:-2], refs[-2:]
    cap, slab_rows, side = stored_ref.shape[1:]
    totals = [own_ref[c] for c in range(cap)]
    for got_ref in got_refs:
        totals = [a + b for a, b in zip(totals, read_message(cap, slab_rows, got_ref))]
    for c in range(cap):
        gradient = totals[c] * norm
        block_ref[0, c] = scales_ref[c, 0:1] * gradient
        dots_ref[c : c + 1, :] = jnp.sum(
            stored_ref[0, c].astype(jnp.float32) * gradient, axis=0, keepdims=True
        )


def finish_kernel(dots_ref, got_ref, grads_ref, scale_out):
    del grads_ref
    total = jnp.sum(dots_ref[...] + got_ref[...], axis=1, keepdims=True)
    cap = total.shape[0]
    row = lax.broadcasted_iota(jnp.int32, (cap, cap), 0)
    column = lax.broadcasted_iota(jnp.int32, (cap, cap), 1)
    scale_out[...] = jnp.sum(jnp.where(row == column, total, 0.0), axis=0, keepdims=True)


def cost(microseconds):
    return pl.CostEstimate(
        flops=int(microseconds * 1_153_000_000), bytes_accessed=int(microseconds * 3_690_000), transcendentals=0
    )


def in_hbm(value):
    return pltpu.with_memory_space_constraint(value, pltpu.HBM)


def flipped(value, bit):
    return lax.ppermute(value, "dp", [(i, i ^ bit) for i in range(lax.axis_size("dp"))])


def is_paired(size):
    return size & (size - 1) == 0


def ahead(places, start, step):
    return start ^ step if is_paired(places) else (start + step) % places


def stepped(value, step):
    size = lax.axis_size("dp")
    return lax.ppermute(
        value, "dp", [(i, ahead(size // 4, i // 4, step) * 4 + i % 4) for i in range(size)]
    )


def stacked(name, estimate, after, *values):
    single = min(value.ndim for value in values)
    count = sum(1 if value.ndim == single else value.shape[0] for value in values)
    shape = (count,) + values[0].shape
    return pl.pallas_call(
        stack_kernel,
        out_shape=jax.ShapeDtypeStruct(shape, values[0].dtype),
        in_specs=[VMEM_SPEC] * len(values) + [ANY_SPEC],
        out_specs=VMEM_SPEC,
        compiler_params=pltpu.CompilerParams(vmem_limit_bytes=VMEM_LIMIT),
        cost_estimate=cost(estimate),
        name=name,
    )(*values, after)


def on_device(
    inputs_t, grad_proj, stored_blocks, block_scales, kept_blocks, assignment, owner_counts
):
    row_blocks, slab_rows, tokens_here = inputs_t.shape
    cap, side = stored_blocks.shape[1], stored_blocks.shape[3]
    entries = assignment.shape[0]
    devices = lax.axis_size("dp")
    outer = devices // 4
    norm = 1.0 / math.sqrt(tokens_here * devices)
    params = pltpu.CompilerParams(vmem_limit_bytes=VMEM_LIMIT)
    block_shape = (cap, slab_rows, side)
    side_shape = (outer, cap, slab_rows, side)
    message_shape = (message_rows(cap, slab_rows), side)

    near_keep, near_send, far_keep, far_send, columns, table, scaled, stored, scale_rows = pl.pallas_call(
        partial_kernel,
        out_shape=[jax.ShapeDtypeStruct(side_shape, jnp.float32)] * 4
        + [
            jax.ShapeDtypeStruct((entries, side, tokens_here), jnp.bfloat16),
            jax.ShapeDtypeStruct((4, entries), jnp.int32),
            jax.ShapeDtypeStruct(block_shape, jnp.bfloat16),
            jax.ShapeDtypeStruct(stored_blocks.shape, jnp.bfloat16),
            jax.ShapeDtypeStruct((cap, 8, side), jnp.float32),
        ],
        in_specs=[HBM_SPEC] * 7,
        out_specs=[VMEM_SPEC] * 5 + [SMEM_SPEC] + [VMEM_SPEC] * 3,
        scratch_shapes=[
            pltpu.VMEM((4 * outer * cap, slab_rows, side), jnp.float32),
            pltpu.VMEM(inputs_t.shape, inputs_t.dtype),
            pltpu.SMEM(block_scales.shape, jnp.float32),
            pltpu.SMEM(kept_blocks.shape, jnp.int32),
            pltpu.SMEM(assignment.shape, jnp.int32),
            pltpu.SMEM(owner_counts.shape, jnp.int32),
            pltpu.SMEM((entries,), jnp.int32),
            pltpu.SemaphoreType.DMA,
            pltpu.SemaphoreType.DMA((5,)),
            pltpu.SemaphoreType.DMA,
        ],
        compiler_params=params,
        cost_estimate=cost(3.5),
        name="partials",
    )(
        *map(
            in_hbm,
            (
                kept_blocks,
                assignment,
                owner_counts,
                inputs_t,
                grad_proj,
                stored_blocks,
                block_scales,
            ),
        )
    )

    far_got = flipped(far_send, 1)
    far_scaled = flipped(scaled, 2)
    far_sums, near_send = pl.pallas_call(
        far_sum_kernel,
        out_shape=(
            jax.ShapeDtypeStruct((message_rows(outer * cap, slab_rows), side), jnp.int16),
            jax.ShapeDtypeStruct(side_shape, jnp.float32),
        ),
        in_specs=[VMEM_SPEC] * 3,
        out_specs=(VMEM_SPEC, VMEM_SPEC),
        compiler_params=params,
        cost_estimate=cost(3.0),
        name="far_sums",
    )(far_keep, far_got, near_send)
    near_got = flipped(near_send, 1)

    pair = stacked("pair", 5.0, far_sums, scaled, far_scaled)
    pairs = [pair] + [stepped(pair, step) for step in range(1, outer)]
    own_sum, *near_sums = pl.pallas_call(
        near_sum_kernel,
        out_shape=[jax.ShapeDtypeStruct(block_shape, jnp.float32)]
        + [jax.ShapeDtypeStruct(message_shape, jnp.int16)] * (outer - 1),
        in_specs=[VMEM_SPEC] * 3,
        out_specs=[VMEM_SPEC] * outer,
        compiler_params=params,
        cost_estimate=cost(0.3),
        name="near_sums",
    )(near_keep, near_got, flipped(far_sums, 2))
    received = [stepped(value, step + 1) for step, value in enumerate(near_sums)]

    for number, group in enumerate((received[:1], received[2:])):
        own_sum = pl.pallas_call(
            add_kernel,
            out_shape=jax.ShapeDtypeStruct(block_shape, jnp.float32),
            in_specs=[VMEM_SPEC] * (1 + len(group)),
            out_specs=VMEM_SPEC,
            compiler_params=params,
            cost_estimate=cost(6.0),
            name="add_%d" % number,
        )(own_sum, *group)
    second = stacked("mine_2", 3.0, near_sums[0], *pairs[2:3])
    others = stacked("mine_3", 3.0, second, *pairs[3:])
    mine = stacked("mine", 0.1, others, pair, pairs[1], second, others)
    other = flipped(mine, 1)

    own_grads, dots = pl.pallas_call(
        functools.partial(owner_sum_kernel, norm),
        out_shape=(
            jax.ShapeDtypeStruct((1,) + block_shape, jnp.float32),
            jax.ShapeDtypeStruct((cap, side), jnp.float32),
        ),
        in_specs=[VMEM_SPEC] * 4,
        out_specs=(VMEM_SPEC, VMEM_SPEC),
        compiler_params=params,
        cost_estimate=cost(6.0),
        name="owner_sums",
    )(scale_rows, stored, own_sum, received[1])
    other_dots = lax.ppermute(dots, "group", [(0, 1), (1, 0)])
    grad_inputs_t, block_grads = pl.pallas_call(
        input_grad_kernel,
        out_shape=(
            jax.ShapeDtypeStruct(inputs_t.shape, jnp.bfloat16),
            jax.ShapeDtypeStruct((1,) + block_shape, jnp.float32),
        ),
        in_specs=[SMEM_SPEC] + [VMEM_SPEC] * 4,
        out_specs=(VMEM_SPEC, VMEM_SPEC),
        scratch_shapes=[pltpu.VMEM(inputs_t.shape, jnp.float32)],
        compiler_params=params,
        cost_estimate=cost(2.0),
        name="input_grads",
    )(table, columns, mine, other, own_grads)
    scale_grads = pl.pallas_call(
        finish_kernel,
        out_shape=jax.ShapeDtypeStruct((1, cap), jnp.float32),
        in_specs=[VMEM_SPEC] * 2 + [HBM_SPEC],
        out_specs=VMEM_SPEC,
        compiler_params=params,
        cost_estimate=cost(0.5),
        name="finish",
    )(dots, other_dots, in_hbm(grad_inputs_t))
    return (grad_inputs_t, block_grads, scale_grads)


def solution(mesh):
    return jax.shard_map(
        on_device,
        mesh=mesh,
        in_specs=(
            P(None, "group", "dp"),
            P(None, None, None, "dp"),
            P("dp", None, "group", None),
            P("dp", None),
            P(),
            P(),
            P(),
        ),
        out_specs=(P(None, "group", "dp"), P("dp", None, "group", None), P("dp", None)),
        check_vma=False,
    )
```

time: 120 us -> 27.9 us (0.23)
  waiting for transfers between devices: 60.3 us -> 5.33 us
  blocking collectives: 25.7 us -> 0 us
  starting transfers between devices: 0.04 us -> 15.2 us
  between operations: 14.2 us -> 0.69 us
  other arithmetic: 8.95 us -> 0 us
  local copies, waits for them, and re-layouts: 7.71 us -> 0 us
  Pallas kernels: 0 us -> 6.52 us
  matrix products: 3.19 us -> 0 us
    reduce_scatter x1 -> x0, waiting for transfers between devices: 60.3 us -> none  [on_device(): lax.psum_scatter(product.reshape(owner_total, slot_count, slab_rows, bloc...]
    all_gather x1 -> x0, blocking collectives: 20.8 us -> none  [on_device(): gathered = lax.all_gather(scaled, 'dp', axis=0, tiled=True)]
    ppermute x0 -> x12, starting transfers between devices: none -> 15.2 us  [the longest x6 8.92 us: stepped(): lax.ppermute(value, 'dp', [(i, ahead(size // 4, i // 4, step) * 4 + i % 4...]
    pallas_call x0 -> x12, Pallas kernels: none -> 6.52 us  [the longest x1 3.44 us: on_device(): pl.pallas_call(partial_kernel, out_shape=[jax.ShapeDtypeStruct(side_shape...]
    gather x4 -> x0, local copies, waits for them, and re-layouts: 5.94 us -> none  [the longest x1 3.83 us: on_device(): columns_all = grad_view[source_rows]]
    ppermute x0 -> x12, waiting for transfers between devices: none -> 5.33 us  [the longest x6 5.01 us: stepped(): lax.ppermute(value, 'dp', [(i, ahead(size // 4, i // 4, step) * 4 + i % 4...]
    psum x1 -> x0, blocking collectives: 4.92 us -> none  [on_device(): scale_total = lax.psum(partial_scale, 'group')]
    scatter-add x1 -> x0, other arithmetic: 3.79 us -> none  [on_device(): totals = empty_sum.at[rows_here].add(contrib)]
  transfers between devices with their start and end apart: 1 -> 12, of which waited for: 1 -> 5; matrix products, arithmetic and copies ran while one was open for 0% -> 0% of each run, Pallas kernels for 0% -> 9%
where the time goes in v1:
time: 27.9 us; the launch traced here: 27.7 us
  starting transfers between devices  15.2 us (54%)
  Pallas kernels  6.52 us (23%)
  waiting for transfers between devices  5.33 us (19%)
  between operations  0.69 us (2%)
    ppermute x6, starting transfers between devices, stepped(): lax.ppermute(value, 'dp', [(i, ahead(size // 4, i // 4, step) * 4 + i % 4...  8.92 us
    ppermute x6, waiting for transfers between devices, stepped(): lax.ppermute(value, 'dp', [(i, ahead(size // 4, i // 4, step) * 4 + i % 4...  5.01 us
    ppermute x5, starting transfers between devices, flipped(): lax.ppermute(value, 'dp', [(i, i ^ bit) for i in range(lax.axis_size('dp'...  4.7 us
    pallas_call x1, Pallas kernels, on_device(): pl.pallas_call(partial_kernel, out_shape=[jax.ShapeDtypeStruct(side_shape...  3.44 us
    pallas_call x1, Pallas kernels, on_device(): pl.pallas_call(input_grad_kernel, out_shape=(jax.ShapeDtypeStruct(inputs_...  2.1 us
    ppermute x1, starting transfers between devices, on_device(): other_dots = lax.ppermute(dots, 'group', [(0, 1), (1, 0)])  1.56 us
    pallas_call x1, Pallas kernels, on_device(): pl.pallas_call(finish_kernel, out_shape=jax.ShapeDtypeStruct((1, cap), jn...  0.6 us
  transfers between devices with their start and end apart: 12, of which 5 were waited for; matrix products, arithmetic and copies ran while one was open for 0% of the time, Pallas kernels for 9%

profile of v1, /device:TPU:0, one launch (start us, length us, event | category | flops | bytes accessed | tf_op | source)
XLA Modules:
  0.0 27.7 jit_solution(13243322153501570894)
XLA Ops:
  0.6 3.4 %partials.1 = (f32[4,2,64,128]{3,2,1,0:T(8,128)S(1)}, f32[4,2,64,128]{3,2,1,0:T(8,128)S(1)}, f32[4,2,64,128]{3,2,1,0:T(8,128)S(1)}, f32[4,2,64,128]{3,2,1,0:T(8,...) custom-call(s32[2,3584]{1,0:T(2,128)} %kept_hbm.1, ...), custom_call_target="tpu_custom_call" | custom-call | flops 4035500032 | bytes 12915000 | tf_op jit(solution)/shard_map/partials/pallas_call | solution.py:294
  4.1 0.5 %collective-permute-start.1 = (f32[4,2,64,128]{3,2,1,0:T(8,128)S(1)}, f32[4,2,64,128]{3,2,1,0:T(8,128)S(1)}, u32[]{:S(2)}, u32[]{:S(2)}) collective-permute-start(f32[4,2,64,128]{3,2,1,0:T(8,128)S(1)} %get-tuple-element.26), channel_id=1, source_target_pairs={{0,2},{2,0},{4,6},{6,4},{8,10},{10,8},{12,14},{14,12},{16,18},{18,... | collective-permute-start | bytes 786440 | tf_op jit(solution)/shard_map/ppermute | solution.py:247
  4.6 2.6 %collective-permute-start = (bf16[2,64,128]{2,1,0:T(8,128)(2,1)S(1)}, bf16[2,64,128]{2,1,0:T(8,128)(2,1)S(1)}, u32[]{:S(2)}, u32[]{:S(2)}) collective-permute-start(bf16[2,64,128]{2,1,0:T(8,128)(2,1)S(1)} %get-tuple-element.24.refs_0_), channel_id=1, source_target_pairs={{0,4},{2,6},{4,0},{6,2},{8,12},{10,14},{12,8},{14,10},{16,20},{18,... | collective-permute-start | bytes 98312 | tf_op jit(solution)/shard_map/ppermute | solution.py:247
  7.2 0.0 collective-permute-done.1.got_ref
  7.2 0.1 far_sums.1
  7.4 1.5 %collective-permute-start.5 = (s16[528,128]{1,0:T(8,128)(2,1)S(1)}, s16[528,128]{1,0:T(8,128)(2,1)S(1)}, u32[]{:S(2)}, u32[]{:S(2)}) collective-permute-start(s16[528,128]{1,0:T(8,128)(2,1)S(1)} %get-tuple-element.28.refs_2_), channel_id=1, source_target_pairs={{0,4},{2,6},{4,0},{6,2},{8,12},{10,14},{12,8},{14,10},{16,20},{18,... | collective-permute-start | bytes 405512 | tf_op jit(solution)/shard_map/ppermute | solution.py:247
  8.9 0.0 collective-permute-start.4
  8.9 0.3 %collective-permute-done.refs_1_ = bf16[2,64,128]{2,1,0:T(8,128)(2,1)S(1)} collective-permute-done((bf16[2,64,128]{2,1,0:T(8,128)(2,1)S(1)}, bf16[2,64,128]{2,1,0:T(8,128)(2,1)S(1)}, u32[]{:S(2)}, u32[]{:S(2)}) %collective-permute-start) | collective-permute-done | bytes 32800 | tf_op jit(solution)/shard_map/ppermute | solution.py:247
  9.2 3.0 %collective-permute-start.3 = (bf16[2,2,64,128]{3,2,1,0:T(8,128)(2,1)S(1)}, bf16[2,2,64,128]{3,2,1,0:T(8,128)(2,1)S(1)}, u32[]{:S(2)}, u32[]{:S(2)}) collective-permute-start(bf16[2,2,64,128]{3,2,1,0:T(8,128)(2,1)S(1)} %pair.1.refs_0_), channel_id=1, source_target_pairs={{0,16},{2,18},{4,20},{6,22},{8,24},{10,26},{12,28},{14,30},{16,0},... | collective-permute-start | bytes 196616 | tf_op jit(solution)/shard_map/ppermute | solution.py:260
  12.2 1.3 %collective-permute-start.6 = (bf16[2,2,64,128]{3,2,1,0:T(8,128)(2,1)S(1)}, bf16[2,2,64,128]{3,2,1,0:T(8,128)(2,1)S(1)}, u32[]{:S(2)}, u32[]{:S(2)}) collective-permute-start(bf16[2,2,64,128]{3,2,1,0:T(8,128)(2,1)S(1)} %pair.1.refs_0_), channel_id=1, source_target_pairs={{0,24},{2,26},{4,28},{6,30},{8,16},{10,18},{12,20},{14,22},{16,8},... | collective-permute-start | bytes 196616 | tf_op jit(solution)/shard_map/ppermute | solution.py:260
  13.5 0.2 collective-permute-start.2
  13.8 0.0 collective-permute-done.5.far_ref
  13.8 0.0 collective-permute-done.4.got_ref
  13.8 0.1 near_sums.1
  13.9 1.9 %collective-permute-start.8 = (s16[144,128]{1,0:T(8,128)(2,1)S(1)}, s16[144,128]{1,0:T(8,128)(2,1)S(1)}, u32[]{:S(2)}, u32[]{:S(2)}) collective-permute-start(s16[144,128]{1,0:T(8,128)(2,1)S(1)} %get-tuple-element.31.refs_1_), channel_id=1, source_target_pairs={{0,8},{2,10},{4,12},{6,14},{8,0},{10,2},{12,4},{14,6},{16,24},{18,... | collective-permute-start | bytes 110600 | tf_op jit(solution)/shard_map/ppermute | solution.py:260
  15.8 2.5 %collective-permute-start.9 = (s16[144,128]{1,0:T(8,128)(2,1)S(1)}, s16[144,128]{1,0:T(8,128)(2,1)S(1)}, u32[]{:S(2)}, u32[]{:S(2)}) collective-permute-start(s16[144,128]{1,0:T(8,128)(2,1)S(1)} %get-tuple-element.35), channel_id=1, source_target_pairs={{0,24},{2,26},{4,28},{6,30},{8,16},{10,18},{12,20},{14,22},{16,8},... | collective-permute-start | bytes 110600 | tf_op jit(solution)/shard_map/ppermute | solution.py:260
  18.3 0.0 collective-permute-done.3.refs_0_
  18.3 0.0 collective-permute-start.10
  18.3 0.4 %collective-permute-done.6.refs_0_ = bf16[2,2,64,128]{3,2,1,0:T(8,128)(2,1)S(1)} collective-permute-done((bf16[2,2,64,128]{3,2,1,0:T(8,128)(2,1)S(1)}, bf16[2,2,64,128]{3,2,1,0:T(8,128)(2,1)S(1)}, u32[]{:S(2)}, u32[]{:S(2)}) %collective-permute-start.6) | collective-permute-done | bytes 65568 | tf_op jit(solution)/shard_map/ppermute | solution.py:260
  18.7 0.0 collective-permute-done.2.refs_1_
  18.7 0.1 collective-permute-start.7
  18.8 0.4 %collective-permute-done.8.refs_0_ = s16[144,128]{1,0:T(8,128)(2,1)S(1)} collective-permute-done((s16[144,128]{1,0:T(8,128)(2,1)S(1)}, s16[144,128]{1,0:T(8,128)(2,1)S(1)}, u32[]{:S(2)}, u32[]{:S(2)}) %collective-permute-start.8) | collective-permute-done | bytes 36896 | tf_op jit(solution)/shard_map/ppermute | solution.py:260
  19.2 2.6 %collective-permute-done.9.refs_0_ = s16[144,128]{1,0:T(8,128)(2,1)S(1)} collective-permute-done((s16[144,128]{1,0:T(8,128)(2,1)S(1)}, s16[144,128]{1,0:T(8,128)(2,1)S(1)}, u32[]{:S(2)}, u32[]{:S(2)}) %collective-permute-start.9) | collective-permute-done | bytes 36896 | tf_op jit(solution)/shard_map/ppermute | solution.py:260
  21.9 1.5 %collective-permute-done.10.refs_0_ = s16[144,128]{1,0:T(8,128)(2,1)S(1)} collective-permute-done((s16[144,128]{1,0:T(8,128)(2,1)S(1)}, s16[144,128]{1,0:T(8,128)(2,1)S(1)}, u32[]{:S(2)}, u32[]{:S(2)}) %collective-permute-start.10) | collective-permute-done | bytes 36896 | tf_op jit(solution)/shard_map/ppermute | solution.py:260
  23.5 1.6 %collective-permute-start.11 = (f32[2,128]{1,0:T(2,128)S(1)}, f32[2,128]{1,0:T(2,128)S(1)}, u32[]{:S(2)}, u32[]{:S(2)}) collective-permute-start(f32[2,128]{1,0:T(2,128)S(1)} %get-tuple-element.40.dots_ref), channel_id=1, source_target_pairs={{0,1},{1,0},{2,3},{3,2},{4,5},{5,4},{6,7},{7,6},{8,9},{9,8},{10,11... | collective-permute-start | bytes 3080 | tf_op jit(solution)/shard_map/ppermute | solution.py:393
  25.0 0.0 collective-permute-done.7.other
  25.0 2.1 %input_grads.1 = (bf16[64,64,128]{2,1,0:T(8,128)(2,1)}, f32[1,2,64,128]{3,2,1,0:T(8,128)}) custom-call(s32[4,24]{1,0:T(4,128)S(1)} %get-tuple-element.22.tab_ref, bf16[24,128,128]{2,1,0:T(8,128)(2,1)S(1)} %get-tuple-element.23.cols_ref, bf16[4,2,2,64,128]{4,3,2,1,0:T(8,128)(2,1)S(1)} %mine.1, bf16[4,2,2,64,128]{4,3,2,1,0:T(8,128)(2,1)S(1)} %collective-permute-done.7.other, ...), custom_call_target="tpu_custom_call" | custom-call | flops 2305999872 | bytes 7380000 | tf_op jit(solution)/shard_map/input_grads/pallas_call | solution.py:394
  27.1 0.0 collective-permute-done.11.got_ref
  27.1 0.6 %finish.1 = f32[1,2]{1,0:T(1,128)} custom-call(f32[2,128]{1,0:T(2,128)S(1)} %get-tuple-element.40.dots_ref, f32[2,128]{1,0:T(2,128)S(1)} %collective-permute-done.11.got_ref, bf16[64,64,128]{2,1,0:T(8,128)(2,1)} %get-tuple-element.19.grads_ref), custom_call_target="tpu_custom_call" | custom-call | flops 576499968 | bytes 1845000 | tf_op jit(solution)/shard_map/finish/pallas_call | solution.py:407
  (7 shorter events, 0.1 us)
Async XLA Ops:
  4.1 3.1 %collective-permute-start.1 = (f32[4,2,64,128]{3,2,1,0:T(8,128)S(1)}, f32[4,2,64,128]{3,2,1,0:T(8,128)S(1)}, u32[]{:S(2)}, u32[]{:S(2)}) collective-permute-start(f32[4,2,64,128]{3,2,1,0:T(8,128)S(1)} %get-tuple-element.26), channel_id=1, source_target_pairs={{0,2},{2,0},{4,6},{6,4},{8,10},{10,8},{12,14},{14,12},{16,18},{18,... | collective-permute-start | bytes 786440 | tf_op jit(solution)/shard_map/ppermute | solution.py:247
  4.6 4.6 %collective-permute-start = (bf16[2,64,128]{2,1,0:T(8,128)(2,1)S(1)}, bf16[2,64,128]{2,1,0:T(8,128)(2,1)S(1)}, u32[]{:S(2)}, u32[]{:S(2)}) collective-permute-start(bf16[2,64,128]{2,1,0:T(8,128)(2,1)S(1)} %get-tuple-element.24.refs_0_), channel_id=1, source_target_pairs={{0,4},{2,6},{4,0},{6,2},{8,12},{10,14},{12,8},{14,10},{16,20},{18,... | collective-permute-start | bytes 98312 | tf_op jit(solution)/shard_map/ppermute | solution.py:247
  7.4 6.4 %collective-permute-start.5 = (s16[528,128]{1,0:T(8,128)(2,1)S(1)}, s16[528,128]{1,0:T(8,128)(2,1)S(1)}, u32[]{:S(2)}, u32[]{:S(2)}) collective-permute-start(s16[528,128]{1,0:T(8,128)(2,1)S(1)} %get-tuple-element.28.refs_2_), channel_id=1, source_target_pairs={{0,4},{2,6},{4,0},{6,2},{8,12},{10,14},{12,8},{14,10},{16,20},{18,... | collective-permute-start | bytes 405512 | tf_op jit(solution)/shard_map/ppermute | solution.py:247
  8.9 4.9 %collective-permute-start.4 = (f32[4,2,64,128]{3,2,1,0:T(8,128)S(1)}, f32[4,2,64,128]{3,2,1,0:T(8,128)S(1)}, u32[]{:S(2)}, u32[]{:S(2)}) collective-permute-start(f32[4,2,64,128]{3,2,1,0:T(8,128)S(1)} %get-tuple-element.30), channel_id=1, source_target_pairs={{0,2},{2,0},{4,6},{6,4},{8,10},{10,8},{12,14},{14,12},{16,18},{18,... | collective-permute-start | bytes 786440 | tf_op jit(solution)/shard_map/ppermute | solution.py:247
  9.2 9.1 %collective-permute-start.3 = (bf16[2,2,64,128]{3,2,1,0:T(8,128)(2,1)S(1)}, bf16[2,2,64,128]{3,2,1,0:T(8,128)(2,1)S(1)}, u32[]{:S(2)}, u32[]{:S(2)}) collective-permute-start(bf16[2,2,64,128]{3,2,1,0:T(8,128)(2,1)S(1)} %pair.1.refs_0_), channel_id=1, source_target_pairs={{0,16},{2,18},{4,20},{6,22},{8,24},{10,26},{12,28},{14,30},{16,0},... | collective-permute-start | bytes 196616 | tf_op jit(solution)/shard_map/ppermute | solution.py:260
  12.2 6.5 %collective-permute-start.6 = (bf16[2,2,64,128]{3,2,1,0:T(8,128)(2,1)S(1)}, bf16[2,2,64,128]{3,2,1,0:T(8,128)(2,1)S(1)}, u32[]{:S(2)}, u32[]{:S(2)}) collective-permute-start(bf16[2,2,64,128]{3,2,1,0:T(8,128)(2,1)S(1)} %pair.1.refs_0_), channel_id=1, source_target_pairs={{0,24},{2,26},{4,28},{6,30},{8,16},{10,18},{12,20},{14,22},{16,8},... | collective-permute-start | bytes 196616 | tf_op jit(solution)/shard_map/ppermute | solution.py:260
  13.5 5.2 %collective-permute-start.2 = (bf16[2,2,64,128]{3,2,1,0:T(8,128)(2,1)S(1)}, bf16[2,2,64,128]{3,2,1,0:T(8,128)(2,1)S(1)}, u32[]{:S(2)}, u32[]{:S(2)}) collective-permute-start(bf16[2,2,64,128]{3,2,1,0:T(8,128)(2,1)S(1)} %pair.1.refs_0_), channel_id=1, source_target_pairs={{0,8},{2,10},{4,12},{6,14},{8,0},{10,2},{12,4},{14,6},{16,24},{18,... | collective-permute-start | bytes 196616 | tf_op jit(solution)/shard_map/ppermute | solution.py:260
  13.9 5.3 %collective-permute-start.8 = (s16[144,128]{1,0:T(8,128)(2,1)S(1)}, s16[144,128]{1,0:T(8,128)(2,1)S(1)}, u32[]{:S(2)}, u32[]{:S(2)}) collective-permute-start(s16[144,128]{1,0:T(8,128)(2,1)S(1)} %get-tuple-element.31.refs_1_), channel_id=1, source_target_pairs={{0,8},{2,10},{4,12},{6,14},{8,0},{10,2},{12,4},{14,6},{16,24},{18,... | collective-permute-start | bytes 110600 | tf_op jit(solution)/shard_map/ppermute | solution.py:260
  15.8 6.1 %collective-permute-start.9 = (s16[144,128]{1,0:T(8,128)(2,1)S(1)}, s16[144,128]{1,0:T(8,128)(2,1)S(1)}, u32[]{:S(2)}, u32[]{:S(2)}) collective-permute-start(s16[144,128]{1,0:T(8,128)(2,1)S(1)} %get-tuple-element.35), channel_id=1, source_target_pairs={{0,24},{2,26},{4,28},{6,30},{8,16},{10,18},{12,20},{14,22},{16,8},... | collective-permute-start | bytes 110600 | tf_op jit(solution)/shard_map/ppermute | solution.py:260
  18.3 5.2 %collective-permute-start.10 = (s16[144,128]{1,0:T(8,128)(2,1)S(1)}, s16[144,128]{1,0:T(8,128)(2,1)S(1)}, u32[]{:S(2)}, u32[]{:S(2)}) collective-permute-start(s16[144,128]{1,0:T(8,128)(2,1)S(1)} %get-tuple-element.36), channel_id=1, source_target_pairs={{0,16},{2,18},{4,20},{6,22},{8,24},{10,26},{12,28},{14,30},{16,0},... | collective-permute-start | bytes 110600 | tf_op jit(solution)/shard_map/ppermute | solution.py:260
  18.7 6.3 %collective-permute-start.7 = (bf16[4,2,2,64,128]{4,3,2,1,0:T(8,128)(2,1)S(1)}, bf16[4,2,2,64,128]{4,3,2,1,0:T(8,128)(2,1)S(1)}, u32[]{:S(2)}, u32[]{:S(2)}) collective-permute-start(bf16[4,2,2,64,128]{4,3,2,1,0:T(8,128)(2,1)S(1)} %mine.1), channel_id=1, source_target_pairs={{0,2},{2,0},{4,6},{6,4},{8,10},{10,8},{12,14},{14,12},{16,18},{18,... | collective-permute-start | bytes 786440 | tf_op jit(solution)/shard_map/ppermute | solution.py:247
  23.5 3.7 %collective-permute-start.11 = (f32[2,128]{1,0:T(2,128)S(1)}, f32[2,128]{1,0:T(2,128)S(1)}, u32[]{:S(2)}, u32[]{:S(2)}) collective-permute-start(f32[2,128]{1,0:T(2,128)S(1)} %get-tuple-element.40.dots_ref), channel_id=1, source_target_pairs={{0,1},{1,0},{2,3},{3,2},{4,5},{5,4},{6,7},{7,6},{8,9},{9,8},{10,11... | collective-permute-start | bytes 3080 | tf_op jit(solution)/shard_map/ppermute | solution.py:393

commit v2 on v1

--- a/solution.py
+++ b/solution.py
@@ -363,7 +363,7 @@
     )(near_keep, near_got, flipped(far_sums, 2))
     received = [stepped(value, step + 1) for step, value in enumerate(near_sums)]
 
-    for number, group in enumerate((received[:1], received[2:])):
+    for number, group in enumerate((received[2:], received[1:2])):
         own_sum = pl.pallas_call(
             add_kernel,
             out_shape=jax.ShapeDtypeStruct(block_shape, jnp.float32),
@@ -389,7 +389,7 @@
         compiler_params=params,
         cost_estimate=cost(6.0),
         name="owner_sums",
-    )(scale_rows, stored, own_sum, received[1])
+    )(scale_rows, stored, own_sum, received[0])
     other_dots = lax.ppermute(dots, "group", [(0, 1), (1, 0)])
     grad_inputs_t, block_grads = pl.pallas_call(
         input_grad_kernel,

time: 27.9 us -> 26.7 us (0.957)
  waiting for transfers between devices: 5.33 us -> 3.92 us
    ppermute x6, waiting for transfers between devices: 5.01 us -> 3.6 us  [stepped(): lax.ppermute(value, 'dp', [(i, ahead(size // 4, i // 4, step) * 4 + i % 4...]
where the time goes in v2:
time: 26.7 us; the launch traced here: 26.4 us
  starting transfers between devices  15.3 us (57%)
  Pallas kernels  6.53 us (24%)
  waiting for transfers between devices  3.92 us (15%)
  between operations  0.7 us (3%)
    ppermute x6, starting transfers between devices, stepped(): lax.ppermute(value, 'dp', [(i, ahead(size // 4, i // 4, step) * 4 + i % 4...  9.03 us
    ppermute x5, starting transfers between devices, flipped(): lax.ppermute(value, 'dp', [(i, i ^ bit) for i in range(lax.axis_size('dp'...  4.7 us
    ppermute x6, waiting for transfers between devices, stepped(): lax.ppermute(value, 'dp', [(i, ahead(size // 4, i // 4, step) * 4 + i % 4...  3.6 us
    pallas_call x1, Pallas kernels, on_device(): pl.pallas_call(partial_kernel, out_shape=[jax.ShapeDtypeStruct(side_shape...  3.44 us
    pallas_call x1, Pallas kernels, on_device(): pl.pallas_call(input_grad_kernel, out_shape=(jax.ShapeDtypeStruct(inputs_...  2.1 us
    ppermute x1, starting transfers between devices, on_device(): other_dots = lax.ppermute(dots, 'group', [(0, 1), (1, 0)])  1.56 us
    pallas_call x1, Pallas kernels, on_device(): pl.pallas_call(finish_kernel, out_shape=jax.ShapeDtypeStruct((1, cap), jn...  0.6 us
  transfers between devices with their start and end apart: 12, of which 5 were waited for; matrix products, arithmetic and copies ran while one was open for 0% of the time, Pallas kernels for 9%

profile of v2, /device:TPU:0, one launch (start us, length us, event | category | flops | bytes accessed | tf_op | source)
XLA Modules:
  0.0 26.4 jit_solution(13204278952303225829)
XLA Ops:
  0.6 3.4 %partials.1 = (f32[4,2,64,128]{3,2,1,0:T(8,128)S(1)}, f32[4,2,64,128]{3,2,1,0:T(8,128)S(1)}, f32[4,2,64,128]{3,2,1,0:T(8,128)S(1)}, f32[4,2,64,128]{3,2,1,0:T(8,...) custom-call(s32[2,3584]{1,0:T(2,128)} %kept_hbm.1, ...), custom_call_target="tpu_custom_call" | custom-call | flops 4035500032 | bytes 12915000 | tf_op jit(solution)/shard_map/partials/pallas_call | solution.py:294
  4.1 0.5 %collective-permute-start.1 = (f32[4,2,64,128]{3,2,1,0:T(8,128)S(1)}, f32[4,2,64,128]{3,2,1,0:T(8,128)S(1)}, u32[]{:S(2)}, u32[]{:S(2)}) collective-permute-start(f32[4,2,64,128]{3,2,1,0:T(8,128)S(1)} %get-tuple-element.26), channel_id=1, source_target_pairs={{0,2},{2,0},{4,6},{6,4},{8,10},{10,8},{12,14},{14,12},{16,18},{18,... | collective-permute-start | bytes 786440 | tf_op jit(solution)/shard_map/ppermute | solution.py:247
  4.6 2.6 %collective-permute-start = (bf16[2,64,128]{2,1,0:T(8,128)(2,1)S(1)}, bf16[2,64,128]{2,1,0:T(8,128)(2,1)S(1)}, u32[]{:S(2)}, u32[]{:S(2)}) collective-permute-start(bf16[2,64,128]{2,1,0:T(8,128)(2,1)S(1)} %get-tuple-element.24.refs_0_), channel_id=1, source_target_pairs={{0,4},{2,6},{4,0},{6,2},{8,12},{10,14},{12,8},{14,10},{16,20},{18,... | collective-permute-start | bytes 98312 | tf_op jit(solution)/shard_map/ppermute | solution.py:247
  7.2 0.0 collective-permute-done.1.got_ref
  7.2 0.1 far_sums.1
  7.4 1.5 %collective-permute-start.5 = (s16[528,128]{1,0:T(8,128)(2,1)S(1)}, s16[528,128]{1,0:T(8,128)(2,1)S(1)}, u32[]{:S(2)}, u32[]{:S(2)}) collective-permute-start(s16[528,128]{1,0:T(8,128)(2,1)S(1)} %get-tuple-element.28.refs_2_), channel_id=1, source_target_pairs={{0,4},{2,6},{4,0},{6,2},{8,12},{10,14},{12,8},{14,10},{16,20},{18,... | collective-permute-start | bytes 405512 | tf_op jit(solution)/shard_map/ppermute | solution.py:247
  8.9 0.0 collective-permute-start.4
  8.9 0.3 %collective-permute-done.refs_1_ = bf16[2,64,128]{2,1,0:T(8,128)(2,1)S(1)} collective-permute-done((bf16[2,64,128]{2,1,0:T(8,128)(2,1)S(1)}, bf16[2,64,128]{2,1,0:T(8,128)(2,1)S(1)}, u32[]{:S(2)}, u32[]{:S(2)}) %collective-permute-start) | collective-permute-done | bytes 32800 | tf_op jit(solution)/shard_map/ppermute | solution.py:247
  9.2 3.0 %collective-permute-start.3 = (bf16[2,2,64,128]{3,2,1,0:T(8,128)(2,1)S(1)}, bf16[2,2,64,128]{3,2,1,0:T(8,128)(2,1)S(1)}, u32[]{:S(2)}, u32[]{:S(2)}) collective-permute-start(bf16[2,2,64,128]{3,2,1,0:T(8,128)(2,1)S(1)} %pair.1.refs_0_), channel_id=1, source_target_pairs={{0,16},{2,18},{4,20},{6,22},{8,24},{10,26},{12,28},{14,30},{16,0},... | collective-permute-start | bytes 196616 | tf_op jit(solution)/shard_map/ppermute | solution.py:260
  12.2 1.3 %collective-permute-start.6 = (bf16[2,2,64,128]{3,2,1,0:T(8,128)(2,1)S(1)}, bf16[2,2,64,128]{3,2,1,0:T(8,128)(2,1)S(1)}, u32[]{:S(2)}, u32[]{:S(2)}) collective-permute-start(bf16[2,2,64,128]{3,2,1,0:T(8,128)(2,1)S(1)} %pair.1.refs_0_), channel_id=1, source_target_pairs={{0,24},{2,26},{4,28},{6,30},{8,16},{10,18},{12,20},{14,22},{16,8},... | collective-permute-start | bytes 196616 | tf_op jit(solution)/shard_map/ppermute | solution.py:260
  13.5 0.2 collective-permute-start.2
  13.8 0.0 collective-permute-done.5.far_ref
  13.8 0.0 collective-permute-done.4.got_ref
  13.8 0.1 near_sums.1
  13.9 3.0 %collective-permute-start.8 = (s16[144,128]{1,0:T(8,128)(2,1)S(1)}, s16[144,128]{1,0:T(8,128)(2,1)S(1)}, u32[]{:S(2)}, u32[]{:S(2)}) collective-permute-start(s16[144,128]{1,0:T(8,128)(2,1)S(1)} %get-tuple-element.35), channel_id=1, source_target_pairs={{0,24},{2,26},{4,28},{6,30},{8,16},{10,18},{12,20},{14,22},{16,8},... | collective-permute-start | bytes 110600 | tf_op jit(solution)/shard_map/ppermute | solution.py:260
  16.9 0.3 %collective-permute-start.9 = (s16[144,128]{1,0:T(8,128)(2,1)S(1)}, s16[144,128]{1,0:T(8,128)(2,1)S(1)}, u32[]{:S(2)}, u32[]{:S(2)}) collective-permute-start(s16[144,128]{1,0:T(8,128)(2,1)S(1)} %get-tuple-element.36), channel_id=1, source_target_pairs={{0,16},{2,18},{4,20},{6,22},{8,24},{10,26},{12,28},{14,30},{16,0},... | collective-permute-start | bytes 110600 | tf_op jit(solution)/shard_map/ppermute | solution.py:260
  17.2 0.0 collective-permute-done.3.refs_0_
  17.2 1.1 %collective-permute-start.10 = (s16[144,128]{1,0:T(8,128)(2,1)S(1)}, s16[144,128]{1,0:T(8,128)(2,1)S(1)}, u32[]{:S(2)}, u32[]{:S(2)}) collective-permute-start(s16[144,128]{1,0:T(8,128)(2,1)S(1)} %get-tuple-element.31.refs_1_), channel_id=1, source_target_pairs={{0,8},{2,10},{4,12},{6,14},{8,0},{10,2},{12,4},{14,6},{16,24},{18,... | collective-permute-start | bytes 110600 | tf_op jit(solution)/shard_map/ppermute | solution.py:260
  18.4 0.4 %collective-permute-done.6.refs_0_ = bf16[2,2,64,128]{3,2,1,0:T(8,128)(2,1)S(1)} collective-permute-done((bf16[2,2,64,128]{3,2,1,0:T(8,128)(2,1)S(1)}, bf16[2,2,64,128]{3,2,1,0:T(8,128)(2,1)S(1)}, u32[]{:S(2)}, u32[]{:S(2)}) %collective-permute-start.6) | collective-permute-done | bytes 65568 | tf_op jit(solution)/shard_map/ppermute | solution.py:260
  18.8 0.1 collective-permute-done.2.refs_1_
  18.9 0.1 collective-permute-start.7
  19.0 1.2 %collective-permute-done.8.refs_0_ = s16[144,128]{1,0:T(8,128)(2,1)S(1)} collective-permute-done((s16[144,128]{1,0:T(8,128)(2,1)S(1)}, s16[144,128]{1,0:T(8,128)(2,1)S(1)}, u32[]{:S(2)}, u32[]{:S(2)}) %collective-permute-start.8) | collective-permute-done | bytes 36896 | tf_op jit(solution)/shard_map/ppermute | solution.py:260
  20.2 1.9 %collective-permute-done.9.refs_0_ = s16[144,128]{1,0:T(8,128)(2,1)S(1)} collective-permute-done((s16[144,128]{1,0:T(8,128)(2,1)S(1)}, s16[144,128]{1,0:T(8,128)(2,1)S(1)}, u32[]{:S(2)}, u32[]{:S(2)}) %collective-permute-start.9) | collective-permute-done | bytes 36896 | tf_op jit(solution)/shard_map/ppermute | solution.py:260
  22.1 0.0 collective-permute-done.10.refs_0_
  22.2 1.6 %collective-permute-start.11 = (f32[2,128]{1,0:T(2,128)S(1)}, f32[2,128]{1,0:T(2,128)S(1)}, u32[]{:S(2)}, u32[]{:S(2)}) collective-permute-start(f32[2,128]{1,0:T(2,128)S(1)} %get-tuple-element.40.dots_ref), channel_id=1, source_target_pairs={{0,1},{1,0},{2,3},{3,2},{4,5},{5,4},{6,7},{7,6},{8,9},{9,8},{10,11... | collective-permute-start | bytes 3080 | tf_op jit(solution)/shard_map/ppermute | solution.py:393
  23.7 0.0 collective-permute-done.7.other
  23.7 2.1 %input_grads.1 = (bf16[64,64,128]{2,1,0:T(8,128)(2,1)}, f32[1,2,64,128]{3,2,1,0:T(8,128)}) custom-call(s32[4,24]{1,0:T(4,128)S(1)} %get-tuple-element.22.tab_ref, bf16[24,128,128]{2,1,0:T(8,128)(2,1)S(1)} %get-tuple-element.23.cols_ref, bf16[4,2,2,64,128]{4,3,2,1,0:T(8,128)(2,1)S(1)} %mine.1, bf16[4,2,2,64,128]{4,3,2,1,0:T(8,128)(2,1)S(1)} %collective-permute-done.7.other, ...), custom_call_target="tpu_custom_call" | custom-call | flops 2305999872 | bytes 7380000 | tf_op jit(solution)/shard_map/input_grads/pallas_call | solution.py:394
  25.8 0.0 collective-permute-done.11.got_ref
  25.8 0.6 %finish.1 = f32[1,2]{1,0:T(1,128)} custom-call(f32[2,128]{1,0:T(2,128)S(1)} %get-tuple-element.40.dots_ref, f32[2,128]{1,0:T(2,128)S(1)} %collective-permute-done.11.got_ref, bf16[64,64,128]{2,1,0:T(8,128)(2,1)} %get-tuple-element.19.grads_ref), custom_call_target="tpu_custom_call" | custom-call | flops 576499968 | bytes 1845000 | tf_op jit(solution)/shard_map/finish/pallas_call | solution.py:407
  (7 shorter events, 0.1 us)
Async XLA Ops:
  4.1 3.1 %collective-permute-start.1 = (f32[4,2,64,128]{3,2,1,0:T(8,128)S(1)}, f32[4,2,64,128]{3,2,1,0:T(8,128)S(1)}, u32[]{:S(2)}, u32[]{:S(2)}) collective-permute-start(f32[4,2,64,128]{3,2,1,0:T(8,128)S(1)} %get-tuple-element.26), channel_id=1, source_target_pairs={{0,2},{2,0},{4,6},{6,4},{8,10},{10,8},{12,14},{14,12},{16,18},{18,... | collective-permute-start | bytes 786440 | tf_op jit(solution)/shard_map/ppermute | solution.py:247
  4.6 4.6 %collective-permute-start = (bf16[2,64,128]{2,1,0:T(8,128)(2,1)S(1)}, bf16[2,64,128]{2,1,0:T(8,128)(2,1)S(1)}, u32[]{:S(2)}, u32[]{:S(2)}) collective-permute-start(bf16[2,64,128]{2,1,0:T(8,128)(2,1)S(1)} %get-tuple-element.24.refs_0_), channel_id=1, source_target_pairs={{0,4},{2,6},{4,0},{6,2},{8,12},{10,14},{12,8},{14,10},{16,20},{18,... | collective-permute-start | bytes 98312 | tf_op jit(solution)/shard_map/ppermute | solution.py:247
  7.4 6.4 %collective-permute-start.5 = (s16[528,128]{1,0:T(8,128)(2,1)S(1)}, s16[528,128]{1,0:T(8,128)(2,1)S(1)}, u32[]{:S(2)}, u32[]{:S(2)}) collective-permute-start(s16[528,128]{1,0:T(8,128)(2,1)S(1)} %get-tuple-element.28.refs_2_), channel_id=1, source_target_pairs={{0,4},{2,6},{4,0},{6,2},{8,12},{10,14},{12,8},{14,10},{16,20},{18,... | collective-permute-start | bytes 405512 | tf_op jit(solution)/shard_map/ppermute | solution.py:247
  8.9 4.9 %collective-permute-start.4 = (f32[4,2,64,128]{3,2,1,0:T(8,128)S(1)}, f32[4,2,64,128]{3,2,1,0:T(8,128)S(1)}, u32[]{:S(2)}, u32[]{:S(2)}) collective-permute-start(f32[4,2,64,128]{3,2,1,0:T(8,128)S(1)} %get-tuple-element.30), channel_id=1, source_target_pairs={{0,2},{2,0},{4,6},{6,4},{8,10},{10,8},{12,14},{14,12},{16,18},{18,... | collective-permute-start | bytes 786440 | tf_op jit(solution)/shard_map/ppermute | solution.py:247
  9.2 8.1 %collective-permute-start.3 = (bf16[2,2,64,128]{3,2,1,0:T(8,128)(2,1)S(1)}, bf16[2,2,64,128]{3,2,1,0:T(8,128)(2,1)S(1)}, u32[]{:S(2)}, u32[]{:S(2)}) collective-permute-start(bf16[2,2,64,128]{3,2,1,0:T(8,128)(2,1)S(1)} %pair.1.refs_0_), channel_id=1, source_target_pairs={{0,16},{2,18},{4,20},{6,22},{8,24},{10,26},{12,28},{14,30},{16,0},... | collective-permute-start | bytes 196616 | tf_op jit(solution)/shard_map/ppermute | solution.py:260
  12.2 6.6 %collective-permute-start.6 = (bf16[2,2,64,128]{3,2,1,0:T(8,128)(2,1)S(1)}, bf16[2,2,64,128]{3,2,1,0:T(8,128)(2,1)S(1)}, u32[]{:S(2)}, u32[]{:S(2)}) collective-permute-start(bf16[2,2,64,128]{3,2,1,0:T(8,128)(2,1)S(1)} %pair.1.refs_0_), channel_id=1, source_target_pairs={{0,24},{2,26},{4,28},{6,30},{8,16},{10,18},{12,20},{14,22},{16,8},... | collective-permute-start | bytes 196616 | tf_op jit(solution)/shard_map/ppermute | solution.py:260
  13.5 5.4 %collective-permute-start.2 = (bf16[2,2,64,128]{3,2,1,0:T(8,128)(2,1)S(1)}, bf16[2,2,64,128]{3,2,1,0:T(8,128)(2,1)S(1)}, u32[]{:S(2)}, u32[]{:S(2)}) collective-permute-start(bf16[2,2,64,128]{3,2,1,0:T(8,128)(2,1)S(1)} %pair.1.refs_0_), channel_id=1, source_target_pairs={{0,8},{2,10},{4,12},{6,14},{8,0},{10,2},{12,4},{14,6},{16,24},{18,... | collective-permute-start | bytes 196616 | tf_op jit(solution)/shard_map/ppermute | solution.py:260
  13.9 6.3 %collective-permute-start.8 = (s16[144,128]{1,0:T(8,128)(2,1)S(1)}, s16[144,128]{1,0:T(8,128)(2,1)S(1)}, u32[]{:S(2)}, u32[]{:S(2)}) collective-permute-start(s16[144,128]{1,0:T(8,128)(2,1)S(1)} %get-tuple-element.35), channel_id=1, source_target_pairs={{0,24},{2,26},{4,28},{6,30},{8,16},{10,18},{12,20},{14,22},{16,8},... | collective-permute-start | bytes 110600 | tf_op jit(solution)/shard_map/ppermute | solution.py:260
  16.9 5.2 %collective-permute-start.9 = (s16[144,128]{1,0:T(8,128)(2,1)S(1)}, s16[144,128]{1,0:T(8,128)(2,1)S(1)}, u32[]{:S(2)}, u32[]{:S(2)}) collective-permute-start(s16[144,128]{1,0:T(8,128)(2,1)S(1)} %get-tuple-element.36), channel_id=1, source_target_pairs={{0,16},{2,18},{4,20},{6,22},{8,24},{10,26},{12,28},{14,30},{16,0},... | collective-permute-start | bytes 110600 | tf_op jit(solution)/shard_map/ppermute | solution.py:260
  17.2 4.9 %collective-permute-start.10 = (s16[144,128]{1,0:T(8,128)(2,1)S(1)}, s16[144,128]{1,0:T(8,128)(2,1)S(1)}, u32[]{:S(2)}, u32[]{:S(2)}) collective-permute-start(s16[144,128]{1,0:T(8,128)(2,1)S(1)} %get-tuple-element.31.refs_1_), channel_id=1, source_target_pairs={{0,8},{2,10},{4,12},{6,14},{8,0},{10,2},{12,4},{14,6},{16,24},{18,... | collective-permute-start | bytes 110600 | tf_op jit(solution)/shard_map/ppermute | solution.py:260
  18.9 4.8 %collective-permute-start.7 = (bf16[4,2,2,64,128]{4,3,2,1,0:T(8,128)(2,1)S(1)}, bf16[4,2,2,64,128]{4,3,2,1,0:T(8,128)(2,1)S(1)}, u32[]{:S(2)}, u32[]{:S(2)}) collective-permute-start(bf16[4,2,2,64,128]{4,3,2,1,0:T(8,128)(2,1)S(1)} %mine.1), channel_id=1, source_target_pairs={{0,2},{2,0},{4,6},{6,4},{8,10},{10,8},{12,14},{14,12},{16,18},{18,... | collective-permute-start | bytes 786440 | tf_op jit(solution)/shard_map/ppermute | solution.py:247
  22.2 3.7 %collective-permute-start.11 = (f32[2,128]{1,0:T(2,128)S(1)}, f32[2,128]{1,0:T(2,128)S(1)}, u32[]{:S(2)}, u32[]{:S(2)}) collective-permute-start(f32[2,128]{1,0:T(2,128)S(1)} %get-tuple-element.40.dots_ref), channel_id=1, source_target_pairs={{0,1},{1,0},{2,3},{3,2},{4,5},{5,4},{6,7},{7,6},{8,9},{9,8},{10,11... | collective-permute-start | bytes 3080 | tf_op jit(solution)/shard_map/ppermute | solution.py:393

commit v3 on v2

--- a/solution.py
+++ b/solution.py
@@ -25,10 +25,33 @@
     return (value * factor) >> shift
 
 
+def slot_blocks(kinds, refs, me, tab_ref, span_ref, x_ref, cols_ref):
+    outer, cap = refs[0].shape[:2]
+    entries = cols_ref.shape[0]
+    home = me >> 2
+
+    def step_blocks(step, carry):
+        place = home ^ step if is_paired(outer) else lax.rem(home + step, outer)
+        for kind, ref in zip(kinds, refs):
+            owner = place * 4 + ((me & 3) ^ kind)
+            for c in range(cap):
+                p = jnp.minimum(span_ref[0, owner] + c, entries - 1)
+                block = lax.dot_general(
+                    x_ref[tab_ref[0, p]],
+                    cols_ref[p],
+                    (((1,), (1,)), ((), ())),
+                    preferred_element_type=jnp.float32,
+                )
+                ref[step, c] = jnp.where(c < span_ref[1, owner], block, 0.0)
+        return carry
+
+    lax.fori_loop(0, outer, step_blocks, 0, unroll=min(outer, 4))
+
+
 def partial_kernel(
     kept_hbm, assign_hbm, counts_hbm, x_hbm, grad_ref, stored_hbm, scales_hbm,
-    near_keep, near_send, far_keep, far_send, cols_ref, tab_ref, scaled_ref, stored_ref, scale_rows,
-    part_ref, x_ref, scales_ref, kept, assign, counts, slot_ref, sem, index_sems, x_sem
+    far_keep, far_send, x_ref, cols_ref, tab_ref, span_ref, scaled_ref, stored_ref, scale_rows,
+    scales_ref, kept, assign, counts, sem, index_sems, x_sem
 ):
     x_copy = pltpu.make_async_copy(x_hbm, x_ref, x_sem)
     index_copies = [
@@ -51,9 +74,8 @@
     total = x_ref.shape[0] * hid_blocks
     owners = counts.shape[0]
     entries = assign.shape[0]
-    outer, cap = near_keep.shape[:2]
+    outer, cap = far_keep.shape[:2]
     me = lax.axis_index("dp")
-    part_ref[...] = jnp.zeros_like(part_ref)
     for copy in index_copies[:2]:
         copy.wait()
 
@@ -74,22 +96,23 @@
     def owner_step(owner, offset):
         kind = (owner & 3) ^ (me & 3)
         if is_paired(outer):
-            step_to = step_from = (owner >> 2) ^ (me >> 2)
+            step_from = (owner >> 2) ^ (me >> 2)
         else:
             away = (owner >> 2) - (me >> 2)
-            step_to = jnp.where(away < 0, away + outer, away)
             step_from = jnp.where(away > 0, outer - away, -away)
+        count = counts[owner]
+        span_ref[0, owner] = offset
+        span_ref[1, owner] = count
         for c in range(cap):
 
-            @pl.when(c < counts[owner])
+            @pl.when(c < count)
             def _():
                 p = offset + c
-                slot_ref[p] = (kind * outer + step_to) * cap + c
                 tab_ref[1, p] = kind
                 tab_ref[2, p] = step_from
                 tab_ref[3, p] = c
 
-        return offset + counts[owner]
+        return offset + count
 
     lax.fori_loop(0, owners, owner_step, 0, unroll=min(owners, 16))
     for c in range(cap):
@@ -98,20 +121,12 @@
         scale_rows[c] = jnp.full(scale_rows.shape[1:], scales_ref[0, c], jnp.float32)
     x_copy.wait()
     pltpu.make_async_copy(cols_ref, cols_ref, sem).wait()
-
-    def entry_step(p, carry):
-        part_ref[slot_ref[p]] = lax.dot_general(
-            x_ref[tab_ref[0, p]],
-            cols_ref[p],
-            (((1,), (1,)), ((), ())),
-            preferred_element_type=jnp.float32,
-        )
-        return carry
-
-    lax.fori_loop(0, entries, entry_step, 0, unroll=min(entries, 24))
-    size = outer * cap
-    for kind, ref in enumerate((near_keep, near_send, far_keep, far_send)):
-        ref[...] = part_ref[kind * size : (kind + 1) * size].reshape(ref.shape)
+    slot_blocks((2, 3), (far_keep, far_send), me, tab_ref, span_ref, x_ref, cols_ref)
+
+
+def near_partial_kernel(tab_ref, span_ref, x_ref, cols_ref, near_keep, near_send):
+    me = lax.axis_index("dp")
+    slot_blocks((0, 1), (near_keep, near_send), me, tab_ref, span_ref, x_ref, cols_ref)
 
 
 def encode(total):
@@ -291,26 +306,27 @@
     side_shape = (outer, cap, slab_rows, side)
     message_shape = (message_rows(cap, slab_rows), side)
 
-    near_keep, near_send, far_keep, far_send, columns, table, scaled, stored, scale_rows = pl.pallas_call(
+    side_sums = jax.ShapeDtypeStruct(side_shape, jnp.float32)
+    far_keep, far_send, rows, columns, table, spans, scaled, stored, scale_rows = pl.pallas_call(
         partial_kernel,
-        out_shape=[jax.ShapeDtypeStruct(side_shape, jnp.float32)] * 4
-        + [
+        out_shape=[
+            side_sums,
+            side_sums,
+            jax.ShapeDtypeStruct(inputs_t.shape, inputs_t.dtype),
             jax.ShapeDtypeStruct((entries, side, tokens_here), jnp.bfloat16),
             jax.ShapeDtypeStruct((4, entries), jnp.int32),
+            jax.ShapeDtypeStruct((2,) + owner_counts.shape, jnp.int32),
             jax.ShapeDtypeStruct(block_shape, jnp.bfloat16),
             jax.ShapeDtypeStruct(stored_blocks.shape, jnp.bfloat16),
             jax.ShapeDtypeStruct((cap, 8, side), jnp.float32),
         ],
         in_specs=[HBM_SPEC] * 7,
-        out_specs=[VMEM_SPEC] * 5 + [SMEM_SPEC] + [VMEM_SPEC] * 3,
+        out_specs=[VMEM_SPEC] * 4 + [SMEM_SPEC] * 2 + [VMEM_SPEC] * 3,
         scratch_shapes=[
-            pltpu.VMEM((4 * outer * cap, slab_rows, side), jnp.float32),
-            pltpu.VMEM(inputs_t.shape, inputs_t.dtype),
             pltpu.SMEM(block_scales.shape, jnp.float32),
             pltpu.SMEM(kept_blocks.shape, jnp.int32),
             pltpu.SMEM(assignment.shape, jnp.int32),
             pltpu.SMEM(owner_counts.shape, jnp.int32),
-            pltpu.SMEM((entries,), jnp.int32),
             pltpu.SemaphoreType.DMA,
             pltpu.SemaphoreType.DMA((5,)),
             pltpu.SemaphoreType.DMA,
@@ -332,6 +348,15 @@
             ),
         )
     )
+    near_keep, near_send = pl.pallas_call(
+        near_partial_kernel,
+        out_shape=[side_sums, side_sums],
+        in_specs=[SMEM_SPEC] * 2 + [VMEM_SPEC] * 2,
+        out_specs=[VMEM_SPEC] * 2,
+        compiler_params=params,
+        cost_estimate=cost(1.0),
+        name="near_partials",
+    )(table, spans, rows, columns)
 
     far_got = flipped(far_send, 1)
     far_scaled = flipped(scaled, 2)

time: 26.7 us -> 27.2 us (1.019)
  starting transfers between devices: 15.3 us -> 14.2 us
  Pallas kernels: 6.53 us -> 7.38 us
  waiting for transfers between devices: 3.92 us -> 4.61 us
    ppermute x5, starting transfers between devices: 4.7 us -> 3.65 us  [flipped(): lax.ppermute(value, 'dp', [(i, i ^ bit) for i in range(lax.axis_size('dp'...]
    pallas_call x1 -> x2, Pallas kernels: 3.44 us -> 4.3 us  [the longest x1 3.25 us: on_device(): pl.pallas_call(partial_kernel, out_shape=[side_sums, side_sums, jax.Shape...]
    ppermute x5, waiting for transfers between devices: 0.31 us -> 0.67 us  [flipped(): lax.ppermute(value, 'dp', [(i, i ^ bit) for i in range(lax.axis_size('dp'...]
    ppermute x6, waiting for transfers between devices: 3.6 us -> 3.93 us  [stepped(): lax.ppermute(value, 'dp', [(i, ahead(size // 4, i // 4, step) * 4 + i % 4...]
  transfers between devices with their start and end apart: 12 -> 12, of which waited for: 5 -> 5; matrix products, arithmetic and copies ran while one was open for 0% -> 0% of each run, Pallas kernels for 9% -> 13%
where the time goes in v3:
time: 27.2 us; the launch traced here: 26.9 us
  starting transfers between devices  14.2 us (52%)
  Pallas kernels  7.38 us (27%)
  waiting for transfers between devices  4.61 us (17%)
  between operations  0.71 us (3%)
    ppermute x6, starting transfers between devices, stepped(): lax.ppermute(value, 'dp', [(i, ahead(size // 4, i // 4, step) * 4 + i % 4...  9.03 us
    ppermute x6, waiting for transfers between devices, stepped(): lax.ppermute(value, 'dp', [(i, ahead(size // 4, i // 4, step) * 4 + i % 4...  3.93 us
    ppermute x5, starting transfers between devices, flipped(): lax.ppermute(value, 'dp', [(i, i ^ bit) for i in range(lax.axis_size('dp'...  3.65 us
    pallas_call x1, Pallas kernels, on_device(): pl.pallas_call(partial_kernel, out_shape=[side_sums, side_sums, jax.Shape...  3.25 us
    pallas_call x1, Pallas kernels, on_device(): pl.pallas_call(input_grad_kernel, out_shape=(jax.ShapeDtypeStruct(inputs_...  2.09 us
    ppermute x1, starting transfers between devices, on_device(): other_dots = lax.ppermute(dots, 'group', [(0, 1), (1, 0)])  1.56 us
    pallas_call x1, Pallas kernels, on_device(): pl.pallas_call(near_partial_kernel, out_shape=[side_sums, side_sums], in_...  1.05 us
    ppermute x5, waiting for transfers between devices, flipped(): lax.ppermute(value, 'dp', [(i, i ^ bit) for i in range(lax.axis_size('dp'...  0.67 us
  transfers between devices with their start and end apart: 12, of which 5 were waited for; matrix products, arithmetic and copies ran while one was open for 0% of the time, Pallas kernels for 13%

profile of v3, /device:TPU:0, one launch (start us, length us, event | category | flops | bytes accessed | tf_op | source)
XLA Modules:
  0.0 26.9 jit_solution(9435651533003971494)
XLA Ops:
  0.6 3.3 %partials.1 = (f32[4,2,64,128]{3,2,1,0:T(8,128)S(1)}, f32[4,2,64,128]{3,2,1,0:T(8,128)S(1)}, bf16[64,64,128]{2,1,0:T(8,128)(2,1)S(1)}, bf16[24,128,128]{2,1,0:T(...) custom-call(s32[2,3584]{1,0:T(2,128)} %kept_hbm.1, ...), custom_call_target="tpu_custom_call" | custom-call | flops 4035500032 | bytes 12915000 | tf_op jit(solution)/shard_map/partials/pallas_call | solution.py:310
  3.9 0.5 %collective-permute-start.1 = (f32[4,2,64,128]{3,2,1,0:T(8,128)S(1)}, f32[4,2,64,128]{3,2,1,0:T(8,128)S(1)}, u32[]{:S(2)}, u32[]{:S(2)}) collective-permute-start(f32[4,2,64,128]{3,2,1,0:T(8,128)S(1)} %get-tuple-element.28), channel_id=1, source_target_pairs={{0,2},{2,0},{4,6},{6,4},{8,10},{10,8},{12,14},{14,12},{16,18},{18,... | collective-permute-start | bytes 786440 | tf_op jit(solution)/shard_map/ppermute | solution.py:262
  4.4 2.6 %collective-permute-start = (bf16[2,64,128]{2,1,0:T(8,128)(2,1)S(1)}, bf16[2,64,128]{2,1,0:T(8,128)(2,1)S(1)}, u32[]{:S(2)}, u32[]{:S(2)}) collective-permute-start(bf16[2,64,128]{2,1,0:T(8,128)(2,1)S(1)} %get-tuple-element.26.refs_0_), channel_id=1, source_target_pairs={{0,4},{2,6},{4,0},{6,2},{8,12},{10,14},{12,8},{14,10},{16,20},{18,... | collective-permute-start | bytes 98312 | tf_op jit(solution)/shard_map/ppermute | solution.py:262
  7.0 1.0 %near_partials.1 = (f32[4,2,64,128]{3,2,1,0:T(8,128)S(1)}, f32[4,2,64,128]{3,2,1,0:T(8,128)S(1)}) custom-call(s32[4,24]{1,0:T(4,128)S(1)} %get-tuple-element.24.tab_ref, s32[2,16]{1,0:T(2,128)S(1)} %get-tuple-element.29.span_ref, bf16[64,64,128]{2,1,0:T(8,128)(2,1)S(1)} %get-tuple-element.30.x_ref, bf16[24,128,128]{2,1,0:T(8,128)(2,1)S(1)} %get-tuple-element.25.cols_ref), custom_call_target="tpu_custom_call" | custom-call | flops 1152999936 | bytes 3690000 | tf_op jit(solution)/shard_map/near_partials/pallas_call | solution.py:351
  8.1 0.0 collective-permute-done.1.got_ref
  8.1 0.1 far_sums.1
  8.2 0.5 %collective-permute-start.5 = (s16[528,128]{1,0:T(8,128)(2,1)S(1)}, s16[528,128]{1,0:T(8,128)(2,1)S(1)}, u32[]{:S(2)}, u32[]{:S(2)}) collective-permute-start(s16[528,128]{1,0:T(8,128)(2,1)S(1)} %get-tuple-element.32.refs_2_), channel_id=1, source_target_pairs={{0,4},{2,6},{4,0},{6,2},{8,12},{10,14},{12,8},{14,10},{16,20},{18,... | collective-permute-start | bytes 405512 | tf_op jit(solution)/shard_map/ppermute | solution.py:262
  8.7 0.0 collective-permute-start.4
  8.7 0.3 %collective-permute-done.refs_1_ = bf16[2,64,128]{2,1,0:T(8,128)(2,1)S(1)} collective-permute-done((bf16[2,64,128]{2,1,0:T(8,128)(2,1)S(1)}, bf16[2,64,128]{2,1,0:T(8,128)(2,1)S(1)}, u32[]{:S(2)}, u32[]{:S(2)}) %collective-permute-start) | collective-permute-done | bytes 32800 | tf_op jit(solution)/shard_map/ppermute | solution.py:262
  9.0 3.0 %collective-permute-start.3 = (bf16[2,2,64,128]{3,2,1,0:T(8,128)(2,1)S(1)}, bf16[2,2,64,128]{3,2,1,0:T(8,128)(2,1)S(1)}, u32[]{:S(2)}, u32[]{:S(2)}) collective-permute-start(bf16[2,2,64,128]{3,2,1,0:T(8,128)(2,1)S(1)} %pair.1.refs_0_), channel_id=1, source_target_pairs={{0,16},{2,18},{4,20},{6,22},{8,24},{10,26},{12,28},{14,30},{16,0},... | collective-permute-start | bytes 196616 | tf_op jit(solution)/shard_map/ppermute | solution.py:275
  12.0 1.3 %collective-permute-start.6 = (bf16[2,2,64,128]{3,2,1,0:T(8,128)(2,1)S(1)}, bf16[2,2,64,128]{3,2,1,0:T(8,128)(2,1)S(1)}, u32[]{:S(2)}, u32[]{:S(2)}) collective-permute-start(bf16[2,2,64,128]{3,2,1,0:T(8,128)(2,1)S(1)} %pair.1.refs_0_), channel_id=1, source_target_pairs={{0,24},{2,26},{4,28},{6,30},{8,16},{10,18},{12,20},{14,22},{16,8},... | collective-permute-start | bytes 196616 | tf_op jit(solution)/shard_map/ppermute | solution.py:275
  13.3 0.2 collective-permute-start.2
  13.6 0.4 %collective-permute-done.5.far_ref = s16[528,128]{1,0:T(8,128)(2,1)S(1)} collective-permute-done((s16[528,128]{1,0:T(8,128)(2,1)S(1)}, s16[528,128]{1,0:T(8,128)(2,1)S(1)}, u32[]{:S(2)}, u32[]{:S(2)}) %collective-permute-start.5) | collective-permute-done | bytes 135200 | tf_op jit(solution)/shard_map/ppermute | solution.py:262
  13.9 0.0 collective-permute-done.4.got_ref
  13.9 0.1 near_sums.1
  14.1 3.7 %collective-permute-start.8 = (s16[144,128]{1,0:T(8,128)(2,1)S(1)}, s16[144,128]{1,0:T(8,128)(2,1)S(1)}, u32[]{:S(2)}, u32[]{:S(2)}) collective-permute-start(s16[144,128]{1,0:T(8,128)(2,1)S(1)} %get-tuple-element.39), channel_id=1, source_target_pairs={{0,24},{2,26},{4,28},{6,30},{8,16},{10,18},{12,20},{14,22},{16,8},... | collective-permute-start | bytes 110600 | tf_op jit(solution)/shard_map/ppermute | solution.py:275
  17.8 0.0 collective-permute-start.9
  17.8 0.0 collective-permute-done.3.refs_0_
  17.8 0.8 %collective-permute-start.10 = (s16[144,128]{1,0:T(8,128)(2,1)S(1)}, s16[144,128]{1,0:T(8,128)(2,1)S(1)}, u32[]{:S(2)}, u32[]{:S(2)}) collective-permute-start(s16[144,128]{1,0:T(8,128)(2,1)S(1)} %get-tuple-element.35.refs_1_), channel_id=1, source_target_pairs={{0,8},{2,10},{4,12},{6,14},{8,0},{10,2},{12,4},{14,6},{16,24},{18,... | collective-permute-start | bytes 110600 | tf_op jit(solution)/shard_map/ppermute | solution.py:275
  18.6 0.1 collective-permute-done.6.refs_0_
  18.6 0.0 collective-permute-done.2.refs_1_
  18.6 0.1 collective-permute-start.7
  18.7 1.5 %collective-permute-done.8.refs_0_ = s16[144,128]{1,0:T(8,128)(2,1)S(1)} collective-permute-done((s16[144,128]{1,0:T(8,128)(2,1)S(1)}, s16[144,128]{1,0:T(8,128)(2,1)S(1)}, u32[]{:S(2)}, u32[]{:S(2)}) %collective-permute-start.8) | collective-permute-done | bytes 36896 | tf_op jit(solution)/shard_map/ppermute | solution.py:275
  20.2 2.4 %collective-permute-done.9.refs_0_ = s16[144,128]{1,0:T(8,128)(2,1)S(1)} collective-permute-done((s16[144,128]{1,0:T(8,128)(2,1)S(1)}, s16[144,128]{1,0:T(8,128)(2,1)S(1)}, u32[]{:S(2)}, u32[]{:S(2)}) %collective-permute-start.9) | collective-permute-done | bytes 36896 | tf_op jit(solution)/shard_map/ppermute | solution.py:275
  22.6 0.0 collective-permute-done.10.refs_0_
  22.7 1.6 %collective-permute-start.11 = (f32[2,128]{1,0:T(2,128)S(1)}, f32[2,128]{1,0:T(2,128)S(1)}, u32[]{:S(2)}, u32[]{:S(2)}) collective-permute-start(f32[2,128]{1,0:T(2,128)S(1)} %get-tuple-element.44.dots_ref), channel_id=1, source_target_pairs={{0,1},{1,0},{2,3},{3,2},{4,5},{5,4},{6,7},{7,6},{8,9},{9,8},{10,11... | collective-permute-start | bytes 3080 | tf_op jit(solution)/shard_map/ppermute | solution.py:418
  24.2 0.0 collective-permute-done.7.other
  24.2 2.1 %input_grads.1 = (bf16[64,64,128]{2,1,0:T(8,128)(2,1)}, f32[1,2,64,128]{3,2,1,0:T(8,128)}) custom-call(s32[4,24]{1,0:T(4,128)S(1)} %get-tuple-element.24.tab_ref, bf16[24,128,128]{2,1,0:T(8,128)(2,1)S(1)} %get-tuple-element.25.cols_ref, bf16[4,2,2,64,128]{4,3,2,1,0:T(8,128)(2,1)S(1)} %mine.1, bf16[4,2,2,64,128]{4,3,2,1,0:T(8,128)(2,1)S(1)} %collective-permute-done.7.other, ...), custom_call_target="tpu_custom_call" | custom-call | flops 2305999872 | bytes 7380000 | tf_op jit(solution)/shard_map/input_grads/pallas_call | solution.py:419
  26.3 0.0 collective-permute-done.11.got_ref
  26.3 0.6 %finish.1 = f32[1,2]{1,0:T(1,128)} custom-call(f32[2,128]{1,0:T(2,128)S(1)} %get-tuple-element.44.dots_ref, f32[2,128]{1,0:T(2,128)S(1)} %collective-permute-done.11.got_ref, bf16[64,64,128]{2,1,0:T(8,128)(2,1)} %get-tuple-element.21.grads_ref), custom_call_target="tpu_custom_call" | custom-call | flops 576499968 | bytes 1845000 | tf_op jit(solution)/shard_map/finish/pallas_call | solution.py:432
  (7 shorter events, 0.1 us)
Async XLA Ops:
  3.9 4.2 %collective-permute-start.1 = (f32[4,2,64,128]{3,2,1,0:T(8,128)S(1)}, f32[4,2,64,128]{3,2,1,0:T(8,128)S(1)}, u32[]{:S(2)}, u32[]{:S(2)}) collective-permute-start(f32[4,2,64,128]{3,2,1,0:T(8,128)S(1)} %get-tuple-element.28), channel_id=1, source_target_pairs={{0,2},{2,0},{4,6},{6,4},{8,10},{10,8},{12,14},{14,12},{16,18},{18,... | collective-permute-start | bytes 786440 | tf_op jit(solution)/shard_map/ppermute | solution.py:262
  4.4 4.6 %collective-permute-start = (bf16[2,64,128]{2,1,0:T(8,128)(2,1)S(1)}, bf16[2,64,128]{2,1,0:T(8,128)(2,1)S(1)}, u32[]{:S(2)}, u32[]{:S(2)}) collective-permute-start(bf16[2,64,128]{2,1,0:T(8,128)(2,1)S(1)} %get-tuple-element.26.refs_0_), channel_id=1, source_target_pairs={{0,4},{2,6},{4,0},{6,2},{8,12},{10,14},{12,8},{14,10},{16,20},{18,... | collective-permute-start | bytes 98312 | tf_op jit(solution)/shard_map/ppermute | solution.py:262
  8.2 5.7 %collective-permute-start.5 = (s16[528,128]{1,0:T(8,128)(2,1)S(1)}, s16[528,128]{1,0:T(8,128)(2,1)S(1)}, u32[]{:S(2)}, u32[]{:S(2)}) collective-permute-start(s16[528,128]{1,0:T(8,128)(2,1)S(1)} %get-tuple-element.32.refs_2_), channel_id=1, source_target_pairs={{0,4},{2,6},{4,0},{6,2},{8,12},{10,14},{12,8},{14,10},{16,20},{18,... | collective-permute-start | bytes 405512 | tf_op jit(solution)/shard_map/ppermute | solution.py:262
  8.7 5.3 %collective-permute-start.4 = (f32[4,2,64,128]{3,2,1,0:T(8,128)S(1)}, f32[4,2,64,128]{3,2,1,0:T(8,128)S(1)}, u32[]{:S(2)}, u32[]{:S(2)}) collective-permute-start(f32[4,2,64,128]{3,2,1,0:T(8,128)S(1)} %get-tuple-element.34), channel_id=1, source_target_pairs={{0,2},{2,0},{4,6},{6,4},{8,10},{10,8},{12,14},{14,12},{16,18},{18,... | collective-permute-start | bytes 786440 | tf_op jit(solution)/shard_map/ppermute | solution.py:262
  9.0 8.8 %collective-permute-start.3 = (bf16[2,2,64,128]{3,2,1,0:T(8,128)(2,1)S(1)}, bf16[2,2,64,128]{3,2,1,0:T(8,128)(2,1)S(1)}, u32[]{:S(2)}, u32[]{:S(2)}) collective-permute-start(bf16[2,2,64,128]{3,2,1,0:T(8,128)(2,1)S(1)} %pair.1.refs_0_), channel_id=1, source_target_pairs={{0,16},{2,18},{4,20},{6,22},{8,24},{10,26},{12,28},{14,30},{16,0},... | collective-permute-start | bytes 196616 | tf_op jit(solution)/shard_map/ppermute | solution.py:275
  12.0 6.6 %collective-permute-start.6 = (bf16[2,2,64,128]{3,2,1,0:T(8,128)(2,1)S(1)}, bf16[2,2,64,128]{3,2,1,0:T(8,128)(2,1)S(1)}, u32[]{:S(2)}, u32[]{:S(2)}) collective-permute-start(bf16[2,2,64,128]{3,2,1,0:T(8,128)(2,1)S(1)} %pair.1.refs_0_), channel_id=1, source_target_pairs={{0,24},{2,26},{4,28},{6,30},{8,16},{10,18},{12,20},{14,22},{16,8},... | collective-permute-start | bytes 196616 | tf_op jit(solution)/shard_map/ppermute | solution.py:275
  13.3 5.3 %collective-permute-start.2 = (bf16[2,2,64,128]{3,2,1,0:T(8,128)(2,1)S(1)}, bf16[2,2,64,128]{3,2,1,0:T(8,128)(2,1)S(1)}, u32[]{:S(2)}, u32[]{:S(2)}) collective-permute-start(bf16[2,2,64,128]{3,2,1,0:T(8,128)(2,1)S(1)} %pair.1.refs_0_), channel_id=1, source_target_pairs={{0,8},{2,10},{4,12},{6,14},{8,0},{10,2},{12,4},{14,6},{16,24},{18,... | collective-permute-start | bytes 196616 | tf_op jit(solution)/shard_map/ppermute | solution.py:275
  14.1 6.1 %collective-permute-start.8 = (s16[144,128]{1,0:T(8,128)(2,1)S(1)}, s16[144,128]{1,0:T(8,128)(2,1)S(1)}, u32[]{:S(2)}, u32[]{:S(2)}) collective-permute-start(s16[144,128]{1,0:T(8,128)(2,1)S(1)} %get-tuple-element.39), channel_id=1, source_target_pairs={{0,24},{2,26},{4,28},{6,30},{8,16},{10,18},{12,20},{14,22},{16,8},... | collective-permute-start | bytes 110600 | tf_op jit(solution)/shard_map/ppermute | solution.py:275
  17.8 4.9 %collective-permute-start.9 = (s16[144,128]{1,0:T(8,128)(2,1)S(1)}, s16[144,128]{1,0:T(8,128)(2,1)S(1)}, u32[]{:S(2)}, u32[]{:S(2)}) collective-permute-start(s16[144,128]{1,0:T(8,128)(2,1)S(1)} %get-tuple-element.40), channel_id=1, source_target_pairs={{0,16},{2,18},{4,20},{6,22},{8,24},{10,26},{12,28},{14,30},{16,0},... | collective-permute-start | bytes 110600 | tf_op jit(solution)/shard_map/ppermute | solution.py:275
  17.8 4.9 %collective-permute-start.10 = (s16[144,128]{1,0:T(8,128)(2,1)S(1)}, s16[144,128]{1,0:T(8,128)(2,1)S(1)}, u32[]{:S(2)}, u32[]{:S(2)}) collective-permute-start(s16[144,128]{1,0:T(8,128)(2,1)S(1)} %get-tuple-element.35.refs_1_), channel_id=1, source_target_pairs={{0,8},{2,10},{4,12},{6,14},{8,0},{10,2},{12,4},{14,6},{16,24},{18,... | collective-permute-start | bytes 110600 | tf_op jit(solution)/shard_map/ppermute | solution.py:275
  18.6 5.6 %collective-permute-start.7 = (bf16[4,2,2,64,128]{4,3,2,1,0:T(8,128)(2,1)S(1)}, bf16[4,2,2,64,128]{4,3,2,1,0:T(8,128)(2,1)S(1)}, u32[]{:S(2)}, u32[]{:S(2)}) collective-permute-start(bf16[4,2,2,64,128]{4,3,2,1,0:T(8,128)(2,1)S(1)} %mine.1), channel_id=1, source_target_pairs={{0,2},{2,0},{4,6},{6,4},{8,10},{10,8},{12,14},{14,12},{16,18},{18,... | collective-permute-start | bytes 786440 | tf_op jit(solution)/shard_map/ppermute | solution.py:262
  22.7 3.7 %collective-permute-start.11 = (f32[2,128]{1,0:T(2,128)S(1)}, f32[2,128]{1,0:T(2,128)S(1)}, u32[]{:S(2)}, u32[]{:S(2)}) collective-permute-start(f32[2,128]{1,0:T(2,128)S(1)} %get-tuple-element.44.dots_ref), channel_id=1, source_target_pairs={{0,1},{1,0},{2,3},{3,2},{4,5},{5,4},{6,7},{7,6},{8,9},{9,8},{10,11... | collective-permute-start | bytes 3080 | tf_op jit(solution)/shard_map/ppermute | solution.py:418

commit v4 on v2

--- a/solution.py
+++ b/solution.py
@@ -79,12 +79,16 @@
             away = (owner >> 2) - (me >> 2)
             step_to = jnp.where(away < 0, away + outer, away)
             step_from = jnp.where(away > 0, outer - away, -away)
+        split = step_to >= 2
+        summing = jnp.where(split, 1 - (step_to & 1), owner & 1)
+        place = jnp.where(split, (step_to & ~1) + (owner & 1), step_to)
+        part = (kind & 2) | (summing ^ (me & 1))
         for c in range(cap):
 
             @pl.when(c < counts[owner])
             def _():
                 p = offset + c
-                slot_ref[p] = (kind * outer + step_to) * cap + c
+                slot_ref[p] = (part * outer + place) * cap + c
                 tab_ref[1, p] = kind
                 tab_ref[2, p] = step_from
                 tab_ref[3, p] = c
@@ -156,28 +160,33 @@
     write_message(totals, out_ref)
 
 
-def near_sum_kernel(keep_ref, got_ref, far_ref, *out_refs):
+def near_sum_kernel(keep_ref, got_ref, far_ref, own_ref, *out_refs):
     outer, cap, slab_rows, side = keep_ref.shape
     far = read_message(outer * cap, slab_rows, far_ref)
-    for step in range(outer):
-        totals = [
-            keep_ref[step, c] + got_ref[step, c] + far[step * cap + c] for c in range(cap)
-        ]
-        if step == 0:
-            for c in range(cap):
-                out_refs[0][c] = totals[c]
-        else:
-            write_message(totals, out_refs[step])
-
-
-def add_kernel(own_ref, *refs):
-    *got_refs, out_ref = refs
+
+    def totals(places):
+        return [keep_ref[k, c] + got_ref[k, c] + far[k * cap + c] for k in places for c in range(cap)]
+
+    for c, total in enumerate(totals([0])):
+        own_ref[c] = total
+    write_message(totals([1]), out_refs[0])
+    for i, out_ref in enumerate(out_refs[1:]):
+        write_message(totals([2 * i + 2, 2 * i + 3]), out_ref)
+
+
+def split_kernel(own_ref, *refs):
+    *got_refs, mine_ref, other_ref = refs
     cap, slab_rows, side = own_ref.shape
-    totals = [own_ref[c] for c in range(cap)]
+    first_core = (lax.axis_index("dp") & 1) == 0
+    sums = [[own_ref[c] for c in range(cap)], [jnp.zeros((slab_rows, side), jnp.float32)] * cap]
     for got_ref in got_refs:
-        totals = [a + b for a, b in zip(totals, read_message(cap, slab_rows, got_ref))]
+        blocks = read_message(2 * cap, slab_rows, got_ref)
+        for c in range(cap):
+            sums[0][c] = sums[0][c] + jnp.where(first_core, blocks[c], blocks[cap + c])
+            sums[1][c] = sums[1][c] + jnp.where(first_core, blocks[cap + c], blocks[c])
     for c in range(cap):
-        out_ref[c] = totals[c]
+        mine_ref[c] = sums[0][c]
+        other_ref[c] = sums[1][c]
 
 
 def stack_kernel(*refs):
@@ -210,10 +219,10 @@
     out_ref[...] = acc_ref[...].astype(out_ref.dtype)
 
 
-def owner_sum_kernel(norm, scales_ref, stored_ref, own_ref, *refs):
+def owner_sum_kernel(norm, scales_ref, stored_ref, own_ref, other_ref, *refs):
     got_refs, (block_ref, dots_ref) = refs[:-2], refs[-2:]
     cap, slab_rows, side = stored_ref.shape[1:]
-    totals = [own_ref[c] for c in range(cap)]
+    totals = [own_ref[c] + other_ref[c] for c in range(cap)]
     for got_ref in got_refs:
         totals = [a + b for a, b in zip(totals, read_message(cap, slab_rows, got_ref))]
     for c in range(cap):
@@ -255,10 +264,13 @@
     return start ^ step if is_paired(places) else (start + step) % places
 
 
-def stepped(value, step):
+def stepped(value, step, second_core_step=None):
     size = lax.axis_size("dp")
+    steps = (step, step if second_core_step is None else second_core_step)
     return lax.ppermute(
-        value, "dp", [(i, ahead(size // 4, i // 4, step) * 4 + i % 4) for i in range(size)]
+        value,
+        "dp",
+        [(i, ahead(size // 4, i // 4, steps[i % 2]) * 4 + i % 4) for i in range(size)],
     )
 
 
@@ -351,28 +363,33 @@
 
     pair = stacked("pair", 5.0, far_sums, scaled, far_scaled)
     pairs = [pair] + [stepped(pair, step) for step in range(1, outer)]
+    message = jax.ShapeDtypeStruct(message_shape, jnp.int16)
+    chip_message = jax.ShapeDtypeStruct((message_rows(2 * cap, slab_rows), side), jnp.int16)
+    chip_messages = outer // 2 - 1
     own_sum, *near_sums = pl.pallas_call(
         near_sum_kernel,
-        out_shape=[jax.ShapeDtypeStruct(block_shape, jnp.float32)]
-        + [jax.ShapeDtypeStruct(message_shape, jnp.int16)] * (outer - 1),
+        out_shape=[jax.ShapeDtypeStruct(block_shape, jnp.float32), message]
+        + [chip_message] * chip_messages,
         in_specs=[VMEM_SPEC] * 3,
-        out_specs=[VMEM_SPEC] * outer,
+        out_specs=[VMEM_SPEC] * (2 + chip_messages),
         compiler_params=params,
         cost_estimate=cost(0.3),
         name="near_sums",
     )(near_keep, near_got, flipped(far_sums, 2))
-    received = [stepped(value, step + 1) for step, value in enumerate(near_sums)]
-
-    for number, group in enumerate((received[2:], received[1:2])):
-        own_sum = pl.pallas_call(
-            add_kernel,
-            out_shape=jax.ShapeDtypeStruct(block_shape, jnp.float32),
-            in_specs=[VMEM_SPEC] * (1 + len(group)),
-            out_specs=VMEM_SPEC,
-            compiler_params=params,
-            cost_estimate=cost(6.0),
-            name="add_%d" % number,
-        )(own_sum, *group)
+    neighbour = stepped(near_sums[0], 1)
+    received = [
+        stepped(value, 2 * i + 3, 2 * i + 2) for i, value in enumerate(near_sums[1:])
+    ]
+    own_sum, other_sum = pl.pallas_call(
+        split_kernel,
+        out_shape=[jax.ShapeDtypeStruct(block_shape, jnp.float32)] * 2,
+        in_specs=[VMEM_SPEC] * (1 + chip_messages),
+        out_specs=[VMEM_SPEC] * 2,
+        compiler_params=params,
+        cost_estimate=cost(6.0),
+        name="split_sums",
+    )(own_sum, *received)
+    other_sum = flipped(other_sum, 1)
     second = stacked("mine_2", 3.0, near_sums[0], *pairs[2:3])
     others = stacked("mine_3", 3.0, second, *pairs[3:])
     mine = stacked("mine", 0.1, others, pair, pairs[1], second, others)
@@ -384,12 +401,12 @@
             jax.ShapeDtypeStruct((1,) + block_shape, jnp.float32),
             jax.ShapeDtypeStruct((cap, side), jnp.float32),
         ),
-        in_specs=[VMEM_SPEC] * 4,
+        in_specs=[VMEM_SPEC] * 5,
         out_specs=(VMEM_SPEC, VMEM_SPEC),
         compiler_params=params,
         cost_estimate=cost(6.0),
         name="owner_sums",
-    )(scale_rows, stored, own_sum, received[0])
+    )(scale_rows, stored, own_sum, other_sum, neighbour)
     other_dots = lax.ppermute(dots, "group", [(0, 1), (1, 0)])
     grad_inputs_t, block_grads = pl.pallas_call(
         input_grad_kernel,

time: 26.7 us -> 26.9 us (level)
  waiting for transfers between devices: 3.92 us -> 4.64 us
  starting transfers between devices: 15.3 us -> 14.8 us
    ppermute x6 -> x5, starting transfers between devices: 9.03 us -> 8.02 us  [stepped(): lax.ppermute(value, 'dp', [(i, ahead(size // 4, i // 4, steps[i % 2]) * 4...]
    ppermute x5 -> x6, waiting for transfers between devices: 0.31 us -> 0.93 us  [flipped(): lax.ppermute(value, 'dp', [(i, i ^ bit) for i in range(lax.axis_size('dp'...]
    ppermute x5 -> x6, starting transfers between devices: 4.7 us -> 5.25 us  [flipped(): lax.ppermute(value, 'dp', [(i, i ^ bit) for i in range(lax.axis_size('dp'...]
    ppermute x6 -> x5, waiting for transfers between devices: 3.6 us -> 3.7 us  [stepped(): lax.ppermute(value, 'dp', [(i, ahead(size // 4, i // 4, steps[i % 2]) * 4...]
  transfers between devices with their start and end apart: 12 -> 12, of which waited for: 5 -> 3; matrix products, arithmetic and copies ran while one was open for 0% -> 0% of each run, Pallas kernels for 9% -> 9%
where the time goes in v4:
time: 26.9 us; the launch traced here: 26.7 us
  starting transfers between devices  14.8 us (55%)
  Pallas kernels  6.54 us (24%)
  waiting for transfers between devices  4.64 us (17%)
  between operations  0.72 us (3%)
    ppermute x5, starting transfers between devices, stepped(): lax.ppermute(value, 'dp', [(i, ahead(size // 4, i // 4, steps[i % 2]) * 4...  8.02 us
    ppermute x6, starting transfers between devices, flipped(): lax.ppermute(value, 'dp', [(i, i ^ bit) for i in range(lax.axis_size('dp'...  5.25 us
    ppermute x5, waiting for transfers between devices, stepped(): lax.ppermute(value, 'dp', [(i, ahead(size // 4, i // 4, steps[i % 2]) * 4...  3.7 us
    pallas_call x1, Pallas kernels, on_device(): pl.pallas_call(partial_kernel, out_shape=[jax.ShapeDtypeStruct(side_shape...  3.44 us
    pallas_call x1, Pallas kernels, on_device(): pl.pallas_call(input_grad_kernel, out_shape=(jax.ShapeDtypeStruct(inputs_...  2.1 us
    ppermute x1, starting transfers between devices, on_device(): other_dots = lax.ppermute(dots, 'group', [(0, 1), (1, 0)])  1.57 us
    ppermute x6, waiting for transfers between devices, flipped(): lax.ppermute(value, 'dp', [(i, i ^ bit) for i in range(lax.axis_size('dp'...  0.93 us
    pallas_call x1, Pallas kernels, on_device(): pl.pallas_call(finish_kernel, out_shape=jax.ShapeDtypeStruct((1, cap), jn...  0.6 us
  transfers between devices with their start and end apart: 12, of which 3 were waited for; matrix products, arithmetic and copies ran while one was open for 0% of the time, Pallas kernels for 9%

profile of v4, /device:TPU:0, one launch (start us, length us, event | category | flops | bytes accessed | tf_op | source)
XLA Modules:
  0.0 26.7 jit_solution(498345772912857258)
XLA Ops:
  0.6 3.4 %partials.1 = (f32[4,2,64,128]{3,2,1,0:T(8,128)S(1)}, f32[4,2,64,128]{3,2,1,0:T(8,128)S(1)}, f32[4,2,64,128]{3,2,1,0:T(8,128)S(1)}, f32[4,2,64,128]{3,2,1,0:T(8,...) custom-call(s32[2,3584]{1,0:T(2,128)} %kept_hbm.1, ...), custom_call_target="tpu_custom_call" | custom-call | flops 4035500032 | bytes 12915000 | tf_op jit(solution)/shard_map/partials/pallas_call | solution.py:306
  4.1 0.5 %collective-permute-start.1 = (f32[4,2,64,128]{3,2,1,0:T(8,128)S(1)}, f32[4,2,64,128]{3,2,1,0:T(8,128)S(1)}, u32[]{:S(2)}, u32[]{:S(2)}) collective-permute-start(f32[4,2,64,128]{3,2,1,0:T(8,128)S(1)} %get-tuple-element.27), channel_id=1, source_target_pairs={{0,2},{2,0},{4,6},{6,4},{8,10},{10,8},{12,14},{14,12},{16,18},{18,... | collective-permute-start | bytes 786440 | tf_op jit(solution)/shard_map/ppermute | solution.py:256
  4.6 2.6 %collective-permute-start = (bf16[2,64,128]{2,1,0:T(8,128)(2,1)S(1)}, bf16[2,64,128]{2,1,0:T(8,128)(2,1)S(1)}, u32[]{:S(2)}, u32[]{:S(2)}) collective-permute-start(bf16[2,64,128]{2,1,0:T(8,128)(2,1)S(1)} %get-tuple-element.25.refs_0_), channel_id=1, source_target_pairs={{0,4},{2,6},{4,0},{6,2},{8,12},{10,14},{12,8},{14,10},{16,20},{18,... | collective-permute-start | bytes 98312 | tf_op jit(solution)/shard_map/ppermute | solution.py:256
  7.2 0.0 collective-permute-done.1.got_ref
  7.2 0.2 far_sums.1
  7.4 1.5 %collective-permute-start.5 = (s16[528,128]{1,0:T(8,128)(2,1)S(1)}, s16[528,128]{1,0:T(8,128)(2,1)S(1)}, u32[]{:S(2)}, u32[]{:S(2)}) collective-permute-start(s16[528,128]{1,0:T(8,128)(2,1)S(1)} %get-tuple-element.29.refs_2_), channel_id=1, source_target_pairs={{0,4},{2,6},{4,0},{6,2},{8,12},{10,14},{12,8},{14,10},{16,20},{18,... | collective-permute-start | bytes 405512 | tf_op jit(solution)/shard_map/ppermute | solution.py:256
  8.9 0.0 collective-permute-start.4
  8.9 0.3 %collective-permute-done.refs_1_ = bf16[2,64,128]{2,1,0:T(8,128)(2,1)S(1)} collective-permute-done((bf16[2,64,128]{2,1,0:T(8,128)(2,1)S(1)}, bf16[2,64,128]{2,1,0:T(8,128)(2,1)S(1)}, u32[]{:S(2)}, u32[]{:S(2)}) %collective-permute-start) | collective-permute-done | bytes 32800 | tf_op jit(solution)/shard_map/ppermute | solution.py:256
  9.2 3.0 %collective-permute-start.3 = (bf16[2,2,64,128]{3,2,1,0:T(8,128)(2,1)S(1)}, bf16[2,2,64,128]{3,2,1,0:T(8,128)(2,1)S(1)}, u32[]{:S(2)}, u32[]{:S(2)}) collective-permute-start(bf16[2,2,64,128]{3,2,1,0:T(8,128)(2,1)S(1)} %pair.1.refs_0_), channel_id=1, source_target_pairs={{0,16},{2,18},{4,20},{6,22},{8,24},{10,26},{12,28},{14,30},{16,0},... | collective-permute-start | bytes 196616 | tf_op jit(solution)/shard_map/ppermute | solution.py:270
  12.2 1.3 %collective-permute-start.6 = (bf16[2,2,64,128]{3,2,1,0:T(8,128)(2,1)S(1)}, bf16[2,2,64,128]{3,2,1,0:T(8,128)(2,1)S(1)}, u32[]{:S(2)}, u32[]{:S(2)}) collective-permute-start(bf16[2,2,64,128]{3,2,1,0:T(8,128)(2,1)S(1)} %pair.1.refs_0_), channel_id=1, source_target_pairs={{0,24},{2,26},{4,28},{6,30},{8,16},{10,18},{12,20},{14,22},{16,8},... | collective-permute-start | bytes 196616 | tf_op jit(solution)/shard_map/ppermute | solution.py:270
  13.5 0.2 collective-permute-start.2
  13.8 0.0 collective-permute-done.5.far_ref
  13.8 0.0 collective-permute-done.4.got_ref
  13.8 0.1 near_sums.1
  13.9 3.0 %collective-permute-start.8 = (s16[272,128]{1,0:T(8,128)(2,1)S(1)}, s16[272,128]{1,0:T(8,128)(2,1)S(1)}, u32[]{:S(2)}, u32[]{:S(2)}) collective-permute-start(s16[272,128]{1,0:T(8,128)(2,1)S(1)} %get-tuple-element.36), channel_id=1, source_target_pairs={{0,24},{2,18},{4,28},{6,22},{8,16},{10,26},{12,20},{14,30},{16,8},... | collective-permute-start | bytes 208904 | tf_op jit(solution)/shard_map/ppermute | solution.py:270
  16.9 0.4 %collective-permute-start.10 = (s16[144,128]{1,0:T(8,128)(2,1)S(1)}, s16[144,128]{1,0:T(8,128)(2,1)S(1)}, u32[]{:S(2)}, u32[]{:S(2)}) collective-permute-start(s16[144,128]{1,0:T(8,128)(2,1)S(1)} %get-tuple-element.32.refs_1_), channel_id=1, source_target_pairs={{0,8},{2,10},{4,12},{6,14},{8,0},{10,2},{12,4},{14,6},{16,24},{18,... | collective-permute-start | bytes 110600 | tf_op jit(solution)/shard_map/ppermute | solution.py:270
  17.4 0.0 collective-permute-done.3.refs_0_
  17.4 3.7 %collective-permute-done.8.refs_0_ = s16[272,128]{1,0:T(8,128)(2,1)S(1)} collective-permute-done((s16[272,128]{1,0:T(8,128)(2,1)S(1)}, s16[272,128]{1,0:T(8,128)(2,1)S(1)}, u32[]{:S(2)}, u32[]{:S(2)}) %collective-permute-start.8) | collective-permute-done | bytes 69664 | tf_op jit(solution)/shard_map/ppermute | solution.py:270
  21.1 0.1 collective-permute-start.9
  21.2 0.0 collective-permute-done.6.refs_0_
  21.2 0.0 collective-permute-done.2.refs_1_
  21.2 0.5 %collective-permute-start.7 = (bf16[4,2,2,64,128]{4,3,2,1,0:T(8,128)(2,1)S(1)}, bf16[4,2,2,64,128]{4,3,2,1,0:T(8,128)(2,1)S(1)}, u32[]{:S(2)}, u32[]{:S(2)}) collective-permute-start(bf16[4,2,2,64,128]{4,3,2,1,0:T(8,128)(2,1)S(1)} %mine.1), channel_id=1, source_target_pairs={{0,2},{2,0},{4,6},{6,4},{8,10},{10,8},{12,14},{14,12},{16,18},{18,... | collective-permute-start | bytes 786440 | tf_op jit(solution)/shard_map/ppermute | solution.py:256
  21.8 0.0 collective-permute-done.10.refs_0_
  21.8 0.6 %collective-permute-done.9.other_ref = f32[2,64,128]{2,1,0:T(8,128)S(1)} collective-permute-done((f32[2,64,128]{2,1,0:T(8,128)S(1)}, f32[2,64,128]{2,1,0:T(8,128)S(1)}, u32[]{:S(2)}, u32[]{:S(2)}) %collective-permute-start.9) | collective-permute-done | bytes 65568 | tf_op jit(solution)/shard_map/ppermute | solution.py:256
  22.4 1.6 %collective-permute-start.11 = (f32[2,128]{1,0:T(2,128)S(1)}, f32[2,128]{1,0:T(2,128)S(1)}, u32[]{:S(2)}, u32[]{:S(2)}) collective-permute-start(f32[2,128]{1,0:T(2,128)S(1)} %get-tuple-element.42.dots_ref), channel_id=1, source_target_pairs={{0,1},{1,0},{2,3},{3,2},{4,5},{5,4},{6,7},{7,6},{8,9},{9,8},{10,11... | collective-permute-start | bytes 3080 | tf_op jit(solution)/shard_map/ppermute | solution.py:410
  24.0 0.0 collective-permute-done.7.other
  24.0 2.1 %input_grads.1 = (bf16[64,64,128]{2,1,0:T(8,128)(2,1)}, f32[1,2,64,128]{3,2,1,0:T(8,128)}) custom-call(s32[4,24]{1,0:T(4,128)S(1)} %get-tuple-element.23.tab_ref, bf16[24,128,128]{2,1,0:T(8,128)(2,1)S(1)} %get-tuple-element.24.cols_ref, bf16[4,2,2,64,128]{4,3,2,1,0:T(8,128)(2,1)S(1)} %mine.1, bf16[4,2,2,64,128]{4,3,2,1,0:T(8,128)(2,1)S(1)} %collective-permute-done.7.other, ...), custom_call_target="tpu_custom_call" | custom-call | flops 2305999872 | bytes 7380000 | tf_op jit(solution)/shard_map/input_grads/pallas_call | solution.py:411
  26.1 0.0 collective-permute-done.11.got_ref
  26.1 0.6 %finish.1 = f32[1,2]{1,0:T(1,128)} custom-call(f32[2,128]{1,0:T(2,128)S(1)} %get-tuple-element.42.dots_ref, f32[2,128]{1,0:T(2,128)S(1)} %collective-permute-done.11.got_ref, bf16[64,64,128]{2,1,0:T(8,128)(2,1)} %get-tuple-element.20.grads_ref), custom_call_target="tpu_custom_call" | custom-call | flops 576499968 | bytes 1845000 | tf_op jit(solution)/shard_map/finish/pallas_call | solution.py:424
  (6 shorter events, 0.1 us)
Async XLA Ops:
  4.1 3.1 %collective-permute-start.1 = (f32[4,2,64,128]{3,2,1,0:T(8,128)S(1)}, f32[4,2,64,128]{3,2,1,0:T(8,128)S(1)}, u32[]{:S(2)}, u32[]{:S(2)}) collective-permute-start(f32[4,2,64,128]{3,2,1,0:T(8,128)S(1)} %get-tuple-element.27), channel_id=1, source_target_pairs={{0,2},{2,0},{4,6},{6,4},{8,10},{10,8},{12,14},{14,12},{16,18},{18,... | collective-permute-start | bytes 786440 | tf_op jit(solution)/shard_map/ppermute | solution.py:256
  4.6 4.6 %collective-permute-start = (bf16[2,64,128]{2,1,0:T(8,128)(2,1)S(1)}, bf16[2,64,128]{2,1,0:T(8,128)(2,1)S(1)}, u32[]{:S(2)}, u32[]{:S(2)}) collective-permute-start(bf16[2,64,128]{2,1,0:T(8,128)(2,1)S(1)} %get-tuple-element.25.refs_0_), channel_id=1, source_target_pairs={{0,4},{2,6},{4,0},{6,2},{8,12},{10,14},{12,8},{14,10},{16,20},{18,... | collective-permute-start | bytes 98312 | tf_op jit(solution)/shard_map/ppermute | solution.py:256
  7.4 6.4 %collective-permute-start.5 = (s16[528,128]{1,0:T(8,128)(2,1)S(1)}, s16[528,128]{1,0:T(8,128)(2,1)S(1)}, u32[]{:S(2)}, u32[]{:S(2)}) collective-permute-start(s16[528,128]{1,0:T(8,128)(2,1)S(1)} %get-tuple-element.29.refs_2_), channel_id=1, source_target_pairs={{0,4},{2,6},{4,0},{6,2},{8,12},{10,14},{12,8},{14,10},{16,20},{18,... | collective-permute-start | bytes 405512 | tf_op jit(solution)/shard_map/ppermute | solution.py:256
  8.9 4.9 %collective-permute-start.4 = (f32[4,2,64,128]{3,2,1,0:T(8,128)S(1)}, f32[4,2,64,128]{3,2,1,0:T(8,128)S(1)}, u32[]{:S(2)}, u32[]{:S(2)}) collective-permute-start(f32[4,2,64,128]{3,2,1,0:T(8,128)S(1)} %get-tuple-element.31), channel_id=1, source_target_pairs={{0,2},{2,0},{4,6},{6,4},{8,10},{10,8},{12,14},{14,12},{16,18},{18,... | collective-permute-start | bytes 786440 | tf_op jit(solution)/shard_map/ppermute | solution.py:256
  9.2 8.2 %collective-permute-start.3 = (bf16[2,2,64,128]{3,2,1,0:T(8,128)(2,1)S(1)}, bf16[2,2,64,128]{3,2,1,0:T(8,128)(2,1)S(1)}, u32[]{:S(2)}, u32[]{:S(2)}) collective-permute-start(bf16[2,2,64,128]{3,2,1,0:T(8,128)(2,1)S(1)} %pair.1.refs_0_), channel_id=1, source_target_pairs={{0,16},{2,18},{4,20},{6,22},{8,24},{10,26},{12,28},{14,30},{16,0},... | collective-permute-start | bytes 196616 | tf_op jit(solution)/shard_map/ppermute | solution.py:270
  12.2 9.0 %collective-permute-start.6 = (bf16[2,2,64,128]{3,2,1,0:T(8,128)(2,1)S(1)}, bf16[2,2,64,128]{3,2,1,0:T(8,128)(2,1)S(1)}, u32[]{:S(2)}, u32[]{:S(2)}) collective-permute-start(bf16[2,2,64,128]{3,2,1,0:T(8,128)(2,1)S(1)} %pair.1.refs_0_), channel_id=1, source_target_pairs={{0,24},{2,26},{4,28},{6,30},{8,16},{10,18},{12,20},{14,22},{16,8},... | collective-permute-start | bytes 196616 | tf_op jit(solution)/shard_map/ppermute | solution.py:270
  13.5 7.7 %collective-permute-start.2 = (bf16[2,2,64,128]{3,2,1,0:T(8,128)(2,1)S(1)}, bf16[2,2,64,128]{3,2,1,0:T(8,128)(2,1)S(1)}, u32[]{:S(2)}, u32[]{:S(2)}) collective-permute-start(bf16[2,2,64,128]{3,2,1,0:T(8,128)(2,1)S(1)} %pair.1.refs_0_), channel_id=1, source_target_pairs={{0,8},{2,10},{4,12},{6,14},{8,0},{10,2},{12,4},{14,6},{16,24},{18,... | collective-permute-start | bytes 196616 | tf_op jit(solution)/shard_map/ppermute | solution.py:270
  13.9 7.1 %collective-permute-start.8 = (s16[272,128]{1,0:T(8,128)(2,1)S(1)}, s16[272,128]{1,0:T(8,128)(2,1)S(1)}, u32[]{:S(2)}, u32[]{:S(2)}) collective-permute-start(s16[272,128]{1,0:T(8,128)(2,1)S(1)} %get-tuple-element.36), channel_id=1, source_target_pairs={{0,24},{2,18},{4,28},{6,22},{8,16},{10,26},{12,20},{14,30},{16,8},... | collective-permute-start | bytes 208904 | tf_op jit(solution)/shard_map/ppermute | solution.py:270
  16.9 4.9 %collective-permute-start.10 = (s16[144,128]{1,0:T(8,128)(2,1)S(1)}, s16[144,128]{1,0:T(8,128)(2,1)S(1)}, u32[]{:S(2)}, u32[]{:S(2)}) collective-permute-start(s16[144,128]{1,0:T(8,128)(2,1)S(1)} %get-tuple-element.32.refs_1_), channel_id=1, source_target_pairs={{0,8},{2,10},{4,12},{6,14},{8,0},{10,2},{12,4},{14,6},{16,24},{18,... | collective-permute-start | bytes 110600 | tf_op jit(solution)/shard_map/ppermute | solution.py:270
  21.1 1.3 %collective-permute-start.9 = (f32[2,64,128]{2,1,0:T(8,128)S(1)}, f32[2,64,128]{2,1,0:T(8,128)S(1)}, u32[]{:S(2)}, u32[]{:S(2)}) collective-permute-start(f32[2,64,128]{2,1,0:T(8,128)S(1)} %get-tuple-element.38), channel_id=1, source_target_pairs={{0,2},{2,0},{4,6},{6,4},{8,10},{10,8},{12,14},{14,12},{16,18},{18,... | collective-permute-start | bytes 196616 | tf_op jit(solution)/shard_map/ppermute | solution.py:256
  21.2 2.8 %collective-permute-start.7 = (bf16[4,2,2,64,128]{4,3,2,1,0:T(8,128)(2,1)S(1)}, bf16[4,2,2,64,128]{4,3,2,1,0:T(8,128)(2,1)S(1)}, u32[]{:S(2)}, u32[]{:S(2)}) collective-permute-start(bf16[4,2,2,64,128]{4,3,2,1,0:T(8,128)(2,1)S(1)} %mine.1), channel_id=1, source_target_pairs={{0,2},{2,0},{4,6},{6,4},{8,10},{10,8},{12,14},{14,12},{16,18},{18,... | collective-permute-start | bytes 786440 | tf_op jit(solution)/shard_map/ppermute | solution.py:256
  22.4 3.7 %collective-permute-start.11 = (f32[2,128]{1,0:T(2,128)S(1)}, f32[2,128]{1,0:T(2,128)S(1)}, u32[]{:S(2)}, u32[]{:S(2)}) collective-permute-start(f32[2,128]{1,0:T(2,128)S(1)} %get-tuple-element.42.dots_ref), channel_id=1, source_target_pairs={{0,1},{1,0},{2,3},{3,2},{4,5},{5,4},{6,7},{7,6},{8,9},{9,8},{10,11... | collective-permute-start | bytes 3080 | tf_op jit(solution)/shard_map/ppermute | solution.py:410

commit v5 on v4

--- a/solution.py
+++ b/solution.py
@@ -174,11 +174,12 @@
         write_message(totals([2 * i + 2, 2 * i + 3]), out_ref)
 
 
-def split_kernel(own_ref, *refs):
+def split_kernel(own_ref, neighbour_ref, *refs):
     *got_refs, mine_ref, other_ref = refs
     cap, slab_rows, side = own_ref.shape
     first_core = (lax.axis_index("dp") & 1) == 0
-    sums = [[own_ref[c] for c in range(cap)], [jnp.zeros((slab_rows, side), jnp.float32)] * cap]
+    neighbour = read_message(cap, slab_rows, neighbour_ref)
+    sums = [[own_ref[c] + neighbour[c] for c in range(cap)], [jnp.zeros((slab_rows, side), jnp.float32)] * cap]
     for got_ref in got_refs:
         blocks = read_message(2 * cap, slab_rows, got_ref)
         for c in range(cap):
@@ -189,8 +190,8 @@
         other_ref[c] = sums[1][c]
 
 
-def stack_kernel(*refs):
-    *in_refs, _, out_ref = refs
+def stack_kernel(count, *refs):
+    in_refs, out_ref = refs[:count], refs[-1]
     at = 0
     for in_ref in in_refs:
         if in_ref.ndim < out_ref.ndim:
@@ -219,12 +220,9 @@
     out_ref[...] = acc_ref[...].astype(out_ref.dtype)
 
 
-def owner_sum_kernel(norm, scales_ref, stored_ref, own_ref, other_ref, *refs):
-    got_refs, (block_ref, dots_ref) = refs[:-2], refs[-2:]
+def owner_sum_kernel(norm, scales_ref, stored_ref, own_ref, other_ref, block_ref, dots_ref):
     cap, slab_rows, side = stored_ref.shape[1:]
     totals = [own_ref[c] + other_ref[c] for c in range(cap)]
-    for got_ref in got_refs:
-        totals = [a + b for a, b in zip(totals, read_message(cap, slab_rows, got_ref))]
     for c in range(cap):
         gradient = totals[c] * norm
         block_ref[0, c] = scales_ref[c, 0:1] * gradient
@@ -279,14 +277,14 @@
     count = sum(1 if value.ndim == single else value.shape[0] for value in values)
     shape = (count,) + values[0].shape
     return pl.pallas_call(
-        stack_kernel,
+        functools.partial(stack_kernel, len(values)),
         out_shape=jax.ShapeDtypeStruct(shape, values[0].dtype),
-        in_specs=[VMEM_SPEC] * len(values) + [ANY_SPEC],
+        in_specs=[VMEM_SPEC] * len(values) + [ANY_SPEC] * len(after),
         out_specs=VMEM_SPEC,
         compiler_params=pltpu.CompilerParams(vmem_limit_bytes=VMEM_LIMIT),
         cost_estimate=cost(estimate),
         name=name,
-    )(*values, after)
+    )(*values, *after)
 
 
 def on_device(
@@ -361,8 +359,12 @@
     )(far_keep, far_got, near_send)
     near_got = flipped(near_send, 1)
 
-    pair = stacked("pair", 5.0, far_sums, scaled, far_scaled)
-    pairs = [pair] + [stepped(pair, step) for step in range(1, outer)]
+    pair = stacked("pair", 5.0, (far_sums,), scaled, far_scaled)
+    forwarded = [s for s in range(1, outer) if is_paired(outer) and s & (s - 1)]
+    pairs = {0: pair}
+    for step in range(1, outer):
+        if step not in forwarded:
+            pairs[step] = stepped(pair, step)
     message = jax.ShapeDtypeStruct(message_shape, jnp.int16)
     chip_message = jax.ShapeDtypeStruct((message_rows(2 * cap, slab_rows), side), jnp.int16)
     chip_messages = outer // 2 - 1
@@ -383,16 +385,19 @@
     own_sum, other_sum = pl.pallas_call(
         split_kernel,
         out_shape=[jax.ShapeDtypeStruct(block_shape, jnp.float32)] * 2,
-        in_specs=[VMEM_SPEC] * (1 + chip_messages),
+        in_specs=[VMEM_SPEC] * (2 + chip_messages),
         out_specs=[VMEM_SPEC] * 2,
         compiler_params=params,
         cost_estimate=cost(6.0),
         name="split_sums",
-    )(own_sum, *received)
+    )(own_sum, neighbour, *received)
     other_sum = flipped(other_sum, 1)
-    second = stacked("mine_2", 3.0, near_sums[0], *pairs[2:3])
-    others = stacked("mine_3", 3.0, second, *pairs[3:])
-    mine = stacked("mine", 0.1, others, pair, pairs[1], second, others)
+    for step in forwarded:
+        near_bit = step & -step
+        after = (near_sums[0], pairs[near_bit])
+        held = stacked("hold_%d" % step, 0.1, after, pairs[step ^ near_bit])[0]
+        pairs[step] = stepped(held, near_bit)
+    mine = stacked("mine", 0.1, near_sums[:1], *(pairs[step] for step in range(outer)))
     other = flipped(mine, 1)
 
     own_grads, dots = pl.pallas_call(
@@ -401,12 +406,12 @@
             jax.ShapeDtypeStruct((1,) + block_shape, jnp.float32),
             jax.ShapeDtypeStruct((cap, side), jnp.float32),
         ),
-        in_specs=[VMEM_SPEC] * 5,
+        in_specs=[VMEM_SPEC] * 4,
         out_specs=(VMEM_SPEC, VMEM_SPEC),
         compiler_params=params,
         cost_estimate=cost(6.0),
         name="owner_sums",
-    )(scale_rows, stored, own_sum, other_sum, neighbour)
+    )(scale_rows, stored, own_sum, other_sum)
     other_dots = lax.ppermute(dots, "group", [(0, 1), (1, 0)])
     grad_inputs_t, block_grads = pl.pallas_call(
         input_grad_kernel,

time: 26.9 us -> 27 us (level)
    ppermute x5, waiting for transfers between devices: 3.7 us -> 4.44 us  [stepped(): lax.ppermute(value, 'dp', [(i, ahead(size // 4, i // 4, steps[i % 2]) * 4...]
    ppermute x6, waiting for transfers between devices: 0.93 us -> 0.31 us  [flipped(): lax.ppermute(value, 'dp', [(i, i ^ bit) for i in range(lax.axis_size('dp'...]
    ppermute x6, starting transfers between devices: 5.25 us -> 4.77 us  [flipped(): lax.ppermute(value, 'dp', [(i, i ^ bit) for i in range(lax.axis_size('dp'...]
    ppermute x5, starting transfers between devices: 8.02 us -> 8.46 us  [stepped(): lax.ppermute(value, 'dp', [(i, ahead(size // 4, i // 4, steps[i % 2]) * 4...]
  transfers between devices with their start and end apart: 12 -> 12, of which waited for: 3 -> 4; matrix products, arithmetic and copies ran while one was open for 0% -> 0% of each run, Pallas kernels for 9% -> 9%
where the time goes in v5:
time: 27 us; the launch traced here: 26.8 us
  starting transfers between devices  14.8 us (55%)
  Pallas kernels  6.53 us (24%)
  waiting for transfers between devices  4.76 us (18%)
  between operations  0.7 us (3%)
    ppermute x5, starting transfers between devices, stepped(): lax.ppermute(value, 'dp', [(i, ahead(size // 4, i // 4, steps[i % 2]) * 4...  8.46 us
    ppermute x6, starting transfers between devices, flipped(): lax.ppermute(value, 'dp', [(i, i ^ bit) for i in range(lax.axis_size('dp'...  4.77 us
    ppermute x5, waiting for transfers between devices, stepped(): lax.ppermute(value, 'dp', [(i, ahead(size // 4, i // 4, steps[i % 2]) * 4...  4.44 us
    pallas_call x1, Pallas kernels, on_device(): pl.pallas_call(partial_kernel, out_shape=[jax.ShapeDtypeStruct(side_shape...  3.44 us
    pallas_call x1, Pallas kernels, on_device(): pl.pallas_call(input_grad_kernel, out_shape=(jax.ShapeDtypeStruct(inputs_...  2.1 us
    ppermute x1, starting transfers between devices, on_device(): other_dots = lax.ppermute(dots, 'group', [(0, 1), (1, 0)])  1.56 us
    pallas_call x1, Pallas kernels, on_device(): pl.pallas_call(finish_kernel, out_shape=jax.ShapeDtypeStruct((1, cap), jn...  0.6 us
  transfers between devices with their start and end apart: 12, of which 4 were waited for; matrix products, arithmetic and copies ran while one was open for 0% of the time, Pallas kernels for 9%

profile of v5, /device:TPU:0, one launch (start us, length us, event | category | flops | bytes accessed | tf_op | source)
XLA Modules:
  0.0 26.8 jit_solution(8268758825985985558)
XLA Ops:
  0.6 3.4 %partials.1 = (f32[4,2,64,128]{3,2,1,0:T(8,128)S(1)}, f32[4,2,64,128]{3,2,1,0:T(8,128)S(1)}, f32[4,2,64,128]{3,2,1,0:T(8,128)S(1)}, f32[4,2,64,128]{3,2,1,0:T(8,...) custom-call(s32[2,3584]{1,0:T(2,128)} %kept_hbm.1, ...), custom_call_target="tpu_custom_call" | custom-call | flops 4035500032 | bytes 12915000 | tf_op jit(solution)/shard_map/partials/pallas_call | solution.py:304
  4.1 0.5 %collective-permute-start.1 = (f32[4,2,64,128]{3,2,1,0:T(8,128)S(1)}, f32[4,2,64,128]{3,2,1,0:T(8,128)S(1)}, u32[]{:S(2)}, u32[]{:S(2)}) collective-permute-start(f32[4,2,64,128]{3,2,1,0:T(8,128)S(1)} %get-tuple-element.27), channel_id=1, source_target_pairs={{0,2},{2,0},{4,6},{6,4},{8,10},{10,8},{12,14},{14,12},{16,18},{18,... | collective-permute-start | bytes 786440 | tf_op jit(solution)/shard_map/ppermute | solution.py:254
  4.6 2.6 %collective-permute-start = (bf16[2,64,128]{2,1,0:T(8,128)(2,1)S(1)}, bf16[2,64,128]{2,1,0:T(8,128)(2,1)S(1)}, u32[]{:S(2)}, u32[]{:S(2)}) collective-permute-start(bf16[2,64,128]{2,1,0:T(8,128)(2,1)S(1)} %get-tuple-element.25.refs_0_), channel_id=1, source_target_pairs={{0,4},{2,6},{4,0},{6,2},{8,12},{10,14},{12,8},{14,10},{16,20},{18,... | collective-permute-start | bytes 98312 | tf_op jit(solution)/shard_map/ppermute | solution.py:254
  7.2 0.0 collective-permute-done.1.got_ref
  7.2 0.2 far_sums.1
  7.4 1.5 %collective-permute-start.5 = (s16[528,128]{1,0:T(8,128)(2,1)S(1)}, s16[528,128]{1,0:T(8,128)(2,1)S(1)}, u32[]{:S(2)}, u32[]{:S(2)}) collective-permute-start(s16[528,128]{1,0:T(8,128)(2,1)S(1)} %get-tuple-element.29.refs_2_), channel_id=1, source_target_pairs={{0,4},{2,6},{4,0},{6,2},{8,12},{10,14},{12,8},{14,10},{16,20},{18,... | collective-permute-start | bytes 405512 | tf_op jit(solution)/shard_map/ppermute | solution.py:254
  8.9 0.0 collective-permute-start.4
  8.9 0.3 %collective-permute-done.refs_1_ = bf16[2,64,128]{2,1,0:T(8,128)(2,1)S(1)} collective-permute-done((bf16[2,64,128]{2,1,0:T(8,128)(2,1)S(1)}, bf16[2,64,128]{2,1,0:T(8,128)(2,1)S(1)}, u32[]{:S(2)}, u32[]{:S(2)}) %collective-permute-start) | collective-permute-done | bytes 32800 | tf_op jit(solution)/shard_map/ppermute | solution.py:254
  9.2 2.0 %collective-permute-start.2 = (bf16[2,2,64,128]{3,2,1,0:T(8,128)(2,1)S(1)}, bf16[2,2,64,128]{3,2,1,0:T(8,128)(2,1)S(1)}, u32[]{:S(2)}, u32[]{:S(2)}) collective-permute-start(bf16[2,2,64,128]{3,2,1,0:T(8,128)(2,1)S(1)} %pair.1.refs_0_), channel_id=1, source_target_pairs={{0,8},{2,10},{4,12},{6,14},{8,0},{10,2},{12,4},{14,6},{16,24},{18,... | collective-permute-start | bytes 196616 | tf_op jit(solution)/shard_map/ppermute | solution.py:268
  11.2 2.6 %collective-permute-start.3 = (bf16[2,2,64,128]{3,2,1,0:T(8,128)(2,1)S(1)}, bf16[2,2,64,128]{3,2,1,0:T(8,128)(2,1)S(1)}, u32[]{:S(2)}, u32[]{:S(2)}) collective-permute-start(bf16[2,2,64,128]{3,2,1,0:T(8,128)(2,1)S(1)} %pair.1.refs_0_), channel_id=1, source_target_pairs={{0,16},{2,18},{4,20},{6,22},{8,24},{10,26},{12,28},{14,30},{16,0},... | collective-permute-start | bytes 196616 | tf_op jit(solution)/shard_map/ppermute | solution.py:268
  13.8 0.0 collective-permute-done.5.far_ref
  13.8 0.0 collective-permute-done.4.got_ref
  13.8 0.1 near_sums.1
  13.9 3.0 %collective-permute-start.9 = (s16[272,128]{1,0:T(8,128)(2,1)S(1)}, s16[272,128]{1,0:T(8,128)(2,1)S(1)}, u32[]{:S(2)}, u32[]{:S(2)}) collective-permute-start(s16[272,128]{1,0:T(8,128)(2,1)S(1)} %get-tuple-element.36), channel_id=1, source_target_pairs={{0,24},{2,18},{4,28},{6,22},{8,16},{10,26},{12,20},{14,30},{16,8},... | collective-permute-start | bytes 208904 | tf_op jit(solution)/shard_map/ppermute | solution.py:268
  16.9 0.0 collective-permute-start.8
  16.9 0.0 collective-permute-done.2.refs_2_.refs_1_
  16.9 1.2 %collective-permute-done.3.refs_0_.refs_2_ = bf16[2,2,64,128]{3,2,1,0:T(8,128)(2,1)S(1)} collective-permute-done((bf16[2,2,64,128]{3,2,1,0:T(8,128)(2,1)S(1)}, bf16[2,2,64,128]{3,2,1,0:T(8,128)(2,1)S(1)}, u32[]{:S(2)}, u32[]{:S(2)}) %collective-permute-start.3) | collective-permute-done | bytes 65568 | tf_op jit(solution)/shard_map/ppermute | solution.py:268
  18.1 0.9 %collective-permute-start.6 = (bf16[2,2,64,128]{3,2,1,0:T(8,128)(2,1)S(1)}, bf16[2,2,64,128]{3,2,1,0:T(8,128)(2,1)S(1)}, u32[]{:S(2)}, u32[]{:S(2)}) collective-permute-start(bf16[2,2,64,128]{3,2,1,0:T(8,128)(2,1)S(1)} %bitcast.1), channel_id=1, source_target_pairs={{0,8},{2,10},{4,12},{6,14},{8,0},{10,2},{12,4},{14,6},{16,24},{18,... | collective-permute-start | bytes 196616 | tf_op jit(solution)/shard_map/ppermute | solution.py:268
  19.0 2.0 %collective-permute-done.8.neighbour_ref = s16[144,128]{1,0:T(8,128)(2,1)S(1)} collective-permute-done((s16[144,128]{1,0:T(8,128)(2,1)S(1)}, s16[144,128]{1,0:T(8,128)(2,1)S(1)}, u32[]{:S(2)}, u32[]{:S(2)}) %collective-permute-start.8) | collective-permute-done | bytes 36896 | tf_op jit(solution)/shard_map/ppermute | solution.py:268
  21.0 0.0 collective-permute-done.9.refs_0_
  21.0 0.1 collective-permute-start.10
  21.1 1.3 %collective-permute-done.6.refs_3_ = bf16[2,2,64,128]{3,2,1,0:T(8,128)(2,1)S(1)} collective-permute-done((bf16[2,2,64,128]{3,2,1,0:T(8,128)(2,1)S(1)}, bf16[2,2,64,128]{3,2,1,0:T(8,128)(2,1)S(1)}, u32[]{:S(2)}, u32[]{:S(2)}) %collective-permute-start.6) | collective-permute-done | bytes 65568 | tf_op jit(solution)/shard_map/ppermute | solution.py:268
  22.4 0.1 collective-permute-start.7
  22.5 0.0 collective-permute-done.10.other_ref
  22.5 1.6 %collective-permute-start.11 = (f32[2,128]{1,0:T(2,128)S(1)}, f32[2,128]{1,0:T(2,128)S(1)}, u32[]{:S(2)}, u32[]{:S(2)}) collective-permute-start(f32[2,128]{1,0:T(2,128)S(1)} %get-tuple-element.42.dots_ref), channel_id=1, source_target_pairs={{0,1},{1,0},{2,3},{3,2},{4,5},{5,4},{6,7},{7,6},{8,9},{9,8},{10,11... | collective-permute-start | bytes 3080 | tf_op jit(solution)/shard_map/ppermute | solution.py:415
  24.1 0.0 collective-permute-done.7.other
  24.1 2.1 %input_grads.1 = (bf16[64,64,128]{2,1,0:T(8,128)(2,1)}, f32[1,2,64,128]{3,2,1,0:T(8,128)}) custom-call(s32[4,24]{1,0:T(4,128)S(1)} %get-tuple-element.23.tab_ref, bf16[24,128,128]{2,1,0:T(8,128)(2,1)S(1)} %get-tuple-element.24.cols_ref, bf16[4,2,2,64,128]{4,3,2,1,0:T(8,128)(2,1)S(1)} %mine.1, bf16[4,2,2,64,128]{4,3,2,1,0:T(8,128)(2,1)S(1)} %collective-permute-done.7.other, ...), custom_call_target="tpu_custom_call" | custom-call | flops 2305999872 | bytes 7380000 | tf_op jit(solution)/shard_map/input_grads/pallas_call | solution.py:416
  26.2 0.0 collective-permute-done.11.got_ref
  26.2 0.6 %finish.1 = f32[1,2]{1,0:T(1,128)} custom-call(f32[2,128]{1,0:T(2,128)S(1)} %get-tuple-element.42.dots_ref, f32[2,128]{1,0:T(2,128)S(1)} %collective-permute-done.11.got_ref, bf16[64,64,128]{2,1,0:T(8,128)(2,1)} %get-tuple-element.20.grads_ref), custom_call_target="tpu_custom_call" | custom-call | flops 576499968 | bytes 1845000 | tf_op jit(solution)/shard_map/finish/pallas_call | solution.py:429
  (5 shorter events, 0.1 us)
Async XLA Ops:
  4.1 3.1 %collective-permute-start.1 = (f32[4,2,64,128]{3,2,1,0:T(8,128)S(1)}, f32[4,2,64,128]{3,2,1,0:T(8,128)S(1)}, u32[]{:S(2)}, u32[]{:S(2)}) collective-permute-start(f32[4,2,64,128]{3,2,1,0:T(8,128)S(1)} %get-tuple-element.27), channel_id=1, source_target_pairs={{0,2},{2,0},{4,6},{6,4},{8,10},{10,8},{12,14},{14,12},{16,18},{18,... | collective-permute-start | bytes 786440 | tf_op jit(solution)/shard_map/ppermute | solution.py:254
  4.6 4.6 %collective-permute-start = (bf16[2,64,128]{2,1,0:T(8,128)(2,1)S(1)}, bf16[2,64,128]{2,1,0:T(8,128)(2,1)S(1)}, u32[]{:S(2)}, u32[]{:S(2)}) collective-permute-start(bf16[2,64,128]{2,1,0:T(8,128)(2,1)S(1)} %get-tuple-element.25.refs_0_), channel_id=1, source_target_pairs={{0,4},{2,6},{4,0},{6,2},{8,12},{10,14},{12,8},{14,10},{16,20},{18,... | collective-permute-start | bytes 98312 | tf_op jit(solution)/shard_map/ppermute | solution.py:254
  7.4 6.4 %collective-permute-start.5 = (s16[528,128]{1,0:T(8,128)(2,1)S(1)}, s16[528,128]{1,0:T(8,128)(2,1)S(1)}, u32[]{:S(2)}, u32[]{:S(2)}) collective-permute-start(s16[528,128]{1,0:T(8,128)(2,1)S(1)} %get-tuple-element.29.refs_2_), channel_id=1, source_target_pairs={{0,4},{2,6},{4,0},{6,2},{8,12},{10,14},{12,8},{14,10},{16,20},{18,... | collective-permute-start | bytes 405512 | tf_op jit(solution)/shard_map/ppermute | solution.py:254
  8.9 4.9 %collective-permute-start.4 = (f32[4,2,64,128]{3,2,1,0:T(8,128)S(1)}, f32[4,2,64,128]{3,2,1,0:T(8,128)S(1)}, u32[]{:S(2)}, u32[]{:S(2)}) collective-permute-start(f32[4,2,64,128]{3,2,1,0:T(8,128)S(1)} %get-tuple-element.31), channel_id=1, source_target_pairs={{0,2},{2,0},{4,6},{6,4},{8,10},{10,8},{12,14},{14,12},{16,18},{18,... | collective-permute-start | bytes 786440 | tf_op jit(solution)/shard_map/ppermute | solution.py:254
  9.2 7.7 %collective-permute-start.2 = (bf16[2,2,64,128]{3,2,1,0:T(8,128)(2,1)S(1)}, bf16[2,2,64,128]{3,2,1,0:T(8,128)(2,1)S(1)}, u32[]{:S(2)}, u32[]{:S(2)}) collective-permute-start(bf16[2,2,64,128]{3,2,1,0:T(8,128)(2,1)S(1)} %pair.1.refs_0_), channel_id=1, source_target_pairs={{0,8},{2,10},{4,12},{6,14},{8,0},{10,2},{12,4},{14,6},{16,24},{18,... | collective-permute-start | bytes 196616 | tf_op jit(solution)/shard_map/ppermute | solution.py:268
  11.2 6.9 %collective-permute-start.3 = (bf16[2,2,64,128]{3,2,1,0:T(8,128)(2,1)S(1)}, bf16[2,2,64,128]{3,2,1,0:T(8,128)(2,1)S(1)}, u32[]{:S(2)}, u32[]{:S(2)}) collective-permute-start(bf16[2,2,64,128]{3,2,1,0:T(8,128)(2,1)S(1)} %pair.1.refs_0_), channel_id=1, source_target_pairs={{0,16},{2,18},{4,20},{6,22},{8,24},{10,26},{12,28},{14,30},{16,0},... | collective-permute-start | bytes 196616 | tf_op jit(solution)/shard_map/ppermute | solution.py:268
  13.9 7.1 %collective-permute-start.9 = (s16[272,128]{1,0:T(8,128)(2,1)S(1)}, s16[272,128]{1,0:T(8,128)(2,1)S(1)}, u32[]{:S(2)}, u32[]{:S(2)}) collective-permute-start(s16[272,128]{1,0:T(8,128)(2,1)S(1)} %get-tuple-element.36), channel_id=1, source_target_pairs={{0,24},{2,18},{4,28},{6,22},{8,16},{10,26},{12,20},{14,30},{16,8},... | collective-permute-start | bytes 208904 | tf_op jit(solution)/shard_map/ppermute | solution.py:268
  16.9 4.1 %collective-permute-start.8 = (s16[144,128]{1,0:T(8,128)(2,1)S(1)}, s16[144,128]{1,0:T(8,128)(2,1)S(1)}, u32[]{:S(2)}, u32[]{:S(2)}) collective-permute-start(s16[144,128]{1,0:T(8,128)(2,1)S(1)} %get-tuple-element.32.refs_1_.refs_4_), channel_id=1, source_target_pairs={{0,8},{2,10},{4,12},{6,14},{8,0},{10,2},{12,4},{14,6},{16,24},{18,... | collective-permute-start | bytes 110600 | tf_op jit(solution)/shard_map/ppermute | solution.py:268
  18.1 4.3 %collective-permute-start.6 = (bf16[2,2,64,128]{3,2,1,0:T(8,128)(2,1)S(1)}, bf16[2,2,64,128]{3,2,1,0:T(8,128)(2,1)S(1)}, u32[]{:S(2)}, u32[]{:S(2)}) collective-permute-start(bf16[2,2,64,128]{3,2,1,0:T(8,128)(2,1)S(1)} %bitcast.1), channel_id=1, source_target_pairs={{0,8},{2,10},{4,12},{6,14},{8,0},{10,2},{12,4},{14,6},{16,24},{18,... | collective-permute-start | bytes 196616 | tf_op jit(solution)/shard_map/ppermute | solution.py:268
  21.0 1.4 %collective-permute-start.10 = (f32[2,64,128]{2,1,0:T(8,128)S(1)}, f32[2,64,128]{2,1,0:T(8,128)S(1)}, u32[]{:S(2)}, u32[]{:S(2)}) collective-permute-start(f32[2,64,128]{2,1,0:T(8,128)S(1)} %get-tuple-element.38), channel_id=1, source_target_pairs={{0,2},{2,0},{4,6},{6,4},{8,10},{10,8},{12,14},{14,12},{16,18},{18,... | collective-permute-start | bytes 196616 | tf_op jit(solution)/shard_map/ppermute | solution.py:254
  22.4 1.7 %collective-permute-start.7 = (bf16[4,2,2,64,128]{4,3,2,1,0:T(8,128)(2,1)S(1)}, bf16[4,2,2,64,128]{4,3,2,1,0:T(8,128)(2,1)S(1)}, u32[]{:S(2)}, u32[]{:S(2)}) collective-permute-start(bf16[4,2,2,64,128]{4,3,2,1,0:T(8,128)(2,1)S(1)} %mine.1), channel_id=1, source_target_pairs={{0,2},{2,0},{4,6},{6,4},{8,10},{10,8},{12,14},{14,12},{16,18},{18,... | collective-permute-start | bytes 786440 | tf_op jit(solution)/shard_map/ppermute | solution.py:254
  22.5 3.7 %collective-permute-start.11 = (f32[2,128]{1,0:T(2,128)S(1)}, f32[2,128]{1,0:T(2,128)S(1)}, u32[]{:S(2)}, u32[]{:S(2)}) collective-permute-start(f32[2,128]{1,0:T(2,128)S(1)} %get-tuple-element.42.dots_ref), channel_id=1, source_target_pairs={{0,1},{1,0},{2,3},{3,2},{4,5},{5,4},{6,7},{7,6},{8,9},{9,8},{10,11... | collective-permute-start | bytes 3080 | tf_op jit(solution)/shard_map/ppermute | solution.py:415

commit v6 on v2

--- a/solution.py
+++ b/solution.py
@@ -31,17 +31,14 @@
     part_ref, x_ref, scales_ref, kept, assign, counts, slot_ref, sem, index_sems, x_sem
 ):
     x_copy = pltpu.make_async_copy(x_hbm, x_ref, x_sem)
+    pieces = 4 if kept.shape[1] % 512 == 0 else 1
+    width = kept.shape[1] // pieces
+    columns = [pl.ds(i * width, width) for i in range(pieces)]
+    early = [(assign_hbm, assign)] + [(kept_hbm.at[:, c], kept.at[:, c]) for c in columns]
+    late = [(counts_hbm, counts), (scales_hbm, scales_ref), (stored_hbm, stored_ref)]
     index_copies = [
         pltpu.make_async_copy(source, target, index_sems.at[i])
-        for i, (source, target) in enumerate(
-            (
-                (assign_hbm, assign),
-                (kept_hbm, kept),
-                (counts_hbm, counts),
-                (scales_hbm, scales_ref),
-                (stored_hbm, stored_ref),
-            )
-        )
+        for i, (source, target) in enumerate(early + late)
     ]
     for copy in index_copies:
         copy.start()
@@ -54,7 +51,7 @@
     outer, cap = near_keep.shape[:2]
     me = lax.axis_index("dp")
     part_ref[...] = jnp.zeros_like(part_ref)
-    for copy in index_copies[:2]:
+    for copy in index_copies[: len(early)]:
         copy.wait()
 
     def fetch_step(p, carry):
@@ -68,7 +65,7 @@
         return carry
 
     lax.fori_loop(0, entries, fetch_step, 0, unroll=min(entries, 24))
-    for copy in index_copies[2:]:
+    for copy in index_copies[len(early) :]:
         copy.wait()
 
     def owner_step(owner, offset):
@@ -312,7 +309,7 @@
             pltpu.SMEM(owner_counts.shape, jnp.int32),
             pltpu.SMEM((entries,), jnp.int32),
             pltpu.SemaphoreType.DMA,
-            pltpu.SemaphoreType.DMA((5,)),
+            pltpu.SemaphoreType.DMA((8,)),
             pltpu.SemaphoreType.DMA,
         ],
         compiler_params=params,

time: 26.7 us -> 26.7 us (level)
  no operation moved by 1% of the time
where the time goes in v6:
time: 26.7 us; the launch traced here: 26.5 us
  starting transfers between devices  15.3 us (57%)
  Pallas kernels  6.55 us (25%)
  waiting for transfers between devices  3.92 us (15%)
  between operations  0.7 us (3%)
    ppermute x6, starting transfers between devices, stepped(): lax.ppermute(value, 'dp', [(i, ahead(size // 4, i // 4, step) * 4 + i % 4...  9.03 us
    ppermute x5, starting transfers between devices, flipped(): lax.ppermute(value, 'dp', [(i, i ^ bit) for i in range(lax.axis_size('dp'...  4.7 us
    ppermute x6, waiting for transfers between devices, stepped(): lax.ppermute(value, 'dp', [(i, ahead(size // 4, i // 4, step) * 4 + i % 4...  3.6 us
    pallas_call x1, Pallas kernels, on_device(): pl.pallas_call(partial_kernel, out_shape=[jax.ShapeDtypeStruct(side_shape...  3.47 us
    pallas_call x1, Pallas kernels, on_device(): pl.pallas_call(input_grad_kernel, out_shape=(jax.ShapeDtypeStruct(inputs_...  2.1 us
    ppermute x1, starting transfers between devices, on_device(): other_dots = lax.ppermute(dots, 'group', [(0, 1), (1, 0)])  1.56 us
    pallas_call x1, Pallas kernels, on_device(): pl.pallas_call(finish_kernel, out_shape=jax.ShapeDtypeStruct((1, cap), jn...  0.6 us
  transfers between devices with their start and end apart: 12, of which 5 were waited for; matrix products, arithmetic and copies ran while one was open for 0% of the time, Pallas kernels for 9%

profile of v6, /device:TPU:0, one launch (start us, length us, event | category | flops | bytes accessed | tf_op | source)
XLA Modules:
  0.0 26.5 jit_solution(13195234573943776122)
XLA Ops:
  0.6 3.5 %partials.1 = (f32[4,2,64,128]{3,2,1,0:T(8,128)S(1)}, f32[4,2,64,128]{3,2,1,0:T(8,128)S(1)}, f32[4,2,64,128]{3,2,1,0:T(8,128)S(1)}, f32[4,2,64,128]{3,2,1,0:T(8,...) custom-call(s32[2,3584]{1,0:T(2,128)} %kept_hbm.1, ...), custom_call_target="tpu_custom_call" | custom-call | flops 4035500032 | bytes 12915000 | tf_op jit(solution)/shard_map/partials/pallas_call | solution.py:291
  4.1 0.5 %collective-permute-start.1 = (f32[4,2,64,128]{3,2,1,0:T(8,128)S(1)}, f32[4,2,64,128]{3,2,1,0:T(8,128)S(1)}, u32[]{:S(2)}, u32[]{:S(2)}) collective-permute-start(f32[4,2,64,128]{3,2,1,0:T(8,128)S(1)} %get-tuple-element.26), channel_id=1, source_target_pairs={{0,2},{2,0},{4,6},{6,4},{8,10},{10,8},{12,14},{14,12},{16,18},{18,... | collective-permute-start | bytes 786440 | tf_op jit(solution)/shard_map/ppermute | solution.py:244
  4.6 2.6 %collective-permute-start = (bf16[2,64,128]{2,1,0:T(8,128)(2,1)S(1)}, bf16[2,64,128]{2,1,0:T(8,128)(2,1)S(1)}, u32[]{:S(2)}, u32[]{:S(2)}) collective-permute-start(bf16[2,64,128]{2,1,0:T(8,128)(2,1)S(1)} %get-tuple-element.24.refs_0_), channel_id=1, source_target_pairs={{0,4},{2,6},{4,0},{6,2},{8,12},{10,14},{12,8},{14,10},{16,20},{18,... | collective-permute-start | bytes 98312 | tf_op jit(solution)/shard_map/ppermute | solution.py:244
  7.2 0.0 collective-permute-done.1.got_ref
  7.2 0.1 far_sums.1
  7.4 1.5 %collective-permute-start.5 = (s16[528,128]{1,0:T(8,128)(2,1)S(1)}, s16[528,128]{1,0:T(8,128)(2,1)S(1)}, u32[]{:S(2)}, u32[]{:S(2)}) collective-permute-start(s16[528,128]{1,0:T(8,128)(2,1)S(1)} %get-tuple-element.28.refs_2_), channel_id=1, source_target_pairs={{0,4},{2,6},{4,0},{6,2},{8,12},{10,14},{12,8},{14,10},{16,20},{18,... | collective-permute-start | bytes 405512 | tf_op jit(solution)/shard_map/ppermute | solution.py:244
  8.9 0.0 collective-permute-start.4
  8.9 0.3 %collective-permute-done.refs_1_ = bf16[2,64,128]{2,1,0:T(8,128)(2,1)S(1)} collective-permute-done((bf16[2,64,128]{2,1,0:T(8,128)(2,1)S(1)}, bf16[2,64,128]{2,1,0:T(8,128)(2,1)S(1)}, u32[]{:S(2)}, u32[]{:S(2)}) %collective-permute-start) | collective-permute-done | bytes 32800 | tf_op jit(solution)/shard_map/ppermute | solution.py:244
  9.2 3.0 %collective-permute-start.3 = (bf16[2,2,64,128]{3,2,1,0:T(8,128)(2,1)S(1)}, bf16[2,2,64,128]{3,2,1,0:T(8,128)(2,1)S(1)}, u32[]{:S(2)}, u32[]{:S(2)}) collective-permute-start(bf16[2,2,64,128]{3,2,1,0:T(8,128)(2,1)S(1)} %pair.1.refs_0_), channel_id=1, source_target_pairs={{0,16},{2,18},{4,20},{6,22},{8,24},{10,26},{12,28},{14,30},{16,0},... | collective-permute-start | bytes 196616 | tf_op jit(solution)/shard_map/ppermute | solution.py:257
  12.2 1.3 %collective-permute-start.6 = (bf16[2,2,64,128]{3,2,1,0:T(8,128)(2,1)S(1)}, bf16[2,2,64,128]{3,2,1,0:T(8,128)(2,1)S(1)}, u32[]{:S(2)}, u32[]{:S(2)}) collective-permute-start(bf16[2,2,64,128]{3,2,1,0:T(8,128)(2,1)S(1)} %pair.1.refs_0_), channel_id=1, source_target_pairs={{0,24},{2,26},{4,28},{6,30},{8,16},{10,18},{12,20},{14,22},{16,8},... | collective-permute-start | bytes 196616 | tf_op jit(solution)/shard_map/ppermute | solution.py:257
  13.6 0.2 collective-permute-start.2
  13.8 0.0 collective-permute-done.5.far_ref
  13.8 0.0 collective-permute-done.4.got_ref
  13.8 0.1 near_sums.1
  13.9 3.0 %collective-permute-start.8 = (s16[144,128]{1,0:T(8,128)(2,1)S(1)}, s16[144,128]{1,0:T(8,128)(2,1)S(1)}, u32[]{:S(2)}, u32[]{:S(2)}) collective-permute-start(s16[144,128]{1,0:T(8,128)(2,1)S(1)} %get-tuple-element.35), channel_id=1, source_target_pairs={{0,24},{2,26},{4,28},{6,30},{8,16},{10,18},{12,20},{14,22},{16,8},... | collective-permute-start | bytes 110600 | tf_op jit(solution)/shard_map/ppermute | solution.py:257
  16.9 0.3 %collective-permute-start.9 = (s16[144,128]{1,0:T(8,128)(2,1)S(1)}, s16[144,128]{1,0:T(8,128)(2,1)S(1)}, u32[]{:S(2)}, u32[]{:S(2)}) collective-permute-start(s16[144,128]{1,0:T(8,128)(2,1)S(1)} %get-tuple-element.36), channel_id=1, source_target_pairs={{0,16},{2,18},{4,20},{6,22},{8,24},{10,26},{12,28},{14,30},{16,0},... | collective-permute-start | bytes 110600 | tf_op jit(solution)/shard_map/ppermute | solution.py:257
  17.3 0.0 collective-permute-done.3.refs_0_
  17.3 1.1 %collective-permute-start.10 = (s16[144,128]{1,0:T(8,128)(2,1)S(1)}, s16[144,128]{1,0:T(8,128)(2,1)S(1)}, u32[]{:S(2)}, u32[]{:S(2)}) collective-permute-start(s16[144,128]{1,0:T(8,128)(2,1)S(1)} %get-tuple-element.31.refs_1_), channel_id=1, source_target_pairs={{0,8},{2,10},{4,12},{6,14},{8,0},{10,2},{12,4},{14,6},{16,24},{18,... | collective-permute-start | bytes 110600 | tf_op jit(solution)/shard_map/ppermute | solution.py:257
  18.4 0.4 %collective-permute-done.6.refs_0_ = bf16[2,2,64,128]{3,2,1,0:T(8,128)(2,1)S(1)} collective-permute-done((bf16[2,2,64,128]{3,2,1,0:T(8,128)(2,1)S(1)}, bf16[2,2,64,128]{3,2,1,0:T(8,128)(2,1)S(1)}, u32[]{:S(2)}, u32[]{:S(2)}) %collective-permute-start.6) | collective-permute-done | bytes 65568 | tf_op jit(solution)/shard_map/ppermute | solution.py:257
  18.9 0.1 collective-permute-done.2.refs_1_
  19.0 0.1 collective-permute-start.7
  19.0 1.2 %collective-permute-done.8.refs_0_ = s16[144,128]{1,0:T(8,128)(2,1)S(1)} collective-permute-done((s16[144,128]{1,0:T(8,128)(2,1)S(1)}, s16[144,128]{1,0:T(8,128)(2,1)S(1)}, u32[]{:S(2)}, u32[]{:S(2)}) %collective-permute-start.8) | collective-permute-done | bytes 36896 | tf_op jit(solution)/shard_map/ppermute | solution.py:257
  20.2 1.9 %collective-permute-done.9.refs_0_ = s16[144,128]{1,0:T(8,128)(2,1)S(1)} collective-permute-done((s16[144,128]{1,0:T(8,128)(2,1)S(1)}, s16[144,128]{1,0:T(8,128)(2,1)S(1)}, u32[]{:S(2)}, u32[]{:S(2)}) %collective-permute-start.9) | collective-permute-done | bytes 36896 | tf_op jit(solution)/shard_map/ppermute | solution.py:257
  22.1 0.0 collective-permute-done.10.refs_0_
  22.2 1.6 %collective-permute-start.11 = (f32[2,128]{1,0:T(2,128)S(1)}, f32[2,128]{1,0:T(2,128)S(1)}, u32[]{:S(2)}, u32[]{:S(2)}) collective-permute-start(f32[2,128]{1,0:T(2,128)S(1)} %get-tuple-element.40.dots_ref), channel_id=1, source_target_pairs={{0,1},{1,0},{2,3},{3,2},{4,5},{5,4},{6,7},{7,6},{8,9},{9,8},{10,11... | collective-permute-start | bytes 3080 | tf_op jit(solution)/shard_map/ppermute | solution.py:390
  23.8 0.0 collective-permute-done.7.other
  23.8 2.1 %input_grads.1 = (bf16[64,64,128]{2,1,0:T(8,128)(2,1)}, f32[1,2,64,128]{3,2,1,0:T(8,128)}) custom-call(s32[4,24]{1,0:T(4,128)S(1)} %get-tuple-element.22.tab_ref, bf16[24,128,128]{2,1,0:T(8,128)(2,1)S(1)} %get-tuple-element.23.cols_ref, bf16[4,2,2,64,128]{4,3,2,1,0:T(8,128)(2,1)S(1)} %mine.1, bf16[4,2,2,64,128]{4,3,2,1,0:T(8,128)(2,1)S(1)} %collective-permute-done.7.other, ...), custom_call_target="tpu_custom_call" | custom-call | flops 2305999872 | bytes 7380000 | tf_op jit(solution)/shard_map/input_grads/pallas_call | solution.py:391
  25.9 0.0 collective-permute-done.11.got_ref
  25.9 0.6 %finish.1 = f32[1,2]{1,0:T(1,128)} custom-call(f32[2,128]{1,0:T(2,128)S(1)} %get-tuple-element.40.dots_ref, f32[2,128]{1,0:T(2,128)S(1)} %collective-permute-done.11.got_ref, bf16[64,64,128]{2,1,0:T(8,128)(2,1)} %get-tuple-element.19.grads_ref), custom_call_target="tpu_custom_call" | custom-call | flops 576499968 | bytes 1845000 | tf_op jit(solution)/shard_map/finish/pallas_call | solution.py:404
  (7 shorter events, 0.1 us)
Async XLA Ops:
  4.1 3.1 %collective-permute-start.1 = (f32[4,2,64,128]{3,2,1,0:T(8,128)S(1)}, f32[4,2,64,128]{3,2,1,0:T(8,128)S(1)}, u32[]{:S(2)}, u32[]{:S(2)}) collective-permute-start(f32[4,2,64,128]{3,2,1,0:T(8,128)S(1)} %get-tuple-element.26), channel_id=1, source_target_pairs={{0,2},{2,0},{4,6},{6,4},{8,10},{10,8},{12,14},{14,12},{16,18},{18,... | collective-permute-start | bytes 786440 | tf_op jit(solution)/shard_map/ppermute | solution.py:244
  4.6 4.6 %collective-permute-start = (bf16[2,64,128]{2,1,0:T(8,128)(2,1)S(1)}, bf16[2,64,128]{2,1,0:T(8,128)(2,1)S(1)}, u32[]{:S(2)}, u32[]{:S(2)}) collective-permute-start(bf16[2,64,128]{2,1,0:T(8,128)(2,1)S(1)} %get-tuple-element.24.refs_0_), channel_id=1, source_target_pairs={{0,4},{2,6},{4,0},{6,2},{8,12},{10,14},{12,8},{14,10},{16,20},{18,... | collective-permute-start | bytes 98312 | tf_op jit(solution)/shard_map/ppermute | solution.py:244
  7.4 6.4 %collective-permute-start.5 = (s16[528,128]{1,0:T(8,128)(2,1)S(1)}, s16[528,128]{1,0:T(8,128)(2,1)S(1)}, u32[]{:S(2)}, u32[]{:S(2)}) collective-permute-start(s16[528,128]{1,0:T(8,128)(2,1)S(1)} %get-tuple-element.28.refs_2_), channel_id=1, source_target_pairs={{0,4},{2,6},{4,0},{6,2},{8,12},{10,14},{12,8},{14,10},{16,20},{18,... | collective-permute-start | bytes 405512 | tf_op jit(solution)/shard_map/ppermute | solution.py:244
  8.9 4.9 %collective-permute-start.4 = (f32[4,2,64,128]{3,2,1,0:T(8,128)S(1)}, f32[4,2,64,128]{3,2,1,0:T(8,128)S(1)}, u32[]{:S(2)}, u32[]{:S(2)}) collective-permute-start(f32[4,2,64,128]{3,2,1,0:T(8,128)S(1)} %get-tuple-element.30), channel_id=1, source_target_pairs={{0,2},{2,0},{4,6},{6,4},{8,10},{10,8},{12,14},{14,12},{16,18},{18,... | collective-permute-start | bytes 786440 | tf_op jit(solution)/shard_map/ppermute | solution.py:244
  9.2 8.1 %collective-permute-start.3 = (bf16[2,2,64,128]{3,2,1,0:T(8,128)(2,1)S(1)}, bf16[2,2,64,128]{3,2,1,0:T(8,128)(2,1)S(1)}, u32[]{:S(2)}, u32[]{:S(2)}) collective-permute-start(bf16[2,2,64,128]{3,2,1,0:T(8,128)(2,1)S(1)} %pair.1.refs_0_), channel_id=1, source_target_pairs={{0,16},{2,18},{4,20},{6,22},{8,24},{10,26},{12,28},{14,30},{16,0},... | collective-permute-start | bytes 196616 | tf_op jit(solution)/shard_map/ppermute | solution.py:257
  12.2 6.6 %collective-permute-start.6 = (bf16[2,2,64,128]{3,2,1,0:T(8,128)(2,1)S(1)}, bf16[2,2,64,128]{3,2,1,0:T(8,128)(2,1)S(1)}, u32[]{:S(2)}, u32[]{:S(2)}) collective-permute-start(bf16[2,2,64,128]{3,2,1,0:T(8,128)(2,1)S(1)} %pair.1.refs_0_), channel_id=1, source_target_pairs={{0,24},{2,26},{4,28},{6,30},{8,16},{10,18},{12,20},{14,22},{16,8},... | collective-permute-start | bytes 196616 | tf_op jit(solution)/shard_map/ppermute | solution.py:257
  13.6 5.4 %collective-permute-start.2 = (bf16[2,2,64,128]{3,2,1,0:T(8,128)(2,1)S(1)}, bf16[2,2,64,128]{3,2,1,0:T(8,128)(2,1)S(1)}, u32[]{:S(2)}, u32[]{:S(2)}) collective-permute-start(bf16[2,2,64,128]{3,2,1,0:T(8,128)(2,1)S(1)} %pair.1.refs_0_), channel_id=1, source_target_pairs={{0,8},{2,10},{4,12},{6,14},{8,0},{10,2},{12,4},{14,6},{16,24},{18,... | collective-permute-start | bytes 196616 | tf_op jit(solution)/shard_map/ppermute | solution.py:257
  13.9 6.3 %collective-permute-start.8 = (s16[144,128]{1,0:T(8,128)(2,1)S(1)}, s16[144,128]{1,0:T(8,128)(2,1)S(1)}, u32[]{:S(2)}, u32[]{:S(2)}) collective-permute-start(s16[144,128]{1,0:T(8,128)(2,1)S(1)} %get-tuple-element.35), channel_id=1, source_target_pairs={{0,24},{2,26},{4,28},{6,30},{8,16},{10,18},{12,20},{14,22},{16,8},... | collective-permute-start | bytes 110600 | tf_op jit(solution)/shard_map/ppermute | solution.py:257
  16.9 5.2 %collective-permute-start.9 = (s16[144,128]{1,0:T(8,128)(2,1)S(1)}, s16[144,128]{1,0:T(8,128)(2,1)S(1)}, u32[]{:S(2)}, u32[]{:S(2)}) collective-permute-start(s16[144,128]{1,0:T(8,128)(2,1)S(1)} %get-tuple-element.36), channel_id=1, source_target_pairs={{0,16},{2,18},{4,20},{6,22},{8,24},{10,26},{12,28},{14,30},{16,0},... | collective-permute-start | bytes 110600 | tf_op jit(solution)/shard_map/ppermute | solution.py:257
  17.3 4.9 %collective-permute-start.10 = (s16[144,128]{1,0:T(8,128)(2,1)S(1)}, s16[144,128]{1,0:T(8,128)(2,1)S(1)}, u32[]{:S(2)}, u32[]{:S(2)}) collective-permute-start(s16[144,128]{1,0:T(8,128)(2,1)S(1)} %get-tuple-element.31.refs_1_), channel_id=1, source_target_pairs={{0,8},{2,10},{4,12},{6,14},{8,0},{10,2},{12,4},{14,6},{16,24},{18,... | collective-permute-start | bytes 110600 | tf_op jit(solution)/shard_map/ppermute | solution.py:257
  19.0 4.8 %collective-permute-start.7 = (bf16[4,2,2,64,128]{4,3,2,1,0:T(8,128)(2,1)S(1)}, bf16[4,2,2,64,128]{4,3,2,1,0:T(8,128)(2,1)S(1)}, u32[]{:S(2)}, u32[]{:S(2)}) collective-permute-start(bf16[4,2,2,64,128]{4,3,2,1,0:T(8,128)(2,1)S(1)} %mine.1), channel_id=1, source_target_pairs={{0,2},{2,0},{4,6},{6,4},{8,10},{10,8},{12,14},{14,12},{16,18},{18,... | collective-permute-start | bytes 786440 | tf_op jit(solution)/shard_map/ppermute | solution.py:244
  22.2 3.7 %collective-permute-start.11 = (f32[2,128]{1,0:T(2,128)S(1)}, f32[2,128]{1,0:T(2,128)S(1)}, u32[]{:S(2)}, u32[]{:S(2)}) collective-permute-start(f32[2,128]{1,0:T(2,128)S(1)} %get-tuple-element.40.dots_ref), channel_id=1, source_target_pairs={{0,1},{1,0},{2,3},{3,2},{4,5},{5,4},{6,7},{7,6},{8,9},{9,8},{10,11... | collective-permute-start | bytes 3080 | tf_op jit(solution)/shard_map/ppermute | solution.py:390

commit v7 on v2

--- a/solution.py
+++ b/solution.py
@@ -110,8 +110,9 @@
 
     lax.fori_loop(0, entries, entry_step, 0, unroll=min(entries, 24))
     size = outer * cap
-    for kind, ref in enumerate((near_keep, near_send, far_keep, far_send)):
+    for kind, ref in enumerate((near_keep, near_send, far_keep)):
         ref[...] = part_ref[kind * size : (kind + 1) * size].reshape(ref.shape)
+    write_message([part_ref[i] for i in range(3 * size, 4 * size)], far_send)
 
 
 def encode(total):
@@ -152,7 +153,8 @@
 def far_sum_kernel(keep_ref, got_ref, near_send, out_ref, near_out):
     near_out[...] = near_send[...]
     outer, cap = keep_ref.shape[:2]
-    totals = [keep_ref[k, c] + got_ref[k, c] for k in range(outer) for c in range(cap)]
+    got = read_message(outer * cap, keep_ref.shape[2], got_ref)
+    totals = [keep_ref[k, c] + got[k * cap + c] for k in range(outer) for c in range(cap)]
     write_message(totals, out_ref)
 
 
@@ -293,8 +295,9 @@
 
     near_keep, near_send, far_keep, far_send, columns, table, scaled, stored, scale_rows = pl.pallas_call(
         partial_kernel,
-        out_shape=[jax.ShapeDtypeStruct(side_shape, jnp.float32)] * 4
+        out_shape=[jax.ShapeDtypeStruct(side_shape, jnp.float32)] * 3
         + [
+            jax.ShapeDtypeStruct((message_rows(outer * cap, slab_rows), side), jnp.int16),
             jax.ShapeDtypeStruct((entries, side, tokens_here), jnp.bfloat16),
             jax.ShapeDtypeStruct((4, entries), jnp.int32),
             jax.ShapeDtypeStruct(block_shape, jnp.bfloat16),

time: 26.7 us -> 26.6 us (level)
  no operation moved by 1% of the time
where the time goes in v7:
time: 26.6 us; the launch traced here: 26.4 us
  starting transfers between devices  15.1 us (57%)
  Pallas kernels  6.53 us (25%)
  waiting for transfers between devices  4.02 us (15%)
  between operations  0.69 us (3%)
    ppermute x6, starting transfers between devices, stepped(): lax.ppermute(value, 'dp', [(i, ahead(size // 4, i // 4, step) * 4 + i % 4...  9.03 us
    ppermute x5, starting transfers between devices, flipped(): lax.ppermute(value, 'dp', [(i, i ^ bit) for i in range(lax.axis_size('dp'...  4.52 us
    ppermute x6, waiting for transfers between devices, stepped(): lax.ppermute(value, 'dp', [(i, ahead(size // 4, i // 4, step) * 4 + i % 4...  3.54 us
    pallas_call x1, Pallas kernels, on_device(): pl.pallas_call(partial_kernel, out_shape=[jax.ShapeDtypeStruct(side_shape...  3.44 us
    pallas_call x1, Pallas kernels, on_device(): pl.pallas_call(input_grad_kernel, out_shape=(jax.ShapeDtypeStruct(inputs_...  2.09 us
    ppermute x1, starting transfers between devices, on_device(): other_dots = lax.ppermute(dots, 'group', [(0, 1), (1, 0)])  1.56 us
    pallas_call x1, Pallas kernels, on_device(): pl.pallas_call(finish_kernel, out_shape=jax.ShapeDtypeStruct((1, cap), jn...  0.6 us
  transfers between devices with their start and end apart: 12, of which 5 were waited for; matrix products, arithmetic and copies ran while one was open for 0% of the time, Pallas kernels for 9%

profile of v7, /device:TPU:0, one launch (start us, length us, event | category | flops | bytes accessed | tf_op | source)
XLA Modules:
  0.0 26.4 jit_solution(6602559184565121235)
XLA Ops:
  0.6 3.4 %partials.1 = (f32[4,2,64,128]{3,2,1,0:T(8,128)S(1)}, f32[4,2,64,128]{3,2,1,0:T(8,128)S(1)}, f32[4,2,64,128]{3,2,1,0:T(8,128)S(1)}, s16[528,128]{1,0:T(8,128)(2,...) custom-call(s32[2,3584]{1,0:T(2,128)} %kept_hbm.1, ...), custom_call_target="tpu_custom_call" | custom-call | flops 4035500032 | bytes 12915000 | tf_op jit(solution)/shard_map/partials/pallas_call | solution.py:296
  4.1 0.5 %collective-permute-start.1 = (s16[528,128]{1,0:T(8,128)(2,1)S(1)}, s16[528,128]{1,0:T(8,128)(2,1)S(1)}, u32[]{:S(2)}, u32[]{:S(2)}) collective-permute-start(s16[528,128]{1,0:T(8,128)(2,1)S(1)} %get-tuple-element.26), channel_id=1, source_target_pairs={{0,2},{2,0},{4,6},{6,4},{8,10},{10,8},{12,14},{14,12},{16,18},{18,... | collective-permute-start | bytes 405512 | tf_op jit(solution)/shard_map/ppermute | solution.py:249
  4.6 2.6 %collective-permute-start = (bf16[2,64,128]{2,1,0:T(8,128)(2,1)S(1)}, bf16[2,64,128]{2,1,0:T(8,128)(2,1)S(1)}, u32[]{:S(2)}, u32[]{:S(2)}) collective-permute-start(bf16[2,64,128]{2,1,0:T(8,128)(2,1)S(1)} %get-tuple-element.24.refs_0_), channel_id=1, source_target_pairs={{0,4},{2,6},{4,0},{6,2},{8,12},{10,14},{12,8},{14,10},{16,20},{18,... | collective-permute-start | bytes 98312 | tf_op jit(solution)/shard_map/ppermute | solution.py:249
  7.2 0.0 collective-permute-done.1.got_ref
  7.2 0.2 far_sums.1
  7.4 1.3 %collective-permute-start.5 = (s16[528,128]{1,0:T(8,128)(2,1)S(1)}, s16[528,128]{1,0:T(8,128)(2,1)S(1)}, u32[]{:S(2)}, u32[]{:S(2)}) collective-permute-start(s16[528,128]{1,0:T(8,128)(2,1)S(1)} %get-tuple-element.28.refs_2_), channel_id=1, source_target_pairs={{0,4},{2,6},{4,0},{6,2},{8,12},{10,14},{12,8},{14,10},{16,20},{18,... | collective-permute-start | bytes 405512 | tf_op jit(solution)/shard_map/ppermute | solution.py:249
  8.7 0.0 collective-permute-start.4
  8.7 0.5 %collective-permute-done.refs_1_ = bf16[2,64,128]{2,1,0:T(8,128)(2,1)S(1)} collective-permute-done((bf16[2,64,128]{2,1,0:T(8,128)(2,1)S(1)}, bf16[2,64,128]{2,1,0:T(8,128)(2,1)S(1)}, u32[]{:S(2)}, u32[]{:S(2)}) %collective-permute-start) | collective-permute-done | bytes 32800 | tf_op jit(solution)/shard_map/ppermute | solution.py:249
  9.2 3.0 %collective-permute-start.3 = (bf16[2,2,64,128]{3,2,1,0:T(8,128)(2,1)S(1)}, bf16[2,2,64,128]{3,2,1,0:T(8,128)(2,1)S(1)}, u32[]{:S(2)}, u32[]{:S(2)}) collective-permute-start(bf16[2,2,64,128]{3,2,1,0:T(8,128)(2,1)S(1)} %pair.1.refs_0_), channel_id=1, source_target_pairs={{0,16},{2,18},{4,20},{6,22},{8,24},{10,26},{12,28},{14,30},{16,0},... | collective-permute-start | bytes 196616 | tf_op jit(solution)/shard_map/ppermute | solution.py:262
  12.2 1.4 %collective-permute-start.6 = (bf16[2,2,64,128]{3,2,1,0:T(8,128)(2,1)S(1)}, bf16[2,2,64,128]{3,2,1,0:T(8,128)(2,1)S(1)}, u32[]{:S(2)}, u32[]{:S(2)}) collective-permute-start(bf16[2,2,64,128]{3,2,1,0:T(8,128)(2,1)S(1)} %pair.1.refs_0_), channel_id=1, source_target_pairs={{0,24},{2,26},{4,28},{6,30},{8,16},{10,18},{12,20},{14,22},{16,8},... | collective-permute-start | bytes 196616 | tf_op jit(solution)/shard_map/ppermute | solution.py:262
  13.5 0.2 collective-permute-start.2
  13.8 0.0 collective-permute-done.5.far_ref
  13.8 0.0 collective-permute-done.4.got_ref
  13.8 0.1 near_sums.1
  13.9 3.0 %collective-permute-start.8 = (s16[144,128]{1,0:T(8,128)(2,1)S(1)}, s16[144,128]{1,0:T(8,128)(2,1)S(1)}, u32[]{:S(2)}, u32[]{:S(2)}) collective-permute-start(s16[144,128]{1,0:T(8,128)(2,1)S(1)} %get-tuple-element.35), channel_id=1, source_target_pairs={{0,24},{2,26},{4,28},{6,30},{8,16},{10,18},{12,20},{14,22},{16,8},... | collective-permute-start | bytes 110600 | tf_op jit(solution)/shard_map/ppermute | solution.py:262
  16.9 0.3 %collective-permute-start.9 = (s16[144,128]{1,0:T(8,128)(2,1)S(1)}, s16[144,128]{1,0:T(8,128)(2,1)S(1)}, u32[]{:S(2)}, u32[]{:S(2)}) collective-permute-start(s16[144,128]{1,0:T(8,128)(2,1)S(1)} %get-tuple-element.36), channel_id=1, source_target_pairs={{0,16},{2,18},{4,20},{6,22},{8,24},{10,26},{12,28},{14,30},{16,0},... | collective-permute-start | bytes 110600 | tf_op jit(solution)/shard_map/ppermute | solution.py:262
  17.2 0.0 collective-permute-done.3.refs_0_
  17.2 1.1 %collective-permute-start.10 = (s16[144,128]{1,0:T(8,128)(2,1)S(1)}, s16[144,128]{1,0:T(8,128)(2,1)S(1)}, u32[]{:S(2)}, u32[]{:S(2)}) collective-permute-start(s16[144,128]{1,0:T(8,128)(2,1)S(1)} %get-tuple-element.31.refs_1_), channel_id=1, source_target_pairs={{0,8},{2,10},{4,12},{6,14},{8,0},{10,2},{12,4},{14,6},{16,24},{18,... | collective-permute-start | bytes 110600 | tf_op jit(solution)/shard_map/ppermute | solution.py:262
  18.4 0.4 %collective-permute-done.6.refs_0_ = bf16[2,2,64,128]{3,2,1,0:T(8,128)(2,1)S(1)} collective-permute-done((bf16[2,2,64,128]{3,2,1,0:T(8,128)(2,1)S(1)}, bf16[2,2,64,128]{3,2,1,0:T(8,128)(2,1)S(1)}, u32[]{:S(2)}, u32[]{:S(2)}) %collective-permute-start.6) | collective-permute-done | bytes 65568 | tf_op jit(solution)/shard_map/ppermute | solution.py:262
  18.8 0.2 collective-permute-done.2.refs_1_
  19.0 0.1 collective-permute-start.7
  19.1 1.1 %collective-permute-done.8.refs_0_ = s16[144,128]{1,0:T(8,128)(2,1)S(1)} collective-permute-done((s16[144,128]{1,0:T(8,128)(2,1)S(1)}, s16[144,128]{1,0:T(8,128)(2,1)S(1)}, u32[]{:S(2)}, u32[]{:S(2)}) %collective-permute-start.8) | collective-permute-done | bytes 36896 | tf_op jit(solution)/shard_map/ppermute | solution.py:262
  20.2 1.8 %collective-permute-done.9.refs_0_ = s16[144,128]{1,0:T(8,128)(2,1)S(1)} collective-permute-done((s16[144,128]{1,0:T(8,128)(2,1)S(1)}, s16[144,128]{1,0:T(8,128)(2,1)S(1)}, u32[]{:S(2)}, u32[]{:S(2)}) %collective-permute-start.9) | collective-permute-done | bytes 36896 | tf_op jit(solution)/shard_map/ppermute | solution.py:262
  22.1 0.0 collective-permute-done.10.refs_0_
  22.1 1.6 %collective-permute-start.11 = (f32[2,128]{1,0:T(2,128)S(1)}, f32[2,128]{1,0:T(2,128)S(1)}, u32[]{:S(2)}, u32[]{:S(2)}) collective-permute-start(f32[2,128]{1,0:T(2,128)S(1)} %get-tuple-element.40.dots_ref), channel_id=1, source_target_pairs={{0,1},{1,0},{2,3},{3,2},{4,5},{5,4},{6,7},{7,6},{8,9},{9,8},{10,11... | collective-permute-start | bytes 3080 | tf_op jit(solution)/shard_map/ppermute | solution.py:396
  23.7 0.0 collective-permute-done.7.other
  23.7 2.1 %input_grads.1 = (bf16[64,64,128]{2,1,0:T(8,128)(2,1)}, f32[1,2,64,128]{3,2,1,0:T(8,128)}) custom-call(s32[4,24]{1,0:T(4,128)S(1)} %get-tuple-element.22.tab_ref, bf16[24,128,128]{2,1,0:T(8,128)(2,1)S(1)} %get-tuple-element.23.cols_ref, bf16[4,2,2,64,128]{4,3,2,1,0:T(8,128)(2,1)S(1)} %mine.1, bf16[4,2,2,64,128]{4,3,2,1,0:T(8,128)(2,1)S(1)} %collective-permute-done.7.other, ...), custom_call_target="tpu_custom_call" | custom-call | flops 2305999872 | bytes 7380000 | tf_op jit(solution)/shard_map/input_grads/pallas_call | solution.py:397
  25.8 0.0 collective-permute-done.11.got_ref
  25.8 0.6 %finish.1 = f32[1,2]{1,0:T(1,128)} custom-call(f32[2,128]{1,0:T(2,128)S(1)} %get-tuple-element.40.dots_ref, f32[2,128]{1,0:T(2,128)S(1)} %collective-permute-done.11.got_ref, bf16[64,64,128]{2,1,0:T(8,128)(2,1)} %get-tuple-element.19.grads_ref), custom_call_target="tpu_custom_call" | custom-call | flops 576499968 | bytes 1845000 | tf_op jit(solution)/shard_map/finish/pallas_call | solution.py:410
  (7 shorter events, 0.1 us)
Async XLA Ops:
  4.1 3.1 %collective-permute-start.1 = (s16[528,128]{1,0:T(8,128)(2,1)S(1)}, s16[528,128]{1,0:T(8,128)(2,1)S(1)}, u32[]{:S(2)}, u32[]{:S(2)}) collective-permute-start(s16[528,128]{1,0:T(8,128)(2,1)S(1)} %get-tuple-element.26), channel_id=1, source_target_pairs={{0,2},{2,0},{4,6},{6,4},{8,10},{10,8},{12,14},{14,12},{16,18},{18,... | collective-permute-start | bytes 405512 | tf_op jit(solution)/shard_map/ppermute | solution.py:249
  4.6 4.6 %collective-permute-start = (bf16[2,64,128]{2,1,0:T(8,128)(2,1)S(1)}, bf16[2,64,128]{2,1,0:T(8,128)(2,1)S(1)}, u32[]{:S(2)}, u32[]{:S(2)}) collective-permute-start(bf16[2,64,128]{2,1,0:T(8,128)(2,1)S(1)} %get-tuple-element.24.refs_0_), channel_id=1, source_target_pairs={{0,4},{2,6},{4,0},{6,2},{8,12},{10,14},{12,8},{14,10},{16,20},{18,... | collective-permute-start | bytes 98312 | tf_op jit(solution)/shard_map/ppermute | solution.py:249
  7.4 6.4 %collective-permute-start.5 = (s16[528,128]{1,0:T(8,128)(2,1)S(1)}, s16[528,128]{1,0:T(8,128)(2,1)S(1)}, u32[]{:S(2)}, u32[]{:S(2)}) collective-permute-start(s16[528,128]{1,0:T(8,128)(2,1)S(1)} %get-tuple-element.28.refs_2_), channel_id=1, source_target_pairs={{0,4},{2,6},{4,0},{6,2},{8,12},{10,14},{12,8},{14,10},{16,20},{18,... | collective-permute-start | bytes 405512 | tf_op jit(solution)/shard_map/ppermute | solution.py:249
  8.7 5.1 %collective-permute-start.4 = (f32[4,2,64,128]{3,2,1,0:T(8,128)S(1)}, f32[4,2,64,128]{3,2,1,0:T(8,128)S(1)}, u32[]{:S(2)}, u32[]{:S(2)}) collective-permute-start(f32[4,2,64,128]{3,2,1,0:T(8,128)S(1)} %get-tuple-element.30), channel_id=1, source_target_pairs={{0,2},{2,0},{4,6},{6,4},{8,10},{10,8},{12,14},{14,12},{16,18},{18,... | collective-permute-start | bytes 786440 | tf_op jit(solution)/shard_map/ppermute | solution.py:249
  9.2 8.1 %collective-permute-start.3 = (bf16[2,2,64,128]{3,2,1,0:T(8,128)(2,1)S(1)}, bf16[2,2,64,128]{3,2,1,0:T(8,128)(2,1)S(1)}, u32[]{:S(2)}, u32[]{:S(2)}) collective-permute-start(bf16[2,2,64,128]{3,2,1,0:T(8,128)(2,1)S(1)} %pair.1.refs_0_), channel_id=1, source_target_pairs={{0,16},{2,18},{4,20},{6,22},{8,24},{10,26},{12,28},{14,30},{16,0},... | collective-permute-start | bytes 196616 | tf_op jit(solution)/shard_map/ppermute | solution.py:262
  12.2 6.6 %collective-permute-start.6 = (bf16[2,2,64,128]{3,2,1,0:T(8,128)(2,1)S(1)}, bf16[2,2,64,128]{3,2,1,0:T(8,128)(2,1)S(1)}, u32[]{:S(2)}, u32[]{:S(2)}) collective-permute-start(bf16[2,2,64,128]{3,2,1,0:T(8,128)(2,1)S(1)} %pair.1.refs_0_), channel_id=1, source_target_pairs={{0,24},{2,26},{4,28},{6,30},{8,16},{10,18},{12,20},{14,22},{16,8},... | collective-permute-start | bytes 196616 | tf_op jit(solution)/shard_map/ppermute | solution.py:262
  13.5 5.4 %collective-permute-start.2 = (bf16[2,2,64,128]{3,2,1,0:T(8,128)(2,1)S(1)}, bf16[2,2,64,128]{3,2,1,0:T(8,128)(2,1)S(1)}, u32[]{:S(2)}, u32[]{:S(2)}) collective-permute-start(bf16[2,2,64,128]{3,2,1,0:T(8,128)(2,1)S(1)} %pair.1.refs_0_), channel_id=1, source_target_pairs={{0,8},{2,10},{4,12},{6,14},{8,0},{10,2},{12,4},{14,6},{16,24},{18,... | collective-permute-start | bytes 196616 | tf_op jit(solution)/shard_map/ppermute | solution.py:262
  13.9 6.3 %collective-permute-start.8 = (s16[144,128]{1,0:T(8,128)(2,1)S(1)}, s16[144,128]{1,0:T(8,128)(2,1)S(1)}, u32[]{:S(2)}, u32[]{:S(2)}) collective-permute-start(s16[144,128]{1,0:T(8,128)(2,1)S(1)} %get-tuple-element.35), channel_id=1, source_target_pairs={{0,24},{2,26},{4,28},{6,30},{8,16},{10,18},{12,20},{14,22},{16,8},... | collective-permute-start | bytes 110600 | tf_op jit(solution)/shard_map/ppermute | solution.py:262
  16.9 5.1 %collective-permute-start.9 = (s16[144,128]{1,0:T(8,128)(2,1)S(1)}, s16[144,128]{1,0:T(8,128)(2,1)S(1)}, u32[]{:S(2)}, u32[]{:S(2)}) collective-permute-start(s16[144,128]{1,0:T(8,128)(2,1)S(1)} %get-tuple-element.36), channel_id=1, source_target_pairs={{0,16},{2,18},{4,20},{6,22},{8,24},{10,26},{12,28},{14,30},{16,0},... | collective-permute-start | bytes 110600 | tf_op jit(solution)/shard_map/ppermute | solution.py:262
  17.2 4.8 %collective-permute-start.10 = (s16[144,128]{1,0:T(8,128)(2,1)S(1)}, s16[144,128]{1,0:T(8,128)(2,1)S(1)}, u32[]{:S(2)}, u32[]{:S(2)}) collective-permute-start(s16[144,128]{1,0:T(8,128)(2,1)S(1)} %get-tuple-element.31.refs_1_), channel_id=1, source_target_pairs={{0,8},{2,10},{4,12},{6,14},{8,0},{10,2},{12,4},{14,6},{16,24},{18,... | collective-permute-start | bytes 110600 | tf_op jit(solution)/shard_map/ppermute | solution.py:262
  19.0 4.7 %collective-permute-start.7 = (bf16[4,2,2,64,128]{4,3,2,1,0:T(8,128)(2,1)S(1)}, bf16[4,2,2,64,128]{4,3,2,1,0:T(8,128)(2,1)S(1)}, u32[]{:S(2)}, u32[]{:S(2)}) collective-permute-start(bf16[4,2,2,64,128]{4,3,2,1,0:T(8,128)(2,1)S(1)} %mine.1), channel_id=1, source_target_pairs={{0,2},{2,0},{4,6},{6,4},{8,10},{10,8},{12,14},{14,12},{16,18},{18,... | collective-permute-start | bytes 786440 | tf_op jit(solution)/shard_map/ppermute | solution.py:249
  22.1 3.7 %collective-permute-start.11 = (f32[2,128]{1,0:T(2,128)S(1)}, f32[2,128]{1,0:T(2,128)S(1)}, u32[]{:S(2)}, u32[]{:S(2)}) collective-permute-start(f32[2,128]{1,0:T(2,128)S(1)} %get-tuple-element.40.dots_ref), channel_id=1, source_target_pairs={{0,1},{1,0},{2,3},{3,2},{4,5},{5,4},{6,7},{7,6},{8,9},{9,8},{10,11... | collective-permute-start | bytes 3080 | tf_op jit(solution)/shard_map/ppermute | solution.py:396

commit v8 on v7

--- a/solution.py
+++ b/solution.py
@@ -110,8 +110,9 @@
 
     lax.fori_loop(0, entries, entry_step, 0, unroll=min(entries, 24))
     size = outer * cap
-    for kind, ref in enumerate((near_keep, near_send, far_keep)):
-        ref[...] = part_ref[kind * size : (kind + 1) * size].reshape(ref.shape)
+    near_keep[...] = part_ref[:size].reshape(near_keep.shape)
+    far_keep[...] = part_ref[2 * size : 3 * size].reshape(far_keep.shape)
+    write_message([part_ref[i] for i in range(size, 2 * size)], near_send)
     write_message([part_ref[i] for i in range(3 * size, 4 * size)], far_send)
 
 
@@ -160,10 +161,11 @@
 
 def near_sum_kernel(keep_ref, got_ref, far_ref, *out_refs):
     outer, cap, slab_rows, side = keep_ref.shape
+    got = read_message(outer * cap, slab_rows, got_ref)
     far = read_message(outer * cap, slab_rows, far_ref)
     for step in range(outer):
         totals = [
-            keep_ref[step, c] + got_ref[step, c] + far[step * cap + c] for c in range(cap)
+            keep_ref[step, c] + got[step * cap + c] + far[step * cap + c] for c in range(cap)
         ]
         if step == 0:
             for c in range(cap):
@@ -293,11 +295,14 @@
     side_shape = (outer, cap, slab_rows, side)
     message_shape = (message_rows(cap, slab_rows), side)
 
+    side_message = jax.ShapeDtypeStruct((message_rows(outer * cap, slab_rows), side), jnp.int16)
     near_keep, near_send, far_keep, far_send, columns, table, scaled, stored, scale_rows = pl.pallas_call(
         partial_kernel,
-        out_shape=[jax.ShapeDtypeStruct(side_shape, jnp.float32)] * 3
-        + [
-            jax.ShapeDtypeStruct((message_rows(outer * cap, slab_rows), side), jnp.int16),
+        out_shape=[
+            jax.ShapeDtypeStruct(side_shape, jnp.float32),
+            side_message,
+            jax.ShapeDtypeStruct(side_shape, jnp.float32),
+            side_message,
             jax.ShapeDtypeStruct((entries, side, tokens_here), jnp.bfloat16),
             jax.ShapeDtypeStruct((4, entries), jnp.int32),
             jax.ShapeDtypeStruct(block_shape, jnp.bfloat16),
@@ -342,7 +347,7 @@
         far_sum_kernel,
         out_shape=(
             jax.ShapeDtypeStruct((message_rows(outer * cap, slab_rows), side), jnp.int16),
-            jax.ShapeDtypeStruct(side_shape, jnp.float32),
+            side_message,
         ),
         in_specs=[VMEM_SPEC] * 3,
         out_specs=(VMEM_SPEC, VMEM_SPEC),

time: 26.6 us -> 26.7 us (level)
  no operation moved by 1% of the time
where the time goes in v8:
time: 26.7 us; the launch traced here: 26.5 us
  starting transfers between devices  15.1 us (57%)
  Pallas kernels  6.64 us (25%)
  waiting for transfers between devices  4.03 us (15%)
  between operations  0.69 us (3%)
    ppermute x6, starting transfers between devices, stepped(): lax.ppermute(value, 'dp', [(i, ahead(size // 4, i // 4, step) * 4 + i % 4...  9.03 us
    ppermute x5, starting transfers between devices, flipped(): lax.ppermute(value, 'dp', [(i, i ^ bit) for i in range(lax.axis_size('dp'...  4.52 us
    ppermute x6, waiting for transfers between devices, stepped(): lax.ppermute(value, 'dp', [(i, ahead(size // 4, i // 4, step) * 4 + i % 4...  3.54 us
    pallas_call x1, Pallas kernels, on_device(): pl.pallas_call(partial_kernel, out_shape=[jax.ShapeDtypeStruct(side_shape...  3.54 us
    pallas_call x1, Pallas kernels, on_device(): pl.pallas_call(input_grad_kernel, out_shape=(jax.ShapeDtypeStruct(inputs_...  2.09 us
    ppermute x1, starting transfers between devices, on_device(): other_dots = lax.ppermute(dots, 'group', [(0, 1), (1, 0)])  1.56 us
    pallas_call x1, Pallas kernels, on_device(): pl.pallas_call(finish_kernel, out_shape=jax.ShapeDtypeStruct((1, cap), jn...  0.6 us
  transfers between devices with their start and end apart: 12, of which 5 were waited for; matrix products, arithmetic and copies ran while one was open for 0% of the time, Pallas kernels for 9%

profile of v8, /device:TPU:0, one launch (start us, length us, event | category | flops | bytes accessed | tf_op | source)
XLA Modules:
  0.0 26.5 jit_solution(15152597480405013879)
XLA Ops:
  0.6 3.5 %partials.1 = (f32[4,2,64,128]{3,2,1,0:T(8,128)S(1)}, s16[528,128]{1,0:T(8,128)(2,1)S(1)}, f32[4,2,64,128]{3,2,1,0:T(8,128)S(1)}, s16[528,128]{1,0:T(8,128)(2,1)...) custom-call(s32[2,3584]{1,0:T(2,128)} %kept_hbm.1, ...), custom_call_target="tpu_custom_call" | custom-call | flops 4035500032 | bytes 12915000 | tf_op jit(solution)/shard_map/partials/pallas_call | solution.py:299
  4.2 0.5 %collective-permute-start.1 = (s16[528,128]{1,0:T(8,128)(2,1)S(1)}, s16[528,128]{1,0:T(8,128)(2,1)S(1)}, u32[]{:S(2)}, u32[]{:S(2)}) collective-permute-start(s16[528,128]{1,0:T(8,128)(2,1)S(1)} %get-tuple-element.26), channel_id=1, source_target_pairs={{0,2},{2,0},{4,6},{6,4},{8,10},{10,8},{12,14},{14,12},{16,18},{18,... | collective-permute-start | bytes 405512 | tf_op jit(solution)/shard_map/ppermute | solution.py:251
  4.7 2.6 %collective-permute-start = (bf16[2,64,128]{2,1,0:T(8,128)(2,1)S(1)}, bf16[2,64,128]{2,1,0:T(8,128)(2,1)S(1)}, u32[]{:S(2)}, u32[]{:S(2)}) collective-permute-start(bf16[2,64,128]{2,1,0:T(8,128)(2,1)S(1)} %get-tuple-element.24.refs_0_), channel_id=1, source_target_pairs={{0,4},{2,6},{4,0},{6,2},{8,12},{10,14},{12,8},{14,10},{16,20},{18,... | collective-permute-start | bytes 98312 | tf_op jit(solution)/shard_map/ppermute | solution.py:251
  7.3 0.0 collective-permute-done.1.got_ref
  7.3 0.2 far_sums.1
  7.5 1.3 %collective-permute-start.5 = (s16[528,128]{1,0:T(8,128)(2,1)S(1)}, s16[528,128]{1,0:T(8,128)(2,1)S(1)}, u32[]{:S(2)}, u32[]{:S(2)}) collective-permute-start(s16[528,128]{1,0:T(8,128)(2,1)S(1)} %get-tuple-element.28.refs_2_), channel_id=1, source_target_pairs={{0,4},{2,6},{4,0},{6,2},{8,12},{10,14},{12,8},{14,10},{16,20},{18,... | collective-permute-start | bytes 405512 | tf_op jit(solution)/shard_map/ppermute | solution.py:251
  8.8 0.0 collective-permute-start.4
  8.8 0.5 %collective-permute-done.refs_1_ = bf16[2,64,128]{2,1,0:T(8,128)(2,1)S(1)} collective-permute-done((bf16[2,64,128]{2,1,0:T(8,128)(2,1)S(1)}, bf16[2,64,128]{2,1,0:T(8,128)(2,1)S(1)}, u32[]{:S(2)}, u32[]{:S(2)}) %collective-permute-start) | collective-permute-done | bytes 32800 | tf_op jit(solution)/shard_map/ppermute | solution.py:251
  9.3 3.0 %collective-permute-start.3 = (bf16[2,2,64,128]{3,2,1,0:T(8,128)(2,1)S(1)}, bf16[2,2,64,128]{3,2,1,0:T(8,128)(2,1)S(1)}, u32[]{:S(2)}, u32[]{:S(2)}) collective-permute-start(bf16[2,2,64,128]{3,2,1,0:T(8,128)(2,1)S(1)} %pair.1.refs_0_), channel_id=1, source_target_pairs={{0,16},{2,18},{4,20},{6,22},{8,24},{10,26},{12,28},{14,30},{16,0},... | collective-permute-start | bytes 196616 | tf_op jit(solution)/shard_map/ppermute | solution.py:264
  12.3 1.4 %collective-permute-start.6 = (bf16[2,2,64,128]{3,2,1,0:T(8,128)(2,1)S(1)}, bf16[2,2,64,128]{3,2,1,0:T(8,128)(2,1)S(1)}, u32[]{:S(2)}, u32[]{:S(2)}) collective-permute-start(bf16[2,2,64,128]{3,2,1,0:T(8,128)(2,1)S(1)} %pair.1.refs_0_), channel_id=1, source_target_pairs={{0,24},{2,26},{4,28},{6,30},{8,16},{10,18},{12,20},{14,22},{16,8},... | collective-permute-start | bytes 196616 | tf_op jit(solution)/shard_map/ppermute | solution.py:264
  13.6 0.2 collective-permute-start.2
  13.9 0.0 collective-permute-done.5.far_ref
  13.9 0.0 collective-permute-done.4.got_ref
  13.9 0.2 near_sums.1
  14.0 3.0 %collective-permute-start.8 = (s16[144,128]{1,0:T(8,128)(2,1)S(1)}, s16[144,128]{1,0:T(8,128)(2,1)S(1)}, u32[]{:S(2)}, u32[]{:S(2)}) collective-permute-start(s16[144,128]{1,0:T(8,128)(2,1)S(1)} %get-tuple-element.35), channel_id=1, source_target_pairs={{0,24},{2,26},{4,28},{6,30},{8,16},{10,18},{12,20},{14,22},{16,8},... | collective-permute-start | bytes 110600 | tf_op jit(solution)/shard_map/ppermute | solution.py:264
  17.0 0.3 %collective-permute-start.9 = (s16[144,128]{1,0:T(8,128)(2,1)S(1)}, s16[144,128]{1,0:T(8,128)(2,1)S(1)}, u32[]{:S(2)}, u32[]{:S(2)}) collective-permute-start(s16[144,128]{1,0:T(8,128)(2,1)S(1)} %get-tuple-element.36), channel_id=1, source_target_pairs={{0,16},{2,18},{4,20},{6,22},{8,24},{10,26},{12,28},{14,30},{16,0},... | collective-permute-start | bytes 110600 | tf_op jit(solution)/shard_map/ppermute | solution.py:264
  17.4 0.0 collective-permute-done.3.refs_0_
  17.4 1.1 %collective-permute-start.10 = (s16[144,128]{1,0:T(8,128)(2,1)S(1)}, s16[144,128]{1,0:T(8,128)(2,1)S(1)}, u32[]{:S(2)}, u32[]{:S(2)}) collective-permute-start(s16[144,128]{1,0:T(8,128)(2,1)S(1)} %get-tuple-element.31.refs_1_), channel_id=1, source_target_pairs={{0,8},{2,10},{4,12},{6,14},{8,0},{10,2},{12,4},{14,6},{16,24},{18,... | collective-permute-start | bytes 110600 | tf_op jit(solution)/shard_map/ppermute | solution.py:264
  18.5 0.4 %collective-permute-done.6.refs_0_ = bf16[2,2,64,128]{3,2,1,0:T(8,128)(2,1)S(1)} collective-permute-done((bf16[2,2,64,128]{3,2,1,0:T(8,128)(2,1)S(1)}, bf16[2,2,64,128]{3,2,1,0:T(8,128)(2,1)S(1)}, u32[]{:S(2)}, u32[]{:S(2)}) %collective-permute-start.6) | collective-permute-done | bytes 65568 | tf_op jit(solution)/shard_map/ppermute | solution.py:264
  18.9 0.2 collective-permute-done.2.refs_1_
  19.1 0.1 collective-permute-start.7
  19.2 1.1 %collective-permute-done.8.refs_0_ = s16[144,128]{1,0:T(8,128)(2,1)S(1)} collective-permute-done((s16[144,128]{1,0:T(8,128)(2,1)S(1)}, s16[144,128]{1,0:T(8,128)(2,1)S(1)}, u32[]{:S(2)}, u32[]{:S(2)}) %collective-permute-start.8) | collective-permute-done | bytes 36896 | tf_op jit(solution)/shard_map/ppermute | solution.py:264
  20.3 1.8 %collective-permute-done.9.refs_0_ = s16[144,128]{1,0:T(8,128)(2,1)S(1)} collective-permute-done((s16[144,128]{1,0:T(8,128)(2,1)S(1)}, s16[144,128]{1,0:T(8,128)(2,1)S(1)}, u32[]{:S(2)}, u32[]{:S(2)}) %collective-permute-start.9) | collective-permute-done | bytes 36896 | tf_op jit(solution)/shard_map/ppermute | solution.py:264
  22.2 0.0 collective-permute-done.10.refs_0_
  22.2 1.6 %collective-permute-start.11 = (f32[2,128]{1,0:T(2,128)S(1)}, f32[2,128]{1,0:T(2,128)S(1)}, u32[]{:S(2)}, u32[]{:S(2)}) collective-permute-start(f32[2,128]{1,0:T(2,128)S(1)} %get-tuple-element.40.dots_ref), channel_id=1, source_target_pairs={{0,1},{1,0},{2,3},{3,2},{4,5},{5,4},{6,7},{7,6},{8,9},{9,8},{10,11... | collective-permute-start | bytes 3080 | tf_op jit(solution)/shard_map/ppermute | solution.py:401
  23.8 0.0 collective-permute-done.7.other
  23.8 2.1 %input_grads.1 = (bf16[64,64,128]{2,1,0:T(8,128)(2,1)}, f32[1,2,64,128]{3,2,1,0:T(8,128)}) custom-call(s32[4,24]{1,0:T(4,128)S(1)} %get-tuple-element.22.tab_ref, bf16[24,128,128]{2,1,0:T(8,128)(2,1)S(1)} %get-tuple-element.23.cols_ref, bf16[4,2,2,64,128]{4,3,2,1,0:T(8,128)(2,1)S(1)} %mine.1, bf16[4,2,2,64,128]{4,3,2,1,0:T(8,128)(2,1)S(1)} %collective-permute-done.7.other, ...), custom_call_target="tpu_custom_call" | custom-call | flops 2305999872 | bytes 7380000 | tf_op jit(solution)/shard_map/input_grads/pallas_call | solution.py:402
  25.9 0.0 collective-permute-done.11.got_ref
  25.9 0.6 %finish.1 = f32[1,2]{1,0:T(1,128)} custom-call(f32[2,128]{1,0:T(2,128)S(1)} %get-tuple-element.40.dots_ref, f32[2,128]{1,0:T(2,128)S(1)} %collective-permute-done.11.got_ref, bf16[64,64,128]{2,1,0:T(8,128)(2,1)} %get-tuple-element.19.grads_ref), custom_call_target="tpu_custom_call" | custom-call | flops 576499968 | bytes 1845000 | tf_op jit(solution)/shard_map/finish/pallas_call | solution.py:415
  (7 shorter events, 0.1 us)
Async XLA Ops:
  4.2 3.1 %collective-permute-start.1 = (s16[528,128]{1,0:T(8,128)(2,1)S(1)}, s16[528,128]{1,0:T(8,128)(2,1)S(1)}, u32[]{:S(2)}, u32[]{:S(2)}) collective-permute-start(s16[528,128]{1,0:T(8,128)(2,1)S(1)} %get-tuple-element.26), channel_id=1, source_target_pairs={{0,2},{2,0},{4,6},{6,4},{8,10},{10,8},{12,14},{14,12},{16,18},{18,... | collective-permute-start | bytes 405512 | tf_op jit(solution)/shard_map/ppermute | solution.py:251
  4.7 4.6 %collective-permute-start = (bf16[2,64,128]{2,1,0:T(8,128)(2,1)S(1)}, bf16[2,64,128]{2,1,0:T(8,128)(2,1)S(1)}, u32[]{:S(2)}, u32[]{:S(2)}) collective-permute-start(bf16[2,64,128]{2,1,0:T(8,128)(2,1)S(1)} %get-tuple-element.24.refs_0_), channel_id=1, source_target_pairs={{0,4},{2,6},{4,0},{6,2},{8,12},{10,14},{12,8},{14,10},{16,20},{18,... | collective-permute-start | bytes 98312 | tf_op jit(solution)/shard_map/ppermute | solution.py:251
  7.5 6.4 %collective-permute-start.5 = (s16[528,128]{1,0:T(8,128)(2,1)S(1)}, s16[528,128]{1,0:T(8,128)(2,1)S(1)}, u32[]{:S(2)}, u32[]{:S(2)}) collective-permute-start(s16[528,128]{1,0:T(8,128)(2,1)S(1)} %get-tuple-element.28.refs_2_), channel_id=1, source_target_pairs={{0,4},{2,6},{4,0},{6,2},{8,12},{10,14},{12,8},{14,10},{16,20},{18,... | collective-permute-start | bytes 405512 | tf_op jit(solution)/shard_map/ppermute | solution.py:251
  8.8 5.1 %collective-permute-start.4 = (s16[528,128]{1,0:T(8,128)(2,1)S(1)}, s16[528,128]{1,0:T(8,128)(2,1)S(1)}, u32[]{:S(2)}, u32[]{:S(2)}) collective-permute-start(s16[528,128]{1,0:T(8,128)(2,1)S(1)} %get-tuple-element.30), channel_id=1, source_target_pairs={{0,2},{2,0},{4,6},{6,4},{8,10},{10,8},{12,14},{14,12},{16,18},{18,... | collective-permute-start | bytes 405512 | tf_op jit(solution)/shard_map/ppermute | solution.py:251
  9.3 8.1 %collective-permute-start.3 = (bf16[2,2,64,128]{3,2,1,0:T(8,128)(2,1)S(1)}, bf16[2,2,64,128]{3,2,1,0:T(8,128)(2,1)S(1)}, u32[]{:S(2)}, u32[]{:S(2)}) collective-permute-start(bf16[2,2,64,128]{3,2,1,0:T(8,128)(2,1)S(1)} %pair.1.refs_0_), channel_id=1, source_target_pairs={{0,16},{2,18},{4,20},{6,22},{8,24},{10,26},{12,28},{14,30},{16,0},... | collective-permute-start | bytes 196616 | tf_op jit(solution)/shard_map/ppermute | solution.py:264
  12.3 6.6 %collective-permute-start.6 = (bf16[2,2,64,128]{3,2,1,0:T(8,128)(2,1)S(1)}, bf16[2,2,64,128]{3,2,1,0:T(8,128)(2,1)S(1)}, u32[]{:S(2)}, u32[]{:S(2)}) collective-permute-start(bf16[2,2,64,128]{3,2,1,0:T(8,128)(2,1)S(1)} %pair.1.refs_0_), channel_id=1, source_target_pairs={{0,24},{2,26},{4,28},{6,30},{8,16},{10,18},{12,20},{14,22},{16,8},... | collective-permute-start | bytes 196616 | tf_op jit(solution)/shard_map/ppermute | solution.py:264
  13.6 5.4 %collective-permute-start.2 = (bf16[2,2,64,128]{3,2,1,0:T(8,128)(2,1)S(1)}, bf16[2,2,64,128]{3,2,1,0:T(8,128)(2,1)S(1)}, u32[]{:S(2)}, u32[]{:S(2)}) collective-permute-start(bf16[2,2,64,128]{3,2,1,0:T(8,128)(2,1)S(1)} %pair.1.refs_0_), channel_id=1, source_target_pairs={{0,8},{2,10},{4,12},{6,14},{8,0},{10,2},{12,4},{14,6},{16,24},{18,... | collective-permute-start | bytes 196616 | tf_op jit(solution)/shard_map/ppermute | solution.py:264
  14.0 6.3 %collective-permute-start.8 = (s16[144,128]{1,0:T(8,128)(2,1)S(1)}, s16[144,128]{1,0:T(8,128)(2,1)S(1)}, u32[]{:S(2)}, u32[]{:S(2)}) collective-permute-start(s16[144,128]{1,0:T(8,128)(2,1)S(1)} %get-tuple-element.35), channel_id=1, source_target_pairs={{0,24},{2,26},{4,28},{6,30},{8,16},{10,18},{12,20},{14,22},{16,8},... | collective-permute-start | bytes 110600 | tf_op jit(solution)/shard_map/ppermute | solution.py:264
  17.0 5.1 %collective-permute-start.9 = (s16[144,128]{1,0:T(8,128)(2,1)S(1)}, s16[144,128]{1,0:T(8,128)(2,1)S(1)}, u32[]{:S(2)}, u32[]{:S(2)}) collective-permute-start(s16[144,128]{1,0:T(8,128)(2,1)S(1)} %get-tuple-element.36), channel_id=1, source_target_pairs={{0,16},{2,18},{4,20},{6,22},{8,24},{10,26},{12,28},{14,30},{16,0},... | collective-permute-start | bytes 110600 | tf_op jit(solution)/shard_map/ppermute | solution.py:264
  17.4 4.8 %collective-permute-start.10 = (s16[144,128]{1,0:T(8,128)(2,1)S(1)}, s16[144,128]{1,0:T(8,128)(2,1)S(1)}, u32[]{:S(2)}, u32[]{:S(2)}) collective-permute-start(s16[144,128]{1,0:T(8,128)(2,1)S(1)} %get-tuple-element.31.refs_1_), channel_id=1, source_target_pairs={{0,8},{2,10},{4,12},{6,14},{8,0},{10,2},{12,4},{14,6},{16,24},{18,... | collective-permute-start | bytes 110600 | tf_op jit(solution)/shard_map/ppermute | solution.py:264
  19.1 4.7 %collective-permute-start.7 = (bf16[4,2,2,64,128]{4,3,2,1,0:T(8,128)(2,1)S(1)}, bf16[4,2,2,64,128]{4,3,2,1,0:T(8,128)(2,1)S(1)}, u32[]{:S(2)}, u32[]{:S(2)}) collective-permute-start(bf16[4,2,2,64,128]{4,3,2,1,0:T(8,128)(2,1)S(1)} %mine.1), channel_id=1, source_target_pairs={{0,2},{2,0},{4,6},{6,4},{8,10},{10,8},{12,14},{14,12},{16,18},{18,... | collective-permute-start | bytes 786440 | tf_op jit(solution)/shard_map/ppermute | solution.py:251
  22.2 3.7 %collective-permute-start.11 = (f32[2,128]{1,0:T(2,128)S(1)}, f32[2,128]{1,0:T(2,128)S(1)}, u32[]{:S(2)}, u32[]{:S(2)}) collective-permute-start(f32[2,128]{1,0:T(2,128)S(1)} %get-tuple-element.40.dots_ref), channel_id=1, source_target_pairs={{0,1},{1,0},{2,3},{3,2},{4,5},{5,4},{6,7},{7,6},{8,9},{9,8},{10,11... | collective-permute-start | bytes 3080 | tf_op jit(solution)/shard_map/ppermute | solution.py:401
